TPU v7x, 512 devices: a whole 4x4x16 slice. The times are simulated.
512 devices in a mesh: lon: 64 (over x, z), lat: 8 (over y, core).
Axes of the slice: x: 4, y: 4, z: 16, core: 2. Of those that a mesh axis runs over, the one named last changes fastest.
Arguments:
- right_side: float32 [16, 64, 32768], P(None, 'lat', 'lon'), may hold values from -6 to 6
- initial_guess: float32 [16, 64, 32768], P(None, 'lat', 'lon'), may hold values from -3 to 3
- land_mask: float32 [16, 64, 32768], P(None, 'lat', 'lon'), may hold values from 0 to 1
- coefficient_sets: float32 [2, 4, 16], replicated, may hold values from 0.05 to 1
Outputs:
- iterate: float32 [16, 64, 32768], P(None, 'lat', 'lon')
- residual: float32 [16, 64, 32768], P(None, 'lat', 'lon')
- direction: float32 [16, 64, 32768], P(None, 'lat', 'lon')
All inputs are finite; a program needn't handle non-finite values.
Results may differ from a plain program's by a relative error of at most 0.0028.
Values sent between devices are 32-bit elements; how exact they have to be, the bound alone decides.
No kernel may reach another device: no remote copies, remote signals or barrier semaphores. Data moves between devices by JAX's collectives and lax.ppermute only.
A program may use at most 64 MiB of HBM per device.

v0:
```python
import jax
import jax.numpy as jnp
from jax import lax
from jax.sharding import PartitionSpec as P

COARSE_SWEEPS = 4


relax_factor = 0.8


def extended(shard, sides, width):
    for axis, dim in sides:
        peers, length = (lax.axis_size(axis), shard.shape[dim])
        up = [(i, (i + 1) % peers) for i in range(peers)]
        down = [(j, i) for i, j in up]
        last = lax.slice_in_dim(shard, length - width, length, axis=dim)
        first = lax.slice_in_dim(shard, 0, width, axis=dim)
        before = lax.ppermute(last, axis, up)
        after = lax.ppermute(first, axis, down)
        shard = jnp.concatenate([before, shard, after], axis=dim)
    return shard


def blend_set(land_share, coefficient_sets, column):
    sea_value = coefficient_sets[0, column][:, None, None]
    land_value = coefficient_sets[1, column][:, None, None]
    return sea_value + land_share * (land_value - sea_value)


def mean_four(blocks):
    return 0.25 * (
        blocks[:, 0::2, 0::2]
        + blocks[:, 0::2, 1::2]
        + blocks[:, 1::2, 0::2]
        + blocks[:, 1::2, 1::2]
    )


def coarsen(coeffs):
    reaction, face_east, face_west, face_north, face_south, face_upper, face_lower = coeffs
    east_coarse = 0.25 * (face_east[:, 0::2, 1::2] + face_east[:, 1::2, 1::2])
    west_coarse = 0.25 * (face_west[:, 0::2, 0::2] + face_west[:, 1::2, 0::2])
    north_coarse = 0.25 * (face_north[:, 1::2, 0::2] + face_north[:, 1::2, 1::2])
    south_coarse = 0.25 * (face_south[:, 0::2, 0::2] + face_south[:, 0::2, 1::2])
    return (
        mean_four(reaction),
        east_coarse,
        west_coarse,
        north_coarse,
        south_coarse,
        mean_four(face_upper),
        mean_four(face_lower),
    )


def diagonal_of(coeffs):
    return coeffs[0] + coeffs[1] + coeffs[2] + coeffs[3] + coeffs[4] + coeffs[5] + coeffs[6]


def prolong(source):
    return jnp.repeat(jnp.repeat(source, 2, axis=1), 2, axis=2)


def operate(source, padded, coeffs):
    reaction, face_east, face_west, face_north, face_south, face_upper, face_lower = coeffs
    vertical = jnp.pad(source, ((1, 1), (0, 0), (0, 0)))
    applied = reaction * source
    applied = applied + face_east * (source - padded[:, 1:-1, 2:])
    applied = applied + face_west * (source - padded[:, 1:-1, :-2])
    applied = applied + face_north * (source - padded[:, 2:, 1:-1])
    applied = applied + face_south * (source - padded[:, :-2, 1:-1])
    applied = applied + face_upper * (source - vertical[2:])
    applied = applied + face_lower * (source - vertical[:-2])
    return applied


def shards(right_side, initial_guess, land_mask, coefficient_sets):
    lat_index = lax.axis_index("lat")
    lat_count = lax.axis_size("lat")

    def open_edges(padded):
        row_count = padded.shape[-2]
        row_ids = lax.broadcasted_iota(jnp.int32, (row_count, 1), 0)
        outside = (row_ids == 0) & (lat_index == 0) | (row_ids == row_count - 1) & (
            lat_index == lat_count - 1
        )
        return jnp.where(outside, jnp.float32(0.0), padded)

    def field_rims(source):
        return open_edges(extended(source, (("lat", 1), ("lon", 2)), 1))

    reaction = blend_set(land_mask, coefficient_sets, 0)
    lon_weight = blend_set(land_mask, coefficient_sets, 1)
    lat_weight = blend_set(land_mask, coefficient_sets, 2)
    lev_weight = blend_set(land_mask, coefficient_sets, 3)
    stacked = jnp.stack([lon_weight, lat_weight])
    weight_pad = open_edges(extended(stacked, (("lat", 2), ("lon", 3)), 1))
    face_east = 0.5 * (lon_weight + weight_pad[0, :, 1:-1, 2:])
    face_west = 0.5 * (lon_weight + weight_pad[0, :, 1:-1, :-2])
    face_north = 0.5 * (lat_weight + weight_pad[1, :, 2:, 1:-1])
    face_south = 0.5 * (lat_weight + weight_pad[1, :, :-2, 1:-1])
    lev_pad = jnp.pad(lev_weight, ((1, 1), (0, 0), (0, 0)))
    face_upper = 0.5 * (lev_weight + lev_pad[2:])
    face_lower = 0.5 * (lev_weight + lev_pad[:-2])
    fine_coeffs = (reaction, face_east, face_west, face_north, face_south, face_upper, face_lower)
    mid_coeffs = coarsen(fine_coeffs)
    coarse_coeffs = coarsen(mid_coeffs)
    fine_diag = diagonal_of(fine_coeffs)
    mid_diag = diagonal_of(mid_coeffs)
    coarse_diag = diagonal_of(coarse_coeffs)

    def coarse_solve(rhs_coarse):
        coarse_corr = relax_factor * rhs_coarse / coarse_diag
        for sweep_index in range(COARSE_SWEEPS - 1):
            padded = open_edges(extended(coarse_corr, (("lat", 1), ("lon", 2)), 1))
            coarse_corr = (
                coarse_corr
                + relax_factor
                * (rhs_coarse - operate(coarse_corr, padded, coarse_coeffs))
                / coarse_diag
            )
        return coarse_corr

    def vcycle(rhs_fine):
        fine_corr = relax_factor * rhs_fine / fine_diag
        rhs_mid = mean_four(rhs_fine - operate(fine_corr, field_rims(fine_corr), fine_coeffs))
        mid_corr = relax_factor * rhs_mid / mid_diag
        rhs_coarse = mean_four(rhs_mid - operate(mid_corr, field_rims(mid_corr), mid_coeffs))
        coarse_corr = coarse_solve(rhs_coarse)
        mid_corr = mid_corr + prolong(coarse_corr)
        mid_corr = (
            mid_corr
            + relax_factor
            * (rhs_mid - operate(mid_corr, field_rims(mid_corr), mid_coeffs))
            / mid_diag
        )
        fine_corr = fine_corr + prolong(mid_corr)
        fine_corr = (
            fine_corr
            + relax_factor
            * (rhs_fine - operate(fine_corr, field_rims(fine_corr), fine_coeffs))
            / fine_diag
        )
        return fine_corr

    def precond_total(first, second):
        return lax.psum(jnp.sum(first * second), ("lon", "lat"))

    start = right_side - operate(initial_guess, field_rims(initial_guess), fine_coeffs)
    precond = vcycle(start)
    precond_dot = precond_total(start, precond)
    image_dir = operate(precond, field_rims(precond), fine_coeffs)
    curvature = lax.psum(jnp.sum(precond * image_dir), ("lon", "lat"))
    step_length = precond_dot / curvature
    iterate = initial_guess + step_length * precond
    residual = start - step_length * image_dir
    precond_next = vcycle(residual)
    next_dot = precond_total(residual, precond_next)
    direction = precond_next + next_dot / precond_dot * precond
    return (iterate, residual, direction)


def solution(mesh):
    in_specs = (P(None, "lat", "lon"), P(None, "lat", "lon"), P(None, "lat", "lon"), P())
    out_specs = (P(None, "lat", "lon"), P(None, "lat", "lon"), P(None, "lat", "lon"))
    return jax.shard_map(shards, mesh=mesh, in_specs=in_specs, out_specs=out_specs, check_vma=False)
```

profile of v0, /device:TPU:1, one launch (start us, length us, event | category | flops | bytes accessed | tf_op | source)
XLA Modules:
  0.0 647.7 jit_solution(212301930645227232)
XLA Ops:
  16.8 7.9 %collective-permute-start.7 = (f32[16,10,1]{2,0,1:T(8,128)S(1)}, f32[16,10,1]{2,0,1:T(8,128)S(1)}, u32[]{:S(2)}, u32[]{:S(2)}) collective-permute-start(f32[16,10,1]{2,0,1:T(8,128)S(1)} %get-tuple-element.69), channel_id=1, source_target_pairs={{8,0},{16,8},{24,16},{32,24},{40,32},{48,40},{56,48},{64,56},{72,6... | collective-permute-start | bytes 1928 | tf_op jit(solution)/shard_map/ppermute | solution.py:20
  28.9 7.0 %collective-permute-start.3 = (f32[2,16,10,1]{3,1,2,0:T(8,128)S(1)}, f32[2,16,10,1]{3,1,2,0:T(8,128)S(1)}, u32[]{:S(2)}, u32[]{:S(2)}) collective-permute-start(f32[2,16,10,1]{3,1,2,0:T(8,128)S(1)} %get-tuple-element.55), channel_id=1, source_target_pairs={{8,0},{16,8},{24,16},{32,24},{40,32},{48,40},{56,48},{64,56},{72,6... | collective-permute-start | bytes 3848 | tf_op jit(solution)/shard_map/ppermute | solution.py:20
  79.8 7.4 %collective-permute-start.11 = (f32[16,10,1]{2,0,1:T(8,128)S(1)}, f32[16,10,1]{2,0,1:T(8,128)}, u32[]{:S(2)}, u32[]{:S(2)}) collective-permute-start(f32[16,10,1]{2,0,1:T(8,128)S(1)} %get-tuple-element.67), channel_id=1, source_target_pairs={{8,0},{16,8},{24,16},{32,24},{40,32},{48,40},{56,48},{64,56},{72,6... | collective-permute-start | bytes 1928 | tf_op jit(solution)/shard_map/ppermute | solution.py:20
  156.4 6.9 %collective-permute-start.15 = (f32[16,6,1]{2,0,1:T(8,128)S(1)}, f32[16,6,1]{2,0,1:T(8,128)}, u32[]{:S(2)}, u32[]{:S(2)}) collective-permute-start(f32[16,6,1]{2,0,1:T(8,128)S(1)} %get-tuple-element.94), channel_id=1, source_target_pairs={{8,0},{16,8},{24,16},{32,24},{40,32},{48,40},{56,48},{64,56},{72,6... | collective-permute-start | bytes 1160 | tf_op jit(solution)/shard_map/ppermute | solution.py:20
  180.1 6.7 %collective-permute-start.19 = (f32[16,4,1]{2,0,1:T(8,128)S(1)}, f32[16,4,1]{2,0,1:T(8,128)S(1)}, u32[]{:S(2)}, u32[]{:S(2)}) collective-permute-start(f32[16,4,1]{2,0,1:T(8,128)S(1)} %get-tuple-element.114), channel_id=1, source_target_pairs={{8,0},{16,8},{24,16},{32,24},{40,32},{48,40},{56,48},{64,56},{72,6... | collective-permute-start | bytes 776 | tf_op jit(solution)/shard_map/ppermute | solution.py:20
  194.4 7.3 %collective-permute-start.23 = (f32[16,4,1]{2,0,1:T(8,128)S(1)}, f32[16,4,1]{2,0,1:T(8,128)S(1)}, u32[]{:S(2)}, u32[]{:S(2)}) collective-permute-start(f32[16,4,1]{2,0,1:T(8,128)S(1)} %get-tuple-element.112), channel_id=1, source_target_pairs={{8,0},{16,8},{24,16},{32,24},{40,32},{48,40},{56,48},{64,56},{72,6... | collective-permute-start | bytes 776 | tf_op jit(solution)/shard_map/ppermute | solution.py:20
  210.1 7.3 %collective-permute-start.27 = (f32[16,4,1]{2,0,1:T(8,128)S(1)}, f32[16,4,1]{2,0,1:T(8,128)S(1)}, u32[]{:S(2)}, u32[]{:S(2)}) collective-permute-start(f32[16,4,1]{2,0,1:T(8,128)S(1)} %get-tuple-element.110), channel_id=1, source_target_pairs={{8,0},{16,8},{24,16},{32,24},{40,32},{48,40},{56,48},{64,56},{72,6... | collective-permute-start | bytes 776 | tf_op jit(solution)/shard_map/ppermute | solution.py:20
  220.9 4.3 collective-permute-start.29
  228.1 7.3 %collective-permute-start.31 = (f32[16,6,1]{2,0,1:T(8,128)S(1)}, f32[16,6,1]{2,0,1:T(8,128)S(1)}, u32[]{:S(2)}, u32[]{:S(2)}) collective-permute-start(f32[16,6,1]{2,0,1:T(8,128)S(1)} %get-tuple-element.92), channel_id=1, source_target_pairs={{8,0},{16,8},{24,16},{32,24},{40,32},{48,40},{56,48},{64,56},{72,6... | collective-permute-start | bytes 1160 | tf_op jit(solution)/shard_map/ppermute | solution.py:20
  243.5 4.4 collective-permute-start.33
  250.8 7.3 %collective-permute-start.35 = (f32[16,10,1]{2,0,1:T(8,128)S(1)}, f32[16,10,1]{2,0,1:T(8,128)S(1)}, u32[]{:S(2)}, u32[]{:S(2)}) collective-permute-start(f32[16,10,1]{2,0,1:T(8,128)S(1)} %get-tuple-element.65), channel_id=1, source_target_pairs={{8,0},{16,8},{24,16},{32,24},{40,32},{48,40},{56,48},{64,56},{72,6... | collective-permute-start | bytes 1928 | tf_op jit(solution)/shard_map/ppermute | solution.py:20
  260.5 4.7 collective-permute-start.37
  268.1 7.5 %collective-permute-start.39 = (f32[16,10,1]{2,0,1:T(8,128)S(1)}, f32[16,10,1]{2,0,1:T(8,128)S(1)}, u32[]{:S(2)}, u32[]{:S(2)}) collective-permute-start(f32[16,10,1]{2,0,1:T(8,128)S(1)} %get-tuple-element.63), channel_id=1, source_target_pairs={{8,0},{16,8},{24,16},{32,24},{40,32},{48,40},{56,48},{64,56},{72,6... | collective-permute-start | bytes 1928 | tf_op jit(solution)/shard_map/ppermute | solution.py:20
  279.0 107.5 %all-reduce.17 = (f32[]{:T(128)}, f32[]{:T(128)}) all-reduce(f32[]{:T(128)} %get-tuple-element.13, f32[]{:T(128)} %get-tuple-element.12), channel_id=1, replica_groups=mesh['lon'=64,'lat'=8] {'lon','lat'}, use_global_device_ids=true, to_apply=%region_1.2 | all-reduce | flops 2 | bytes 16 | tf_op jit(solution)/shard_map/psum | solution.py:148
  394.3 6.7 %collective-permute-start.43 = (f32[16,10,1]{2,0,1:T(8,128)S(1)}, f32[16,10,1]{2,0,1:T(8,128)S(1)}, u32[]{:S(2)}, u32[]{:S(2)}) collective-permute-start(f32[16,10,1]{2,0,1:T(8,128)S(1)} %get-tuple-element.61), channel_id=1, source_target_pairs={{8,0},{16,8},{24,16},{32,24},{40,32},{48,40},{56,48},{64,56},{72,6... | collective-permute-start | bytes 1928 | tf_op jit(solution)/shard_map/ppermute | solution.py:20
  427.4 7.4 %collective-permute-start.47 = (f32[16,6,1]{2,0,1:T(8,128)S(1)}, f32[16,6,1]{2,0,1:T(8,128)S(1)}, u32[]{:S(2)}, u32[]{:S(2)}) collective-permute-start(f32[16,6,1]{2,0,1:T(8,128)S(1)} %get-tuple-element.90), channel_id=1, source_target_pairs={{8,0},{16,8},{24,16},{32,24},{40,32},{48,40},{56,48},{64,56},{72,6... | collective-permute-start | bytes 1160 | tf_op jit(solution)/shard_map/ppermute | solution.py:20
  452.2 7.3 %collective-permute-start.51 = (f32[16,4,1]{2,0,1:T(8,128)S(1)}, f32[16,4,1]{2,0,1:T(8,128)S(1)}, u32[]{:S(2)}, u32[]{:S(2)}) collective-permute-start(f32[16,4,1]{2,0,1:T(8,128)S(1)} %get-tuple-element.108), channel_id=1, source_target_pairs={{8,0},{16,8},{24,16},{32,24},{40,32},{48,40},{56,48},{64,56},{72,6... | collective-permute-start | bytes 776 | tf_op jit(solution)/shard_map/ppermute | solution.py:20
  468.8 7.3 %collective-permute-start.55 = (f32[16,4,1]{2,0,1:T(8,128)S(1)}, f32[16,4,1]{2,0,1:T(8,128)S(1)}, u32[]{:S(2)}, u32[]{:S(2)}) collective-permute-start(f32[16,4,1]{2,0,1:T(8,128)S(1)} %get-tuple-element.106), channel_id=1, source_target_pairs={{8,0},{16,8},{24,16},{32,24},{40,32},{48,40},{56,48},{64,56},{72,6... | collective-permute-start | bytes 776 | tf_op jit(solution)/shard_map/ppermute | solution.py:20
  477.4 4.3 collective-permute-start.57
  484.6 7.5 %collective-permute-start.59 = (f32[16,4,1]{2,0,1:T(8,128)S(1)}, f32[16,4,1]{2,0,1:T(8,128)S(1)}, u32[]{:S(2)}, u32[]{:S(2)}) collective-permute-start(f32[16,4,1]{2,0,1:T(8,128)S(1)} %get-tuple-element.104), channel_id=1, source_target_pairs={{8,0},{16,8},{24,16},{32,24},{40,32},{48,40},{56,48},{64,56},{72,6... | collective-permute-start | bytes 776 | tf_op jit(solution)/shard_map/ppermute | solution.py:20
  505.6 7.3 %collective-permute-start.63 = (f32[16,6,1]{2,0,1:T(8,128)S(1)}, f32[16,6,1]{2,0,1:T(8,128)S(1)}, u32[]{:S(2)}, u32[]{:S(2)}) collective-permute-start(f32[16,6,1]{2,0,1:T(8,128)S(1)} %get-tuple-element.88), channel_id=1, source_target_pairs={{8,0},{16,8},{24,16},{32,24},{40,32},{48,40},{56,48},{64,56},{72,6... | collective-permute-start | bytes 1160 | tf_op jit(solution)/shard_map/ppermute | solution.py:20
  520.4 4.4 collective-permute-start.65
  527.7 7.3 %collective-permute-start.67 = (f32[16,10,1]{2,0,1:T(8,128)S(1)}, f32[16,10,1]{2,0,1:T(8,128)S(1)}, u32[]{:S(2)}, u32[]{:S(2)}) collective-permute-start(f32[16,10,1]{2,0,1:T(8,128)S(1)} %get-tuple-element.59), channel_id=1, source_target_pairs={{8,0},{16,8},{24,16},{32,24},{40,32},{48,40},{56,48},{64,56},{72,6... | collective-permute-start | bytes 1928 | tf_op jit(solution)/shard_map/ppermute | solution.py:20
  537.9 107.4 %psum.23 = f32[]{:T(128)} all-reduce(f32[]{:T(128)} %get-tuple-element.16), channel_id=1, replica_groups=mesh['lon'=64,'lat'=8] {'lon','lat'}, use_global_device_ids=true, to_apply=%region_5.6 | all-reduce | flops 1 | bytes 8 | tf_op jit(solution)/shard_map/psum | solution.py:148
  (404 shorter events, 282.3 us)
Async XLA Ops:
  1.7 12.9 %collective-permute-start.4 = (f32[16,1,512]{2,0,1:T(8,128)S(1)}, f32[16,1,512]{2,0,1:T(8,128)S(1)}, u32[]{:S(2)}, u32[]{:S(2)}) collective-permute-start(f32[16,1,512]{2,0,1:T(8,128)S(1)} %copy.347), channel_id=1, source_target_pairs={{0,1},{1,2},{2,3},{3,4},{4,5},{5,6},{6,7},{7,0},{8,9},{9,10},{10,1... | collective-permute-start | bytes 98312 | tf_op jit(solution)/shard_map/ppermute | solution.py:19
  4.4 10.4 %collective-permute-start.5 = (f32[16,1,512]{2,0,1:T(8,128)S(1)}, f32[16,1,512]{2,0,1:T(8,128)S(1)}, u32[]{:S(2)}, u32[]{:S(2)}) collective-permute-start(f32[16,1,512]{2,0,1:T(8,128)S(1)} %copy.348), channel_id=1, source_target_pairs={{1,0},{2,1},{3,2},{4,3},{5,4},{6,5},{7,6},{0,7},{9,8},{10,9},{11,1... | collective-permute-start | bytes 98312 | tf_op jit(solution)/shard_map/ppermute | solution.py:20
  11.6 15.2 %collective-permute-start.1 = (f32[2,16,1,512]{3,2,1,0:T(1,128)S(1)}, f32[2,16,1,512]{3,2,1,0:T(1,128)S(1)}, u32[]{:S(2)}, u32[]{:S(2)}) collective-permute-start(f32[2,16,1,512]{3,2,1,0:T(1,128)S(1)} %get-tuple-element.56), channel_id=1, source_target_pairs={{1,0},{2,1},{3,2},{4,3},{5,4},{6,5},{7,6},{0,7},{9,8},{10,9},{11,1... | collective-permute-start | bytes 196616 | tf_op jit(solution)/shard_map/ppermute | solution.py:20
  14.6 11.9 %collective-permute-start = (f32[2,16,1,512]{3,2,1,0:T(1,128)S(1)}, f32[2,16,1,512]{3,2,1,0:T(1,128)S(1)}, u32[]{:S(2)}, u32[]{:S(2)}) collective-permute-start(f32[2,16,1,512]{3,2,1,0:T(1,128)S(1)} %get-tuple-element.57), channel_id=1, source_target_pairs={{0,1},{1,2},{2,3},{3,4},{4,5},{5,6},{6,7},{7,0},{8,9},{9,10},{10,1... | collective-permute-start | bytes 196616 | tf_op jit(solution)/shard_map/ppermute | solution.py:19
  14.9 10.3 %collective-permute-start.6 = (f32[16,10,1]{2,0,1:T(8,128)S(1)}, f32[16,10,1]{2,0,1:T(8,128)S(1)}, u32[]{:S(2)}, u32[]{:S(2)}) collective-permute-start(f32[16,10,1]{2,0,1:T(8,128)S(1)} %get-tuple-element.68), channel_id=1, source_target_pairs={{0,8},{8,16},{16,24},{24,32},{32,40},{40,48},{48,56},{56,64},{64,7... | collective-permute-start | bytes 1928 | tf_op jit(solution)/shard_map/ppermute | solution.py:19
  16.8 9.4 %collective-permute-start.7 = (f32[16,10,1]{2,0,1:T(8,128)S(1)}, f32[16,10,1]{2,0,1:T(8,128)S(1)}, u32[]{:S(2)}, u32[]{:S(2)}) collective-permute-start(f32[16,10,1]{2,0,1:T(8,128)S(1)} %get-tuple-element.69), channel_id=1, source_target_pairs={{8,0},{16,8},{24,16},{32,24},{40,32},{48,40},{56,48},{64,56},{72,6... | collective-permute-start | bytes 1928 | tf_op jit(solution)/shard_map/ppermute | solution.py:20
  26.9 9.7 %collective-permute-start.2 = (f32[2,16,10,1]{3,1,2,0:T(8,128)S(1)}, f32[2,16,10,1]{3,1,2,0:T(8,128)S(1)}, u32[]{:S(2)}, u32[]{:S(2)}) collective-permute-start(f32[2,16,10,1]{3,1,2,0:T(8,128)S(1)} %get-tuple-element.54), channel_id=1, source_target_pairs={{0,8},{8,16},{16,24},{24,32},{32,40},{40,48},{48,56},{56,64},{64,7... | collective-permute-start | bytes 3848 | tf_op jit(solution)/shard_map/ppermute | solution.py:19
  28.9 9.3 %collective-permute-start.3 = (f32[2,16,10,1]{3,1,2,0:T(8,128)S(1)}, f32[2,16,10,1]{3,1,2,0:T(8,128)S(1)}, u32[]{:S(2)}, u32[]{:S(2)}) collective-permute-start(f32[2,16,10,1]{3,1,2,0:T(8,128)S(1)} %get-tuple-element.55), channel_id=1, source_target_pairs={{8,0},{16,8},{24,16},{32,24},{40,32},{48,40},{56,48},{64,56},{72,6... | collective-permute-start | bytes 3848 | tf_op jit(solution)/shard_map/ppermute | solution.py:20
  40.3 33.5 %collective-permute-start.8 = (f32[16,1,512]{2,1,0:T(1,128)S(1)}, f32[16,1,512]{2,1,0:T(1,128)S(1)}, u32[]{:S(2)}, u32[]{:S(2)}) collective-permute-start(f32[16,1,512]{2,1,0:T(1,128)S(1)} %get-tuple-element.81), channel_id=1, source_target_pairs={{0,1},{1,2},{2,3},{3,4},{4,5},{5,6},{6,7},{7,0},{8,9},{9,10},{10,1... | collective-permute-start | bytes 98312 | tf_op jit(solution)/shard_map/ppermute | solution.py:19
  77.9 39.0 %collective-permute-start.10 = (f32[16,10,1]{2,0,1:T(8,128)}, f32[16,10,1]{2,0,1:T(8,128)S(1)}, u32[]{:S(2)}, u32[]{:S(2)}) collective-permute-start(f32[16,10,1]{2,0,1:T(8,128)} %get-tuple-element.66), channel_id=1, source_target_pairs={{0,8},{8,16},{16,24},{24,32},{32,40},{40,48},{48,56},{56,64},{64,7... | collective-permute-start | bytes 1928 | tf_op jit(solution)/shard_map/ppermute | solution.py:19
  79.8 37.1 %collective-permute-start.11 = (f32[16,10,1]{2,0,1:T(8,128)S(1)}, f32[16,10,1]{2,0,1:T(8,128)}, u32[]{:S(2)}, u32[]{:S(2)}) collective-permute-start(f32[16,10,1]{2,0,1:T(8,128)S(1)} %get-tuple-element.67), channel_id=1, source_target_pairs={{8,0},{16,8},{24,16},{32,24},{40,32},{48,40},{56,48},{64,56},{72,6... | collective-permute-start | bytes 1928 | tf_op jit(solution)/shard_map/ppermute | solution.py:20
  132.5 19.0 %collective-permute-start.12 = (f32[16,1,256]{2,1,0:T(1,128)S(1)}, f32[16,1,256]{2,1,0:T(1,128)S(1)}, u32[]{:S(2)}, u32[]{:S(2)}) collective-permute-start(f32[16,1,256]{2,1,0:T(1,128)S(1)} %get-tuple-element.102), channel_id=1, source_target_pairs={{0,1},{1,2},{2,3},{3,4},{4,5},{5,6},{6,7},{7,0},{8,9},{9,10},{10,1... | collective-permute-start | bytes 49160 | tf_op jit(solution)/shard_map/ppermute | solution.py:19
  154.5 14.9 %collective-permute-start.14 = (f32[16,6,1]{2,0,1:T(8,128)S(1)}, f32[16,6,1]{2,0,1:T(8,128)S(1)}, u32[]{:S(2)}, u32[]{:S(2)}) collective-permute-start(f32[16,6,1]{2,0,1:T(8,128)S(1)} %get-tuple-element.93), channel_id=1, source_target_pairs={{0,8},{8,16},{16,24},{24,32},{32,40},{40,48},{48,56},{56,64},{64,7... | collective-permute-start | bytes 1160 | tf_op jit(solution)/shard_map/ppermute | solution.py:19
  156.4 13.0 %collective-permute-start.15 = (f32[16,6,1]{2,0,1:T(8,128)S(1)}, f32[16,6,1]{2,0,1:T(8,128)}, u32[]{:S(2)}, u32[]{:S(2)}) collective-permute-start(f32[16,6,1]{2,0,1:T(8,128)S(1)} %get-tuple-element.94), channel_id=1, source_target_pairs={{8,0},{16,8},{24,16},{32,24},{40,32},{48,40},{56,48},{64,56},{72,6... | collective-permute-start | bytes 1160 | tf_op jit(solution)/shard_map/ppermute | solution.py:20
  192.5 9.2 %collective-permute-start.22 = (f32[16,4,1]{2,0,1:T(8,128)S(1)}, f32[16,4,1]{2,0,1:T(8,128)S(1)}, u32[]{:S(2)}, u32[]{:S(2)}) collective-permute-start(f32[16,4,1]{2,0,1:T(8,128)S(1)} %get-tuple-element.111), channel_id=1, source_target_pairs={{0,8},{8,16},{16,24},{24,32},{32,40},{40,48},{48,56},{56,64},{64,7... | collective-permute-start | bytes 776 | tf_op jit(solution)/shard_map/ppermute | solution.py:19
  208.2 9.2 %collective-permute-start.26 = (f32[16,4,1]{2,0,1:T(8,128)S(1)}, f32[16,4,1]{2,0,1:T(8,128)S(1)}, u32[]{:S(2)}, u32[]{:S(2)}) collective-permute-start(f32[16,4,1]{2,0,1:T(8,128)S(1)} %get-tuple-element.109), channel_id=1, source_target_pairs={{0,8},{8,16},{16,24},{24,32},{32,40},{40,48},{48,56},{56,64},{64,7... | collective-permute-start | bytes 776 | tf_op jit(solution)/shard_map/ppermute | solution.py:19
  226.2 9.2 %collective-permute-start.30 = (f32[16,6,1]{2,0,1:T(8,128)S(1)}, f32[16,6,1]{2,0,1:T(8,128)S(1)}, u32[]{:S(2)}, u32[]{:S(2)}) collective-permute-start(f32[16,6,1]{2,0,1:T(8,128)S(1)} %get-tuple-element.91), channel_id=1, source_target_pairs={{0,8},{8,16},{16,24},{24,32},{32,40},{40,48},{48,56},{56,64},{64,7... | collective-permute-start | bytes 1160 | tf_op jit(solution)/shard_map/ppermute | solution.py:19
  248.9 9.2 %collective-permute-start.34 = (f32[16,10,1]{2,0,1:T(8,128)S(1)}, f32[16,10,1]{2,0,1:T(8,128)S(1)}, u32[]{:S(2)}, u32[]{:S(2)}) collective-permute-start(f32[16,10,1]{2,0,1:T(8,128)S(1)} %get-tuple-element.64), channel_id=1, source_target_pairs={{0,8},{8,16},{16,24},{24,32},{32,40},{40,48},{48,56},{56,64},{64,7... | collective-permute-start | bytes 1928 | tf_op jit(solution)/shard_map/ppermute | solution.py:19
  266.2 9.5 %collective-permute-start.38 = (f32[16,10,1]{2,0,1:T(8,128)S(1)}, f32[16,10,1]{2,0,1:T(8,128)S(1)}, u32[]{:S(2)}, u32[]{:S(2)}) collective-permute-start(f32[16,10,1]{2,0,1:T(8,128)S(1)} %get-tuple-element.62), channel_id=1, source_target_pairs={{0,8},{8,16},{16,24},{24,32},{32,40},{40,48},{48,56},{56,64},{64,7... | collective-permute-start | bytes 1928 | tf_op jit(solution)/shard_map/ppermute | solution.py:19
  425.4 9.4 %collective-permute-start.46 = (f32[16,6,1]{2,0,1:T(8,128)S(1)}, f32[16,6,1]{2,0,1:T(8,128)S(1)}, u32[]{:S(2)}, u32[]{:S(2)}) collective-permute-start(f32[16,6,1]{2,0,1:T(8,128)S(1)} %get-tuple-element.89), channel_id=1, source_target_pairs={{0,8},{8,16},{16,24},{24,32},{32,40},{40,48},{48,56},{56,64},{64,7... | collective-permute-start | bytes 1160 | tf_op jit(solution)/shard_map/ppermute | solution.py:19
  450.3 9.2 %collective-permute-start.50 = (f32[16,4,1]{2,0,1:T(8,128)S(1)}, f32[16,4,1]{2,0,1:T(8,128)S(1)}, u32[]{:S(2)}, u32[]{:S(2)}) collective-permute-start(f32[16,4,1]{2,0,1:T(8,128)S(1)} %get-tuple-element.107), channel_id=1, source_target_pairs={{0,8},{8,16},{16,24},{24,32},{32,40},{40,48},{48,56},{56,64},{64,7... | collective-permute-start | bytes 776 | tf_op jit(solution)/shard_map/ppermute | solution.py:19
  482.7 9.4 %collective-permute-start.58 = (f32[16,4,1]{2,0,1:T(8,128)S(1)}, f32[16,4,1]{2,0,1:T(8,128)S(1)}, u32[]{:S(2)}, u32[]{:S(2)}) collective-permute-start(f32[16,4,1]{2,0,1:T(8,128)S(1)} %get-tuple-element.103), channel_id=1, source_target_pairs={{0,8},{8,16},{16,24},{24,32},{32,40},{40,48},{48,56},{56,64},{64,7... | collective-permute-start | bytes 776 | tf_op jit(solution)/shard_map/ppermute | solution.py:19
  503.7 9.2 %collective-permute-start.62 = (f32[16,6,1]{2,0,1:T(8,128)S(1)}, f32[16,6,1]{2,0,1:T(8,128)S(1)}, u32[]{:S(2)}, u32[]{:S(2)}) collective-permute-start(f32[16,6,1]{2,0,1:T(8,128)S(1)} %get-tuple-element.87), channel_id=1, source_target_pairs={{0,8},{8,16},{16,24},{24,32},{32,40},{40,48},{48,56},{56,64},{64,7... | collective-permute-start | bytes 1160 | tf_op jit(solution)/shard_map/ppermute | solution.py:19
  525.8 9.2 %collective-permute-start.66 = (f32[16,10,1]{2,0,1:T(8,128)S(1)}, f32[16,10,1]{2,0,1:T(8,128)S(1)}, u32[]{:S(2)}, u32[]{:S(2)}) collective-permute-start(f32[16,10,1]{2,0,1:T(8,128)S(1)} %get-tuple-element.58), channel_id=1, source_target_pairs={{0,8},{8,16},{16,24},{24,32},{32,40},{40,48},{48,56},{56,64},{64,7... | collective-permute-start | bytes 1928 | tf_op jit(solution)/shard_map/ppermute | solution.py:19
  (79 other events, 1371.1 us)
where the time goes:
time: 653 us; the launch traced here: 648 us
  starting transfers between devices  219 us (34%)
  blocking collectives  215 us (33%)
  local copies, waits for them, and re-layouts  142 us (22%)
  waiting for transfers between devices  37.9 us (6%)
  other arithmetic  28.5 us (4%)
    psum x2, blocking collectives, precond_total(): return lax.psum(jnp.sum(first * second), ('lon', 'lat'))  215 us
    ppermute x34, starting transfers between devices, extended(): after = lax.ppermute(first, axis, down)  173 us
    ppermute x34, starting transfers between devices, extended(): before = lax.ppermute(last, axis, up)  45.7 us
    ppermute x34, waiting for transfers between devices, extended(): after = lax.ppermute(first, axis, down)  28.3 us
    slice x10, local copies, waits for them, and re-layouts, mean_four(): blocks[:, 0::2, 1::2]  22.2 us
    slice x10, local copies, waits for them, and re-layouts, mean_four(): blocks[:, 0::2, 0::2] + blocks[:, 0::2, 1::2] + blocks[:, 1::2, 0::2]  22 us
    slice x10, local copies, waits for them, and re-layouts, mean_four(): blocks[:, 1::2, 0::2]  21.8 us
    slice x10, local copies, waits for them, and re-layouts, mean_four(): blocks[:, 1::2, 1::2]  21.5 us
  transfers between devices with their start and end apart: 68, of which 42 were waited for; matrix products, arithmetic and copies ran while one was open for 14% of the time, Pallas kernels for 0%

commit v1 on v0

v1 whole, which is shorter than its diff:
```python
import jax
import jax.numpy as jnp
import numpy as np
from jax import lax
from jax.experimental import pallas as pl
from jax.experimental.pallas import tpu as pltpu
from jax.sharding import PartitionSpec as P


LEV = 16
ROWS = 8
OWN = 512
HALF = 64
LANES = OWN + 2 * HALF
RIM = 6
EXT = ROWS + 2 * RIM
MID = EXT // 2
SEND = 5
NEAR = 6
COLS = 256
OWN_COLS = OWN // 4
HALF_COLS = HALF // 4
DAMP = 0.8
KEEP = 1.0 - DAMP
F32 = jnp.float32

VMEM = pl.BlockSpec(memory_space=pltpu.VMEM)
HBM = pl.BlockSpec(memory_space=pltpu.HBM)


def call(body, outs, ins, scratch=(), specs=(), copies=0):
    return pl.pallas_call(
        body,
        out_shape=[jax.ShapeDtypeStruct(o, F32) for o in outs],
        in_specs=list(specs) + [VMEM] * (len(ins) - len(specs)),
        out_specs=[VMEM] * len(outs),
        scratch_shapes=[pltpu.VMEM(s, F32) for s in scratch] + [pltpu.SemaphoreType.DMA((copies,))] * (copies > 0),
        compiler_params=pltpu.CompilerParams(vmem_limit_bytes=(60 if copies else 24) * 1024 * 1024),
        cost_estimate=pl.CostEstimate(flops=1000000, bytes_accessed=1000000, transcendentals=0),
    )(*ins)


def loop(first, end, body, unroll=2):
    def step(i, carry):
        body(i)
        return carry

    lax.fori_loop(first, end, step, 0, unroll=unroll)


def lane_ids():
    return lax.broadcasted_iota(jnp.int32, (LEV, LANES), 1)


def next_lane(v, n=1):
    return pltpu.roll(v, v.shape[-1] - n, axis=1)


def prev_lane(v, n=1):
    return pltpu.roll(v, n, axis=1)


def next_level(v):
    return pltpu.roll(v, LEV - 1, axis=0)


def prev_level(v):
    return pltpu.roll(v, 1, axis=0)


def pair_sum(v, even):
    return v + jnp.where(even, next_lane(v), prev_lane(v))


def around(v, i, east, north, upper, n):
    here = v[i]
    total = east[i] * next_lane(here, n) + prev_lane(east[i] * here, n)
    total = total + upper[i] * next_level(here) + prev_level(upper[i] * here)
    return total + north[i] * v[i + 1] + north[i - 1] * v[i - 1]


def blocks_matrix():
    lane = np.arange(LANES)
    cell = lane // 4
    cell = np.where(cell < OWN_COLS + HALF_COLS, cell, cell + COLS - LANES // 4)
    matrix = np.zeros((LANES, COLS), np.float32)
    matrix[lane, cell] = 1.0
    return jnp.asarray(matrix, jnp.bfloat16)


def times_blocks(rows, blocks, side):
    total = 0.0
    left = rows
    for _ in range(3):
        part = left.astype(jnp.bfloat16)
        left = left - part.astype(F32)
        total = total + lax.dot_general(part, blocks[...], (((1,), (side,)), ((), ())), preferred_element_type=F32)
    return total


def pack_kernel(b_ref, x_ref, c_ref, north_ref, south_ref, east_ref, west_ref, held, turned, arrived):
    low_half = lax.broadcasted_iota(jnp.int32, (LEV, 128), 1) < HALF
    copies = [pltpu.make_async_copy(ref, held.at[j], arrived.at[j]) for j, ref in enumerate((b_ref, x_ref, c_ref))]
    for copy in copies:
        copy.start()
    for j, copy in enumerate(copies):
        copy.wait()
        field = jnp.swapaxes(held[j], 0, 1)
        south_ref[:, j] = field[:RIM]
        north_ref[:, j] = field[ROWS - RIM:]
        turned[j, :, :, :128] = field[:, :, :128]
        turned[j, :, :, 128:] = field[:, :, OWN - 128:]
    for r in range(ROWS):
        west_ref[r] = jnp.where(low_half, turned[0, r, :, :128], prev_lane(turned[1, r, :, :128], HALF))
        east_ref[r] = jnp.where(low_half, prev_lane(turned[0, r, :, 128:], HALF), turned[1, r, :, 128:])
    for r in range(ROWS // 2):
        t = r + ROWS // 2
        west_ref[ROWS + r] = jnp.where(low_half, turned[2, r, :, :128], prev_lane(turned[2, t, :, :128], HALF))
        east_ref[ROWS + r] = jnp.where(low_half, prev_lane(turned[2, r, :, 128:], HALF), turned[2, t, :, 128:])


def own_kernel(_, b_ref, x_ref, c_ref, own_ref):
    for j, ref in enumerate((b_ref, x_ref, c_ref)):
        own_ref[:, j] = jnp.swapaxes(ref[...], 0, 1)


def rim_kernel(from_east, from_west, rim_ref, north_ref, south_ref):
    low_half = lax.broadcasted_iota(jnp.int32, (LEV, 128), 1) < HALF

    for r in range(ROWS):
        east, west = from_east[r], from_west[r]
        rim_ref[r, 0] = jnp.where(low_half, east, prev_lane(west, HALF))
        rim_ref[r, 1] = jnp.where(low_half, prev_lane(east, HALF), west)
    for r in range(ROWS // 2):
        east, west = from_east[ROWS + r], from_west[ROWS + r]
        rim_ref[r, 2] = jnp.where(low_half, east, prev_lane(west, HALF))
        rim_ref[r + ROWS // 2, 2] = jnp.where(low_half, prev_lane(east, HALF), west)
    south_ref[...] = rim_ref[:RIM]
    north_ref[...] = rim_ref[ROWS - RIM:]


def restrict(m, f, e0, f1, e1, winv1, east, north, upper, even):
    i = 2 * m
    left_0 = KEEP * f[i] + around(e0, i, east, north, upper, 1)
    left_1 = KEEP * f[i + 1] + around(e0, i + 1, east, north, upper, 1)
    rhs = 0.25 * pair_sum(left_0 + left_1, even)
    f1[m] = rhs
    e1[m] = winv1 * rhs
    return left_0, left_1


def middle_left(m, f1, e1, east1, north1, upper1):
    return KEEP * f1[m] + around(e1, m, east1, north1, upper1, 2)


def hand_out(f2, e2, to_north, to_south):
    to_north[0], to_north[1] = f2[1], e2[0]
    to_south[0], to_south[1] = f2[0], e2[1]


def first_down_kernel(
    own, from_north, from_south, rim, rim_north, rim_south, sets, blocks,
    f2_out, to_north, to_south, weights2, s, e0, f1, e1, east, north, upper, winv, diag, east1, north1, upper1, winv1,
    x, lat_weight, react, react1, stage,
):
    lane = lane_ids()
    even = lane % 2 == 0
    level = lax.broadcasted_iota(jnp.int32, (LEV, LANES), 0)
    top = level == LEV - 1
    edge = top | (level == 0)
    lat = lax.axis_index("lat")
    south_end = lat == 0
    north_end = lat == lax.axis_size("lat") - 1

    def wide(column):
        return jnp.concatenate([sets[column]] * (LANES // 128), axis=1)

    def load(i, main, rims, r):
        share = jnp.concatenate([main[r, 2], rims[r, 2]], axis=1)
        s[i] = jnp.concatenate([main[r, 0], rims[r, 0]], axis=1)
        x[i] = jnp.concatenate([main[r, 1], rims[r, 1]], axis=1)
        lon_weight = wide(1) + share * wide(5)
        east[i] = 0.5 * (lon_weight + next_lane(lon_weight))
        lat_weight[i] = wide(2) + share * wide(6)
        lev_weight = wide(3) + share * wide(7)
        upper[i] = jnp.where(top, 0.0, 0.5 * (lev_weight + next_level(lev_weight)))
        react[i] = wide(0) + share * wide(4) + jnp.where(edge, 0.5 * lev_weight, 0.0)

    loop(0, RIM, lambda r: load(r, from_south, rim_south, r))
    loop(0, ROWS, lambda r: load(r + RIM, own, rim, r))
    loop(0, RIM, lambda r: load(r + RIM + ROWS, from_north, rim_north, r))

    def face(i):
        closed = (south_end & (i == RIM - 1)) | (north_end & (i == RIM + ROWS - 1))
        north[i] = jnp.where(closed, 0.0, 0.5) * (lat_weight[i] + lat_weight[i + 1])

    face(0)

    def start(i):
        face(i)
        at_end = (south_end & (i == RIM)) | (north_end & (i == RIM + ROWS - 1))
        whole = react[i] + jnp.where(at_end, 0.5, 0.0) * lat_weight[i]
        react[i] = whole
        whole = whole + east[i] + prev_lane(east[i]) + north[i] + north[i - 1]
        whole = whole + upper[i] + prev_level(upper[i])
        diag[i] = whole
        inverse = DAMP / whole
        winv[i] = inverse
        left = s[i] - (whole * x[i] - around(x, i, east, north, upper, 1))
        s[i] = left
        e0[i] = inverse * left

    loop(1, EXT - 1, start)

    north1[0] = 0.25 * pair_sum(north[1], even)

    def middle(m):
        i = 2 * m
        react1[m] = 0.25 * pair_sum(react[i] + react[i + 1], even)
        upper1[m] = 0.25 * pair_sum(upper[i] + upper[i + 1], even)
        eastern = east[i] + east[i + 1]
        east1[m] = 0.25 * jnp.where(even, next_lane(eastern), eastern)
        north1[m] = 0.25 * pair_sum(north[i + 1], even)
        whole = react1[m] + east1[m] + prev_lane(east1[m], 2) + north1[m] + north1[m - 1]
        inverse = DAMP / (whole + upper1[m] + prev_level(upper1[m]))
        winv1[m] = inverse
        restrict(m, s, e0, f1, e1, inverse, east, north, upper, even)

    loop(1, MID - 1, middle)

    last_of_four = lane % 4 == 3
    for c in range(4):
        m = 1 + 2 * c
        stage[c] = 0.125 * (react1[m] + react1[m + 1])
        stage[4 + c] = 0.125 * (upper1[m] + upper1[m + 1])
        stage[8 + c] = jnp.where(last_of_four, 0.25 * (east1[m] + east1[m + 1]), 0.0)
    for c in range(5):
        stage[12 + c] = 0.125 * north1[2 * c]
    for c in range(2):
        m = 3 + 2 * c
        left = middle_left(m, f1, e1, east1, north1, upper1)
        stage[17 + c] = 0.125 * (left + middle_left(m + 1, f1, e1, east1, north1, upper1))
    packed = times_blocks(stage[...].reshape(19 * LEV, LANES), blocks, 0).reshape(19, LEV, COLS)
    col = lax.broadcasted_iota(jnp.int32, (LEV, COLS), 1)
    empty = (col >= OWN_COLS + HALF_COLS) & (col < COLS - HALF_COLS)
    for c in range(4):
        upper2, east2, north2 = packed[4 + c], packed[8 + c], packed[13 + c]
        whole = packed[c] + east2 + prev_lane(east2) + north2 + packed[12 + c]
        whole = whole + upper2 + prev_level(upper2)
        weights2[0, 1 + c] = DAMP / jnp.where(empty, 1.0, whole)
        weights2[1, 1 + c] = east2
        weights2[2, 1 + c] = north2
        weights2[3, 1 + c] = upper2
    weights2[2, 0] = packed[12]
    f2 = (packed[17], packed[18])
    f2_out[0], f2_out[1] = f2
    hand_out(f2, (weights2[0, 2] * f2[0], weights2[0, 3] * f2[1]), to_north, to_south)


def sweep(k, f2, now, weights2):
    return KEEP * now[k] + weights2[0, k] * (
        f2[k] + around(now, k, weights2.at[1], weights2.at[2], weights2.at[3], 1)
    )


def two_sweeps(mine, north, south, weights2, f2, now, later):
    f2[1], f2[2], f2[3], f2[4] = south[0], mine[0], mine[1], north[0]
    now[0], now[5] = south[1], north[1]
    for k in range(1, 5):
        now[k] = weights2[0, k] * f2[k]
    for k in range(1, 5):
        later[k] = sweep(k, f2, now, weights2)
    return sweep(2, f2, later, weights2), sweep(3, f2, later, weights2)


def coarse_kernel(mine, from_north, from_south, weights2, f2, e2, now, later):
    e2[0], e2[1] = two_sweeps(mine, from_north, from_south, weights2, f2, now, later)


def coarse_dot_kernel(mine, from_north, from_south, weights2, sums, sum_wq, f2, e2, dots, now, later):
    e2[0], e2[1] = two_sweeps(mine, from_north, from_south, weights2, f2, now, later)
    total = jnp.zeros((LEV, OWN_COLS), F32)
    for r in range(2):
        k = 2 + r
        first = now[k]
        once, twice = later[k], e2[r]
        term = f2[k] * once + (once - first) * (twice - first) / weights2[0, k]
        total = total + term[:, :OWN_COLS]
    column = lax.broadcasted_iota(jnp.int32, dots.shape, 1)
    line = jnp.where(column == 0, jnp.sum(sums[0]), 0.0) + jnp.where(column == 1, jnp.sum(sums[1]), 0.0)
    dots[...] = line + jnp.where(column == 2, jnp.sum(sum_wq[...]) + 16.0 * jnp.sum(total), 0.0)


def ascend(
    e2, e2_north, e2_south, f2, weights2, blocks, first, end, f, e0, f1, e1, winv, east, north, upper,
    winv1, east1, north1, upper1, now, sum1, sum0, result,
):
    for r in range(2):
        now[r], now[2 + r], now[4 + r] = e2_south[r], e2[r], e2_north[r]
    rows = jnp.concatenate([sweep(k, f2, now, weights2) for k in range(1, 5)], axis=0)
    wide = times_blocks(rows, blocks, 1).reshape(4, LEV, LANES)
    for m in range(1, MID - 1):
        sum1[m] = e1[m] + wide[(m - 1) // 2]

    def middle(m):
        better = KEEP * sum1[m] + winv1[m] * (f1[m] + around(sum1, m, east1, north1, upper1, 2))
        sum0[2 * m] = e0[2 * m] + better
        sum0[2 * m + 1] = e0[2 * m + 1] + better

    loop(2, MID - 2, middle)

    def fine(i):
        result[i] = KEEP * sum0[i] + winv[i] * (f[i] + around(sum0, i, east, north, upper, 1))

    loop(first, end, fine)


def first_up_kernel(
    e2, e2_north, e2_south, f2, weights2, blocks,
    s, e0, f1, e1, winv, east, north, upper, winv1, east1, north1, upper1, diag,
    p_own, w_own, w_north, w_south, s_own, sums,
    now, sum1, sum0, p,
):
    ascend(
        e2, e2_north, e2_south, f2, weights2, blocks, RIM - 1, RIM + ROWS + 1, s, e0, f1, e1, winv, east, north, upper,
        winv1, east1, north1, upper1, now, sum1, sum0, p,
    )

    def image(r, totals):
        i = r + RIM
        w_row = diag[i] * p[i] - around(p, i, east, north, upper, 1)
        w_own[r] = w_row
        p_row, s_row = p[i, :, :OWN], s[i, :, :OWN]
        p_own[r] = p_row
        s_own[r] = s_row
        return totals[0] + s_row * p_row, totals[1] + p_row * w_row[:, :OWN]

    zero = jnp.zeros((LEV, OWN), F32)
    sums[0], sums[1] = lax.fori_loop(0, ROWS, image, (zero, zero), unroll=2)
    w_south[...] = w_own[:SEND]
    w_north[...] = w_own[ROWS - SEND:]


def second_down_kernel(
    w_own, from_north, from_south, weights2, blocks, winv, east, north, upper, winv1, east1, north1, upper1,
    f2_out, to_north, to_south, e0, f1, e1, sum_wq,
    w, stage,
):
    even = lane_ids() % 2 == 0
    w[RIM - SEND:RIM] = from_south[...]
    w[RIM + ROWS:RIM + ROWS + SEND] = from_north[...]
    for r in range(ROWS):
        w[RIM + r] = w_own[r]

    def smooth(i):
        e0[i] = winv[i] * w[i]

    loop(1, EXT - 1, smooth)

    def down(m):
        return restrict(m, w, e0, f1, e1, winv1[m], east, north, upper, even)

    loop(1, 3, down)
    loop(7, MID - 1, down)

    def down_own(m, total):
        left_0, left_1 = down(m)
        i = 2 * m
        term = e0[i] * (w[i] + left_0) + e0[i + 1] * (w[i + 1] + left_1)
        return total + term[:, :OWN]

    total = lax.fori_loop(3, 7, down_own, jnp.zeros((LEV, OWN), F32), unroll=2)
    for c in range(2):
        pair = 0.0
        for m in (3 + 2 * c, 4 + 2 * c):
            left = middle_left(m, f1, e1, east1, north1, upper1)
            total = total + 2.0 * (e1[m] * (f1[m] + left))[:, :OWN]
            pair = pair + left
        stage[c] = 0.125 * pair
    sum_wq[...] = total
    packed = times_blocks(stage[...].reshape(2 * LEV, LANES), blocks, 0).reshape(2, LEV, COLS)
    f2 = (packed[0], packed[1])
    f2_out[0], f2_out[1] = f2
    hand_out(f2, (weights2[0, 2] * f2[0], weights2[0, 3] * f2[1]), to_north, to_south)


def second_up_kernel(
    e2, e2_north, e2_south, f2, weights2, blocks,
    w_own, e0, f1, e1, winv, east, north, upper, winv1, east1, north1, upper1, dots,
    q_out, dots_out,
    now, sum1, sum0, w, result,
):
    for r in range(ROWS):
        w[RIM + r] = w_own[r]
    ascend(
        e2, e2_north, e2_south, f2, weights2, blocks, RIM, RIM + ROWS, w, e0, f1, e1, winv, east, north, upper,
        winv1, east1, north1, upper1, now, sum1, sum0, result,
    )
    dots_out[...] = dots[...]
    q_out[...] = jnp.swapaxes(result[RIM:RIM + ROWS, :, :OWN], 0, 1)


def turn_kernel(p, w, s, p_out, w_out, s_out):
    p_out[...] = jnp.swapaxes(p[...], 0, 1)
    w_out[...] = jnp.swapaxes(w[:, :, :OWN], 0, 1)
    s_out[...] = jnp.swapaxes(s[...], 0, 1)


def total_kernel(lines, total):
    total[...] = jnp.broadcast_to(jnp.sum(lines[...], axis=0, keepdims=True), total.shape)


def finish_kernel(dots, x, p, w, q, s, iterate, residual, direction):
    line = jnp.sum(dots[...], axis=0, keepdims=True)
    column = lax.broadcasted_iota(jnp.int32, (1, 128), 1)
    sp, pw, wq = [jnp.sum(jnp.where(column == j, line, 0.0), axis=1, keepdims=True)[None] for j in range(3)]
    step = sp / pw
    next_dot = (sp - step * pw) - step * (pw - step * wq)
    ratio = next_dot / sp
    iterate[...] = x[...] + step * p[...]
    residual[...] = s[...] - step * w[...]
    direction[...] = (p[...] - step * q[...]) + ratio * p[...]


def shards(right_side, initial_guess, land_mask, coefficient_sets):
    lat_size, lon_size = lax.axis_size("lat"), lax.axis_size("lon")

    def trade(to_next, to_last, axis):
        size = lax.axis_size(axis)
        up = [(i, (i + 1) % size) for i in range(size)]
        from_last = lax.ppermute(to_next, axis, up)
        return lax.ppermute(to_last, axis, [(j, i) for i, j in up]), from_last

    row, fine, mid, line = (LEV, LANES), (EXT, LEV, LANES), (MID, LEV, LANES), (LEV, COLS)
    fields = [right_side, initial_guess, land_mask]
    blocks = blocks_matrix()
    to_north, to_south, to_east, to_west = call(
        pack_kernel,
        [(RIM, 3, LEV, OWN)] * 2 + [(12, LEV, 128)] * 2,
        fields,
        [(3, LEV, ROWS, OWN), (3, ROWS, LEV, 256)],
        specs=[HBM] * 3,
        copies=3,
    )
    lat_rows = trade(to_north, to_south, "lat")
    lon_rims = trade(to_east, to_west, "lon")
    (own,) = call(own_kernel, [(ROWS, 3, LEV, OWN)], [to_west] + fields, specs=[HBM])
    rim, to_north, to_south = call(
        rim_kernel, [(ROWS, 3, LEV, 128), (RIM, 3, LEV, 128), (RIM, 3, LEV, 128)], lon_rims
    )
    lat_rims = trade(to_north, to_south, "lat")
    sea, land = coefficient_sets[0], coefficient_sets[1]
    sets = jnp.broadcast_to(jnp.concatenate([sea, land - sea])[:, :, None], (8, LEV, 128))

    (f2, to_north, to_south, weights2, s, e0, f1, e1, east, north, upper, winv, diag, east1, north1, upper1, winv1) = call(
        first_down_kernel,
        [(2,) + line] * 3 + [(4, NEAR) + line, fine, fine, mid, mid, fine, fine, fine, fine, fine, mid, mid, mid, mid],
        [own, *lat_rows, rim, *lat_rims, sets, blocks],
        [fine, fine, fine, mid, (19,) + row],
    )
    grids = [winv, east, north, upper, winv1, east1, north1, upper1]
    near = (NEAR,) + line
    f2_near, e2 = call(
        coarse_kernel, [near, (2,) + line], [f2, *trade(to_north, to_south, "lat"), weights2], [near, near]
    )
    p_own, w_own, to_north, to_south, s_own, sums = call(
        first_up_kernel,
        [(ROWS, LEV, OWN), (ROWS,) + row, (SEND,) + row, (SEND,) + row, (ROWS, LEV, OWN), (2, LEV, OWN)],
        [e2, *trade(e2, e2, "lat"), f2_near, weights2, blocks, s, e0, f1, e1] + grids + [diag],
        [near, mid, fine, fine],
    )
    w_rows = trade(to_north, to_south, "lat")
    p, w, s = call(turn_kernel, [(LEV, ROWS, OWN)] * 3, [p_own, w_own, s_own])
    f2, to_north, to_south, e0, f1, e1, sum_wq = call(
        second_down_kernel,
        [(2,) + line] * 3 + [fine, mid, mid, (LEV, OWN)],
        [w_own, *w_rows, weights2, blocks] + grids,
        [fine, (2,) + row],
    )
    f2_near, e2, dots = call(
        coarse_dot_kernel,
        [near, (2,) + line, (lon_size, 128)],
        [f2, *trade(to_north, to_south, "lat"), weights2, sums, sum_wq],
        [near, near],
    )
    q, dots = call(
        second_up_kernel,
        [(LEV, ROWS, OWN), (lon_size, 128)],
        [e2, *trade(e2, e2, "lat"), f2_near, weights2, blocks, w_own, e0, f1, e1] + grids + [dots],
        [near, mid, fine, fine, fine],
    )
    (dots,) = call(total_kernel, [(lat_size, 128)], [lax.all_to_all(dots, "lon", 0, 0, tiled=True)])
    dots = lax.all_to_all(dots, "lat", 0, 0, tiled=True)
    return tuple(call(finish_kernel, [(LEV, ROWS, OWN)] * 3, [dots, initial_guess, p, w, q, s]))


def solution(mesh):
    field = P(None, "lat", "lon")
    return jax.shard_map(
        shards, mesh=mesh, in_specs=(field, field, field, P()), out_specs=(field, field, field), check_vma=False
    )
```

time: 653 us -> 106 us (0.16)
  blocking collectives: 215 us -> 23.2 us
  starting transfers between devices: 219 us -> 46.8 us
  local copies, waits for them, and re-layouts: 142 us -> 0.11 us
  other arithmetic: 28.5 us -> 0.01 us
  waiting for transfers between devices: 37.9 us -> 19.5 us
  Pallas kernels: 0 us -> 15.8 us
    psum x2 -> x0, blocking collectives: 215 us -> none  [precond_total(): return lax.psum(jnp.sum(first * second), ('lon', 'lat'))]
    ppermute x68 -> x16, starting transfers between devices: 219 us -> 39.7 us  [the longest x8 33.5 us: trade(): return (lax.ppermute(to_last, axis, [(j, i) for i, j in up]), from_last)]
    slice x89 -> x0, local copies, waits for them, and re-layouts: 124 us -> none  [the longest x10 22.2 us: mean_four(): blocks[:, 0::2, 1::2]]
    all_to_all x0 -> x1, blocking collectives: none -> 23.2 us  [shards(): lax.all_to_all(dots, 'lon', 0, 0, tiled=True)]
    ppermute x68 -> x16, waiting for transfers between devices: 37.9 us -> 15.1 us  [the longest x8 11.5 us: trade(): return (lax.ppermute(to_last, axis, [(j, i) for i, j in up]), from_last)]
    pallas_call x0 -> x12, Pallas kernels: none -> 15.8 us  [call(): pl.pallas_call(body, out_shape=[jax.ShapeDtypeStruct(o, F32) for o in out...]
    add x15 -> x0, other arithmetic: 7.54 us -> none  [the longest x2 1.85 us: vcycle(): mid_corr = mid_corr + prolong(coarse_corr)]
    reshape x4 -> x0, local copies, waits for them, and re-layouts: 7.16 us -> none  [prolong(): return jnp.repeat(jnp.repeat(source, 2, axis=1), 2, axis=2)]
  transfers between devices with their start and end apart: 68 -> 17, of which waited for: 42 -> 15; matrix products, arithmetic and copies ran while one was open for 14% -> 0% of each run, Pallas kernels for 0% -> 0%
where the time goes in v1:
time: 106 us
  starting transfers between devices  46.8 us (44%)
  blocking collectives  23.2 us (22%)
  waiting for transfers between devices  19.5 us (18%)
  Pallas kernels  15.8 us (15%)
    ppermute x8, starting transfers between devices, trade(): return (lax.ppermute(to_last, axis, [(j, i) for i, j in up]), from_last)  33.5 us
    all_to_all x1, blocking collectives, shards(): lax.all_to_all(dots, 'lon', 0, 0, tiled=True)  23.2 us
    pallas_call x12, Pallas kernels, call(): pl.pallas_call(body, out_shape=[jax.ShapeDtypeStruct(o, F32) for o in out...  15.8 us
    ppermute x8, waiting for transfers between devices, trade(): return (lax.ppermute(to_last, axis, [(j, i) for i, j in up]), from_last)  11.5 us
    all_to_all x1, starting transfers between devices, shards(): dots = lax.all_to_all(dots, 'lat', 0, 0, tiled=True)  7.1 us
    ppermute x8, starting transfers between devices, trade(): from_last = lax.ppermute(to_next, axis, up)  6.22 us
    all_to_all x1, waiting for transfers between devices, shards(): dots = lax.all_to_all(dots, 'lat', 0, 0, tiled=True)  4.37 us
    ppermute x8, waiting for transfers between devices, trade(): from_last = lax.ppermute(to_next, axis, up)  3.62 us
  transfers between devices with their start and end apart: 17, of which 15 were waited for; matrix products, arithmetic and copies ran while one was open for 0% of the time, Pallas kernels for 0%

profile of v1, /device:TPU:1, one launch (start us, length us, event | category | flops | bytes accessed | tf_op | source)
XLA Modules:
  0.0 106.2 jit_solution(8607526410497840349)
XLA Ops:
  0.7 2.3 %shard_map.76 = (f32[6,3,16,512]{3,2,1,0:T(8,128)}, f32[6,3,16,512]{3,2,1,0:T(8,128)}, f32[12,16,128]{2,1,0:T(8,128)}, f32[12,16,128]{2,1,0:T(8,128)}) custom-call(f32[16,8,512]{2,1,0:T(8,128)} %b_ref.3, f32[16,8,512]{2,1,0:T(8,128)} %x.1, f32[16,8,512]{2,1,0:T(8,128)} %c_ref.3), custom_call_target="tpu_custom_call" | custom-call | flops 1000000 | bytes 1000000 | tf_op jit(solution)/shard_map/pallas_call | solution.py:32
  3.0 6.9 %collective-permute-start = (f32[6,3,16,512]{3,2,1,0:T(8,128)}, f32[6,3,16,512]{3,2,1,0:T(8,128)S(1)}, u32[]{:S(2)}, u32[]{:S(2)}) collective-permute-start(f32[6,3,16,512]{3,2,1,0:T(8,128)} %get-tuple-element.51), channel_id=1, source_target_pairs={{1,0},{2,1},{3,2},{4,3},{5,4},{6,5},{7,6},{0,7},{9,8},{10,9},{11,1... | collective-permute-start | bytes 1769480 | tf_op jit(solution)/shard_map/ppermute | solution.py:432
  9.9 1.9 %collective-permute-start.3 = (f32[12,16,128]{2,1,0:T(8,128)}, f32[12,16,128]{2,1,0:T(8,128)S(1)}, u32[]{:S(2)}, u32[]{:S(2)}) collective-permute-start(f32[12,16,128]{2,1,0:T(8,128)} %get-tuple-element.53), channel_id=1, source_target_pairs={{0,8},{8,16},{16,24},{24,32},{32,40},{40,48},{48,56},{56,64},{64,7... | collective-permute-start | bytes 294920 | tf_op jit(solution)/shard_map/ppermute | solution.py:431
  11.8 9.1 %collective-permute-start.2 = (f32[12,16,128]{2,1,0:T(8,128)}, f32[12,16,128]{2,1,0:T(8,128)S(1)}, u32[]{:S(2)}, u32[]{:S(2)}) collective-permute-start(f32[12,16,128]{2,1,0:T(8,128)} %get-tuple-element.50._), channel_id=1, source_target_pairs={{8,0},{16,8},{24,16},{32,24},{40,32},{48,40},{56,48},{64,56},{72,6... | collective-permute-start | bytes 294920 | tf_op jit(solution)/shard_map/ppermute | solution.py:432
  21.3 1.7 %collective-permute-done.2.from_east = f32[12,16,128]{2,1,0:T(8,128)S(1)} collective-permute-done((f32[12,16,128]{2,1,0:T(8,128)}, f32[12,16,128]{2,1,0:T(8,128)S(1)}, u32[]{:S(2)}, u32[]{:S(2)}) %collective-permute-start.2) | collective-permute-done | bytes 98336 | tf_op jit(solution)/shard_map/ppermute | solution.py:432
  23.0 2.1 %collective-permute-start.4 = (f32[6,3,16,128]{3,2,1,0:T(8,128)S(1)}, f32[6,3,16,128]{3,2,1,0:T(8,128)S(1)}, u32[]{:S(2)}, u32[]{:S(2)}) collective-permute-start(f32[6,3,16,128]{3,2,1,0:T(8,128)S(1)} %get-tuple-element.55), channel_id=1, source_target_pairs={{1,0},{2,1},{3,2},{4,3},{5,4},{6,5},{7,6},{0,7},{9,8},{10,9},{11,1... | collective-permute-start | bytes 442376 | tf_op jit(solution)/shard_map/ppermute | solution.py:432
  25.4 2.6 %collective-permute-done.4.rim_north = f32[6,3,16,128]{3,2,1,0:T(8,128)S(1)} collective-permute-done((f32[6,3,16,128]{3,2,1,0:T(8,128)S(1)}, f32[6,3,16,128]{3,2,1,0:T(8,128)S(1)}, u32[]{:S(2)}, u32[]{:S(2)}) %collective-permute-start.4) | collective-permute-done | bytes 147488 | tf_op jit(solution)/shard_map/ppermute | solution.py:432
  28.2 5.7 %shard_map.79 = (f32[2,16,256]{2,1,0:T(8,128)S(1)}, f32[2,16,256]{2,1,0:T(8,128)S(1)}, f32[2,16,256]{2,1,0:T(8,128)S(1)}, f32[4,6,16,256]{3,2,1,0:T(8,128)S(1)},...) custom-call(f32[8,3,16,512]{3,2,1,0:T(8,128)S(1)} %shard_map.77.own,, ...), custom_call_target="tpu_custom_call" | custom-call | flops 1000000 | bytes 1000000 | tf_op jit(solution)/shard_map/pallas_call | solution.py:32
  33.9 4.9 %collective-permute-start.6 = (f32[2,16,256]{2,1,0:T(8,128)S(1)}, f32[2,16,256]{2,1,0:T(8,128)S(1)}, u32[]{:S(2)}, u32[]{:S(2)}) collective-permute-start(f32[2,16,256]{2,1,0:T(8,128)S(1)} %get-tuple-element.58), channel_id=1, source_target_pairs={{1,0},{2,1},{3,2},{4,3},{5,4},{6,5},{7,6},{0,7},{9,8},{10,9},{11,1... | collective-permute-start | bytes 98312 | tf_op jit(solution)/shard_map/ppermute | solution.py:432
  40.2 2.1 %collective-permute-start.9 = (f32[2,16,256]{2,1,0:T(8,128)S(1)}, f32[2,16,256]{2,1,0:T(8,128)S(1)}, u32[]{:S(2)}, u32[]{:S(2)}) collective-permute-start(f32[2,16,256]{2,1,0:T(8,128)S(1)} %get-tuple-element.61.e2), channel_id=1, source_target_pairs={{0,1},{1,2},{2,3},{3,4},{4,5},{5,6},{6,7},{7,0},{8,9},{9,10},{10,1... | collective-permute-start | bytes 98312 | tf_op jit(solution)/shard_map/ppermute | solution.py:431
  42.4 1.3 %collective-permute-start.8 = (f32[2,16,256]{2,1,0:T(8,128)S(1)}, f32[2,16,256]{2,1,0:T(8,128)S(1)}, u32[]{:S(2)}, u32[]{:S(2)}) collective-permute-start(f32[2,16,256]{2,1,0:T(8,128)S(1)} %get-tuple-element.61.e2), channel_id=1, source_target_pairs={{1,0},{2,1},{3,2},{4,3},{5,4},{6,5},{7,6},{0,7},{9,8},{10,9},{11,1... | collective-permute-start | bytes 98312 | tf_op jit(solution)/shard_map/ppermute | solution.py:432
  44.3 1.4 %collective-permute-done.8.e2_north = f32[2,16,256]{2,1,0:T(8,128)S(1)} collective-permute-done((f32[2,16,256]{2,1,0:T(8,128)S(1)}, f32[2,16,256]{2,1,0:T(8,128)S(1)}, u32[]{:S(2)}, u32[]{:S(2)}) %collective-permute-start.8) | collective-permute-done | bytes 32800 | tf_op jit(solution)/shard_map/ppermute | solution.py:432
  45.7 2.0 %shard_map.81 = (f32[8,16,512]{2,1,0:T(8,128)S(1)}, f32[8,16,640]{2,1,0:T(8,128)S(1)}, f32[5,16,640]{2,1,0:T(8,128)S(1)}, f32[5,16,640]{2,1,0:T(8,128)S(1)}, f32...) custom-call(f32[2,16,256]{2,1,0:T(8,128)S(1)} %get-tuple-element.61.e2, ...), custom_call_target="tpu_custom_call" | custom-call | flops 1000000 | bytes 1000000 | tf_op jit(solution)/shard_map/pallas_call | solution.py:32
  47.8 2.5 %collective-permute-start.10 = (f32[5,16,640]{2,1,0:T(8,128)S(1)}, f32[5,16,640]{2,1,0:T(8,128)S(1)}, u32[]{:S(2)}, u32[]{:S(2)}) collective-permute-start(f32[5,16,640]{2,1,0:T(8,128)S(1)} %get-tuple-element.77), channel_id=1, source_target_pairs={{1,0},{2,1},{3,2},{4,3},{5,4},{6,5},{7,6},{0,7},{9,8},{10,9},{11,1... | collective-permute-start | bytes 614408 | tf_op jit(solution)/shard_map/ppermute | solution.py:432
  50.2 2.7 %collective-permute-done.10.from_north = f32[5,16,640]{2,1,0:T(8,128)S(1)} collective-permute-done((f32[5,16,640]{2,1,0:T(8,128)S(1)}, f32[5,16,640]{2,1,0:T(8,128)S(1)}, u32[]{:S(2)}, u32[]{:S(2)}) %collective-permute-start.10) | collective-permute-done | bytes 204832 | tf_op jit(solution)/shard_map/ppermute | solution.py:432
  54.1 1.8 %shard_map.82 = (f32[2,16,256]{2,1,0:T(8,128)S(1)}, f32[2,16,256]{2,1,0:T(8,128)S(1)}, f32[2,16,256]{2,1,0:T(8,128)S(1)}, f32[20,16,640]{2,1,0:T(8,128)S(1)}, f3...) custom-call(f32[8,16,640]{2,1,0:T(8,128)S(1)} %get-tuple-element.76.w_own.w, ...), custom_call_target="tpu_custom_call" | custom-call | flops 1000000 | bytes 1000000 | tf_op jit(solution)/shard_map/pallas_call | solution.py:32
  55.9 5.5 %collective-permute-start.12 = (f32[2,16,256]{2,1,0:T(8,128)S(1)}, f32[2,16,256]{2,1,0:T(8,128)S(1)}, u32[]{:S(2)}, u32[]{:S(2)}) collective-permute-start(f32[2,16,256]{2,1,0:T(8,128)S(1)} %get-tuple-element.80), channel_id=1, source_target_pairs={{1,0},{2,1},{3,2},{4,3},{5,4},{6,5},{7,6},{0,7},{9,8},{10,9},{11,1... | collective-permute-start | bytes 98312 | tf_op jit(solution)/shard_map/ppermute | solution.py:432
  62.9 2.1 %collective-permute-start.15 = (f32[2,16,256]{2,1,0:T(8,128)S(1)}, f32[2,16,256]{2,1,0:T(8,128)S(1)}, u32[]{:S(2)}, u32[]{:S(2)}) collective-permute-start(f32[2,16,256]{2,1,0:T(8,128)S(1)} %get-tuple-element.84.e2), channel_id=1, source_target_pairs={{0,1},{1,2},{2,3},{3,4},{4,5},{5,6},{6,7},{7,0},{8,9},{9,10},{10,1... | collective-permute-start | bytes 98312 | tf_op jit(solution)/shard_map/ppermute | solution.py:431
  65.0 1.3 %collective-permute-start.14 = (f32[2,16,256]{2,1,0:T(8,128)S(1)}, f32[2,16,256]{2,1,0:T(8,128)S(1)}, u32[]{:S(2)}, u32[]{:S(2)}) collective-permute-start(f32[2,16,256]{2,1,0:T(8,128)S(1)} %get-tuple-element.84.e2), channel_id=1, source_target_pairs={{1,0},{2,1},{3,2},{4,3},{5,4},{6,5},{7,6},{0,7},{9,8},{10,9},{11,1... | collective-permute-start | bytes 98312 | tf_op jit(solution)/shard_map/ppermute | solution.py:432
  67.0 1.4 %collective-permute-done.14.e2_north = f32[2,16,256]{2,1,0:T(8,128)S(1)} collective-permute-done((f32[2,16,256]{2,1,0:T(8,128)S(1)}, f32[2,16,256]{2,1,0:T(8,128)S(1)}, u32[]{:S(2)}, u32[]{:S(2)}) %collective-permute-start.14) | collective-permute-done | bytes 32800 | tf_op jit(solution)/shard_map/ppermute | solution.py:432
  68.4 1.4 %shard_map.84 = (f32[16,8,512]{2,1,0:T(8,128)S(1)}, f32[64,128]{1,0:T(8,128)S(1)}) custom-call(f32[2,16,256]{2,1,0:T(8,128)S(1)} %get-tuple-element.84.e2, f32[2,16,256]{2,1,0:T(8,128)S(1)} %collective-permute-done.14.e2_north, f32[2,16,256]{2,1,0:T(8,128)S(1)} %collective-permute-done.15.e2_south, f32[6,16,256]{2,1,0:T(8,128)S(1)} %get-tuple-element.85.f2, ...), custom_call_target="tpu_custom_call" | custom-call | flops 1000000 | bytes 1000000 | tf_op jit(solution)/shard_map/pallas_call | solution.py:32
  69.8 23.2 %all_to_all.22 = f32[64,1,128]{2,1,0:T(1,128)S(1)} all-to-all(f32[64,1,128]{2,1,0:T(1,128)S(1)} %bitcast.15), channel_id=1, replica_groups=mesh['lon'=64,'lat'=8] {'lon'}, dimensions={0} | all-to-all | bytes 65536 | tf_op jit(solution)/shard_map/all_to_all | solution.py:492
  93.6 7.1 %all-to-all-start.1 = ((f32[8,1,128]{2,1,0:T(1,128)}), f32[8,1,128]{2,1,0:T(1,128)S(1)}, u32[]{:S(2)}, u32[]{:S(2)}) async-start(f32[8,1,128]{2,1,0:T(1,128)} %bitcast.6), calls=%async_computation.1 | async-start | bytes 8192 | tf_op jit(solution)/shard_map/all_to_all | solution.py:493
  100.8 4.4 %all-to-all-done.1 = f32[8,1,128]{2,1,0:T(1,128)S(1)} async-done(((f32[8,1,128]{2,1,0:T(1,128)}), f32[8,1,128]{2,1,0:T(1,128)S(1)}, u32[]{:S(2)}, u32[]{:S(2)}) %all-to-all-start.1) | async-done | bytes 4128 | tf_op jit(solution)/shard_map/all_to_all | solution.py:493
  (39 shorter events, 8.0 us)
Async XLA Ops:
  0.6 24.5 %copy-start.1 = (f32[16,8,512]{2,1,0:T(8,128)S(1)}, f32[16,8,512]{2,1,0:T(8,128)}, u32[]{:S(2)}) copy-start(f32[16,8,512]{2,1,0:T(8,128)} %x.1) | copy-start | bytes 786436
  0.6 24.5 %copy-start.2 = (f32[16,8,512]{2,1,0:T(8,128)S(1)}, f32[16,8,512]{2,1,0:T(8,128)}, u32[]{:S(2)}) copy-start(f32[16,8,512]{2,1,0:T(8,128)} %b_ref.3) | copy-start | bytes 786436
  0.7 24.5 %copy-start.3 = (f32[16,8,512]{2,1,0:T(8,128)S(1)}, f32[16,8,512]{2,1,0:T(8,128)}, u32[]{:S(2)}) copy-start(f32[16,8,512]{2,1,0:T(8,128)} %c_ref.3) | copy-start | bytes 786436
  3.0 18.0 %copy-start.5 = (f32[2,4,16]{2,1,0:T(4,128)S(1)}, f32[2,4,16]{2,1,0:T(4,128)}, u32[]{:S(2)}) copy-start(f32[2,4,16]{2,1,0:T(4,128)} %param.8) | copy-start | bytes 1540
  3.0 25.1 %collective-permute-start = (f32[6,3,16,512]{3,2,1,0:T(8,128)}, f32[6,3,16,512]{3,2,1,0:T(8,128)S(1)}, u32[]{:S(2)}, u32[]{:S(2)}) collective-permute-start(f32[6,3,16,512]{3,2,1,0:T(8,128)} %get-tuple-element.51), channel_id=1, source_target_pairs={{1,0},{2,1},{3,2},{4,3},{5,4},{6,5},{7,6},{0,7},{9,8},{10,9},{11,1... | collective-permute-start | bytes 1769480 | tf_op jit(solution)/shard_map/ppermute | solution.py:432
  9.9 18.2 %collective-permute-start.1 = (f32[6,3,16,512]{3,2,1,0:T(8,128)}, f32[6,3,16,512]{3,2,1,0:T(8,128)S(1)}, u32[]{:S(2)}, u32[]{:S(2)}) collective-permute-start(f32[6,3,16,512]{3,2,1,0:T(8,128)} %get-tuple-element.52), channel_id=1, source_target_pairs={{0,1},{1,2},{2,3},{3,4},{4,5},{5,6},{6,7},{7,0},{8,9},{9,10},{10,1... | collective-permute-start | bytes 1769480 | tf_op jit(solution)/shard_map/ppermute | solution.py:431
  9.9 11.3 %collective-permute-start.3 = (f32[12,16,128]{2,1,0:T(8,128)}, f32[12,16,128]{2,1,0:T(8,128)S(1)}, u32[]{:S(2)}, u32[]{:S(2)}) collective-permute-start(f32[12,16,128]{2,1,0:T(8,128)} %get-tuple-element.53), channel_id=1, source_target_pairs={{0,8},{8,16},{16,24},{24,32},{32,40},{40,48},{48,56},{56,64},{64,7... | collective-permute-start | bytes 294920 | tf_op jit(solution)/shard_map/ppermute | solution.py:431
  11.8 11.1 %collective-permute-start.2 = (f32[12,16,128]{2,1,0:T(8,128)}, f32[12,16,128]{2,1,0:T(8,128)S(1)}, u32[]{:S(2)}, u32[]{:S(2)}) collective-permute-start(f32[12,16,128]{2,1,0:T(8,128)} %get-tuple-element.50._), channel_id=1, source_target_pairs={{8,0},{16,8},{24,16},{32,24},{40,32},{48,40},{56,48},{64,56},{72,6... | collective-permute-start | bytes 294920 | tf_op jit(solution)/shard_map/ppermute | solution.py:432
  21.0 4.2 %copy-start.4 = (f32[12,16,128]{2,1,0:T(8,128)S(1)}, f32[12,16,128]{2,1,0:T(8,128)}, u32[]{:S(2)}) copy-start(f32[12,16,128]{2,1,0:T(8,128)} %get-tuple-element.50._) | copy-start | bytes 294916
  23.0 4.9 %collective-permute-start.4 = (f32[6,3,16,128]{3,2,1,0:T(8,128)S(1)}, f32[6,3,16,128]{3,2,1,0:T(8,128)S(1)}, u32[]{:S(2)}, u32[]{:S(2)}) collective-permute-start(f32[6,3,16,128]{3,2,1,0:T(8,128)S(1)} %get-tuple-element.55), channel_id=1, source_target_pairs={{1,0},{2,1},{3,2},{4,3},{5,4},{6,5},{7,6},{0,7},{9,8},{10,9},{11,1... | collective-permute-start | bytes 442376 | tf_op jit(solution)/shard_map/ppermute | solution.py:432
  25.2 3.0 %collective-permute-start.5 = (f32[6,3,16,128]{3,2,1,0:T(8,128)S(1)}, f32[6,3,16,128]{3,2,1,0:T(8,128)S(1)}, u32[]{:S(2)}, u32[]{:S(2)}) collective-permute-start(f32[6,3,16,128]{3,2,1,0:T(8,128)S(1)} %get-tuple-element.56), channel_id=1, source_target_pairs={{0,1},{1,2},{2,3},{3,4},{4,5},{5,6},{6,7},{7,0},{8,9},{9,10},{10,1... | collective-permute-start | bytes 442376 | tf_op jit(solution)/shard_map/ppermute | solution.py:431
  25.2 3.0 %copy-start = (bf16[640,256]{1,0:T(8,128)(2,1)S(1)}, bf16[640,256]{1,0:T(8,128)(2,1)}, u32[]{:S(2)}) copy-start(bf16[640,256]{1,0:T(8,128)(2,1)} %constant.2.clone.blocks) | copy-start | bytes 983044
  33.9 5.8 %collective-permute-start.6 = (f32[2,16,256]{2,1,0:T(8,128)S(1)}, f32[2,16,256]{2,1,0:T(8,128)S(1)}, u32[]{:S(2)}, u32[]{:S(2)}) collective-permute-start(f32[2,16,256]{2,1,0:T(8,128)S(1)} %get-tuple-element.58), channel_id=1, source_target_pairs={{1,0},{2,1},{3,2},{4,3},{5,4},{6,5},{7,6},{0,7},{9,8},{10,9},{11,1... | collective-permute-start | bytes 98312 | tf_op jit(solution)/shard_map/ppermute | solution.py:432
  38.8 1.2 %collective-permute-start.7 = (f32[2,16,256]{2,1,0:T(8,128)S(1)}, f32[2,16,256]{2,1,0:T(8,128)S(1)}, u32[]{:S(2)}, u32[]{:S(2)}) collective-permute-start(f32[2,16,256]{2,1,0:T(8,128)S(1)} %get-tuple-element.59), channel_id=1, source_target_pairs={{0,1},{1,2},{2,3},{3,4},{4,5},{5,6},{6,7},{7,0},{8,9},{9,10},{10,1... | collective-permute-start | bytes 98312 | tf_op jit(solution)/shard_map/ppermute | solution.py:431
  40.2 4.1 %collective-permute-start.9 = (f32[2,16,256]{2,1,0:T(8,128)S(1)}, f32[2,16,256]{2,1,0:T(8,128)S(1)}, u32[]{:S(2)}, u32[]{:S(2)}) collective-permute-start(f32[2,16,256]{2,1,0:T(8,128)S(1)} %get-tuple-element.61.e2), channel_id=1, source_target_pairs={{0,1},{1,2},{2,3},{3,4},{4,5},{5,6},{6,7},{7,0},{8,9},{9,10},{10,1... | collective-permute-start | bytes 98312 | tf_op jit(solution)/shard_map/ppermute | solution.py:431
  42.4 3.3 %collective-permute-start.8 = (f32[2,16,256]{2,1,0:T(8,128)S(1)}, f32[2,16,256]{2,1,0:T(8,128)S(1)}, u32[]{:S(2)}, u32[]{:S(2)}) collective-permute-start(f32[2,16,256]{2,1,0:T(8,128)S(1)} %get-tuple-element.61.e2), channel_id=1, source_target_pairs={{1,0},{2,1},{3,2},{4,3},{5,4},{6,5},{7,6},{0,7},{9,8},{10,9},{11,1... | collective-permute-start | bytes 98312 | tf_op jit(solution)/shard_map/ppermute | solution.py:432
  47.8 5.2 %collective-permute-start.10 = (f32[5,16,640]{2,1,0:T(8,128)S(1)}, f32[5,16,640]{2,1,0:T(8,128)S(1)}, u32[]{:S(2)}, u32[]{:S(2)}) collective-permute-start(f32[5,16,640]{2,1,0:T(8,128)S(1)} %get-tuple-element.77), channel_id=1, source_target_pairs={{1,0},{2,1},{3,2},{4,3},{5,4},{6,5},{7,6},{0,7},{9,8},{10,9},{11,1... | collective-permute-start | bytes 614408 | tf_op jit(solution)/shard_map/ppermute | solution.py:432
  50.2 3.9 %collective-permute-start.11 = (f32[5,16,640]{2,1,0:T(8,128)S(1)}, f32[5,16,640]{2,1,0:T(8,128)S(1)}, u32[]{:S(2)}, u32[]{:S(2)}) collective-permute-start(f32[5,16,640]{2,1,0:T(8,128)S(1)} %get-tuple-element.78), channel_id=1, source_target_pairs={{0,1},{1,2},{2,3},{3,4},{4,5},{5,6},{6,7},{7,0},{8,9},{9,10},{10,1... | collective-permute-start | bytes 614408 | tf_op jit(solution)/shard_map/ppermute | solution.py:431
  55.9 6.3 %collective-permute-start.12 = (f32[2,16,256]{2,1,0:T(8,128)S(1)}, f32[2,16,256]{2,1,0:T(8,128)S(1)}, u32[]{:S(2)}, u32[]{:S(2)}) collective-permute-start(f32[2,16,256]{2,1,0:T(8,128)S(1)} %get-tuple-element.80), channel_id=1, source_target_pairs={{1,0},{2,1},{3,2},{4,3},{5,4},{6,5},{7,6},{0,7},{9,8},{10,9},{11,1... | collective-permute-start | bytes 98312 | tf_op jit(solution)/shard_map/ppermute | solution.py:432
  61.4 1.2 %collective-permute-start.13 = (f32[2,16,256]{2,1,0:T(8,128)S(1)}, f32[2,16,256]{2,1,0:T(8,128)S(1)}, u32[]{:S(2)}, u32[]{:S(2)}) collective-permute-start(f32[2,16,256]{2,1,0:T(8,128)S(1)} %get-tuple-element.81), channel_id=1, source_target_pairs={{0,1},{1,2},{2,3},{3,4},{4,5},{5,6},{6,7},{7,0},{8,9},{9,10},{10,1... | collective-permute-start | bytes 98312 | tf_op jit(solution)/shard_map/ppermute | solution.py:431
  62.9 4.1 %collective-permute-start.15 = (f32[2,16,256]{2,1,0:T(8,128)S(1)}, f32[2,16,256]{2,1,0:T(8,128)S(1)}, u32[]{:S(2)}, u32[]{:S(2)}) collective-permute-start(f32[2,16,256]{2,1,0:T(8,128)S(1)} %get-tuple-element.84.e2), channel_id=1, source_target_pairs={{0,1},{1,2},{2,3},{3,4},{4,5},{5,6},{6,7},{7,0},{8,9},{9,10},{10,1... | collective-permute-start | bytes 98312 | tf_op jit(solution)/shard_map/ppermute | solution.py:431
  65.0 3.3 %collective-permute-start.14 = (f32[2,16,256]{2,1,0:T(8,128)S(1)}, f32[2,16,256]{2,1,0:T(8,128)S(1)}, u32[]{:S(2)}, u32[]{:S(2)}) collective-permute-start(f32[2,16,256]{2,1,0:T(8,128)S(1)} %get-tuple-element.84.e2), channel_id=1, source_target_pairs={{1,0},{2,1},{3,2},{4,3},{5,4},{6,5},{7,6},{0,7},{9,8},{10,9},{11,1... | collective-permute-start | bytes 98312 | tf_op jit(solution)/shard_map/ppermute | solution.py:432
  93.6 11.6 %all-to-all-start.1 = ((f32[8,1,128]{2,1,0:T(1,128)}), f32[8,1,128]{2,1,0:T(1,128)S(1)}, u32[]{:S(2)}, u32[]{:S(2)}) async-start(f32[8,1,128]{2,1,0:T(1,128)} %bitcast.6), calls=%async_computation.1 | async-start | bytes 8192 | tf_op jit(solution)/shard_map/all_to_all | solution.py:493

commit v2 on v1

--- a/solution.py
+++ b/solution.py
@@ -11,6 +11,7 @@
 ROWS = 8
 OWN = 512
 HALF = 64
+DEEP = 42
 LANES = OWN + 2 * HALF
 RIM = 6
 EXT = ROWS + 2 * RIM
@@ -40,7 +41,7 @@
     )(*ins)
 
 
-def loop(first, end, body, unroll=2):
+def loop(first, end, body, unroll=3):
     def step(i, carry):
         body(i)
         return carry
@@ -99,7 +100,7 @@
 
 
 def pack_kernel(b_ref, x_ref, c_ref, north_ref, south_ref, east_ref, west_ref, held, turned, arrived):
-    low_half = lax.broadcasted_iota(jnp.int32, (LEV, 128), 1) < HALF
+    lane = lax.broadcasted_iota(jnp.int32, (LEV, 128), 1)
     copies = [pltpu.make_async_copy(ref, held.at[j], arrived.at[j]) for j, ref in enumerate((b_ref, x_ref, c_ref))]
     for copy in copies:
         copy.start()
@@ -111,30 +112,21 @@
         turned[j, :, :, :128] = field[:, :, :128]
         turned[j, :, :, 128:] = field[:, :, OWN - 128:]
     for r in range(ROWS):
-        west_ref[r] = jnp.where(low_half, turned[0, r, :, :128], prev_lane(turned[1, r, :, :128], HALF))
-        east_ref[r] = jnp.where(low_half, prev_lane(turned[0, r, :, 128:], HALF), turned[1, r, :, 128:])
-    for r in range(ROWS // 2):
-        t = r + ROWS // 2
-        west_ref[ROWS + r] = jnp.where(low_half, turned[2, r, :, :128], prev_lane(turned[2, t, :, :128], HALF))
-        east_ref[ROWS + r] = jnp.where(low_half, prev_lane(turned[2, r, :, 128:], HALF), turned[2, t, :, 128:])
-
-
-def own_kernel(_, b_ref, x_ref, c_ref, own_ref):
-    for j, ref in enumerate((b_ref, x_ref, c_ref)):
-        own_ref[:, j] = jnp.swapaxes(ref[...], 0, 1)
+        b, x, c = [turned[j, r, :, :128] for j in range(3)]
+        west_ref[r] = jnp.where(lane < DEEP, b, jnp.where(lane < 2 * DEEP, prev_lane(x, DEEP), prev_lane(c, 2 * DEEP)))
+        b, x, c = [turned[j, r, :, 128:] for j in range(3)]
+        x, c = next_lane(x, DEEP), next_lane(c, 2 * DEEP)
+        east_ref[r] = jnp.where(lane >= 128 - DEEP, b, jnp.where(lane >= 128 - 2 * DEEP, x, c))
 
 
 def rim_kernel(from_east, from_west, rim_ref, north_ref, south_ref):
-    low_half = lax.broadcasted_iota(jnp.int32, (LEV, 128), 1) < HALF
-
+    lane = lax.broadcasted_iota(jnp.int32, (LEV, 128), 1)
     for r in range(ROWS):
         east, west = from_east[r], from_west[r]
-        rim_ref[r, 0] = jnp.where(low_half, east, prev_lane(west, HALF))
-        rim_ref[r, 1] = jnp.where(low_half, prev_lane(east, HALF), west)
-    for r in range(ROWS // 2):
-        east, west = from_east[ROWS + r], from_west[ROWS + r]
-        rim_ref[r, 2] = jnp.where(low_half, east, prev_lane(west, HALF))
-        rim_ref[r + ROWS // 2, 2] = jnp.where(low_half, prev_lane(east, HALF), west)
+        for j in range(3):
+            if j > 0:
+                east, west = next_lane(east, DEEP), prev_lane(west, DEEP)
+            rim_ref[r, j] = jnp.where(lane < DEEP, east, jnp.where(lane >= 128 - DEEP, west, 0.0))
     south_ref[...] = rim_ref[:RIM]
     north_ref[...] = rim_ref[ROWS - RIM:]
 
@@ -158,37 +150,83 @@
     to_south[0], to_south[1] = f2[0], e2[1]
 
 
+def weigh(sets, share, width):
+    level = lax.broadcasted_iota(jnp.int32, (LEV, width), 0)
+    top = level == LEV - 1
+    edge = top | (level == 0)
+
+    def blend(column):
+        sea = jnp.concatenate([sets[column]] * (width // 128), axis=1)
+        return sea + share * jnp.concatenate([sets[column + 4]] * (width // 128), axis=1)
+
+    lev_weight = blend(3)
+    react = blend(0) + jnp.where(edge, 0.5 * lev_weight, 0.0)
+    upper = jnp.where(top, 0.0, 0.5 * (lev_weight + next_level(lev_weight)))
+    return react, upper, blend(1), blend(2)
+
+
+def weigh_kernel(
+    b_ref, x_ref, c_ref, from_north, from_south, sets,
+    b, x, react, upper, lon_weight, lat_weight,
+    share,
+):
+    share[...] = jnp.swapaxes(c_ref[...], 0, 1)
+    b[RIM:RIM + ROWS] = jnp.swapaxes(b_ref[...], 0, 1)
+    x[RIM:RIM + ROWS] = jnp.swapaxes(x_ref[...], 0, 1)
+
+    def own(r):
+        i = r + RIM
+        react[i], upper[i], lon_weight[i], lat_weight[i] = weigh(sets, share[r], OWN)
+
+    def outer(i, rows, r):
+        b[i] = rows[r, 0]
+        x[i] = rows[r, 1]
+        react[i], upper[i], lon_weight[i], lat_weight[i] = weigh(sets, rows[r, 2], OWN)
+
+    loop(0, ROWS, own)
+    loop(0, RIM, lambda r: outer(r, from_south, r))
+    loop(0, RIM, lambda r: outer(r + RIM + ROWS, from_north, r))
+
+
+class Joined:
+    def __init__(self, main, rims):
+        self.main, self.rims = main, rims
+
+    def __getitem__(self, i):
+        return jnp.concatenate([self.main[i], self.rims[i]], axis=1)
+
+
 def first_down_kernel(
-    own, from_north, from_south, rim, rim_north, rim_south, sets, blocks,
-    f2_out, to_north, to_south, weights2, s, e0, f1, e1, east, north, upper, winv, diag, east1, north1, upper1, winv1,
-    x, lat_weight, react, react1, stage,
+    b_main, x_main, react_main, upper_main, lon_main, lat_main, rim, rim_north, rim_south, sets, blocks,
+    s, f2_out, to_north, to_south, weights2, e0, f1, e1, east, north, upper, winv, diag, east1, north1, upper1, winv1,
+    b_rims, x_rims, react_rims, upper_rims, lon_rims, lat_rims, react, react1, stage,
 ):
+    b, x, react_in = Joined(b_main, b_rims), Joined(x_main, x_rims), Joined(react_main, react_rims)
+    upper_in, lon_weight, lat_weight = Joined(upper_main, upper_rims), Joined(lon_main, lon_rims), Joined(lat_main, lat_rims)
     lane = lane_ids()
     even = lane % 2 == 0
-    level = lax.broadcasted_iota(jnp.int32, (LEV, LANES), 0)
-    top = level == LEV - 1
-    edge = top | (level == 0)
     lat = lax.axis_index("lat")
     south_end = lat == 0
     north_end = lat == lax.axis_size("lat") - 1
 
-    def wide(column):
-        return jnp.concatenate([sets[column]] * (LANES // 128), axis=1)
-
-    def load(i, main, rims, r):
-        share = jnp.concatenate([main[r, 2], rims[r, 2]], axis=1)
-        s[i] = jnp.concatenate([main[r, 0], rims[r, 0]], axis=1)
-        x[i] = jnp.concatenate([main[r, 1], rims[r, 1]], axis=1)
-        lon_weight = wide(1) + share * wide(5)
-        east[i] = 0.5 * (lon_weight + next_lane(lon_weight))
-        lat_weight[i] = wide(2) + share * wide(6)
-        lev_weight = wide(3) + share * wide(7)
-        upper[i] = jnp.where(top, 0.0, 0.5 * (lev_weight + next_level(lev_weight)))
-        react[i] = wide(0) + share * wide(4) + jnp.where(edge, 0.5 * lev_weight, 0.0)
-
-    loop(0, RIM, lambda r: load(r, from_south, rim_south, r))
-    loop(0, ROWS, lambda r: load(r + RIM, own, rim, r))
-    loop(0, RIM, lambda r: load(r + RIM + ROWS, from_north, rim_north, r))
+    def take(i, rows, r):
+        b_rims[i] = rows[r, 0]
+        x_rims[i] = rows[r, 1]
+        react_rims[i], upper_rims[i], lon_rims[i], lat_rims[i] = weigh(sets, rows[r, 2], 128)
+
+    for r in range(RIM):
+        take(r, rim_south, r)
+        take(r + RIM + ROWS, rim_north, r)
+    for r in range(ROWS):
+        take(r + RIM, rim, r)
+
+    def face_east(i):
+        here = lon_weight[i]
+        east[i] = 0.5 * (here + next_lane(here))
+        upper[i] = upper_in[i]
+
+    face_east(0)
+    face_east(EXT - 1)
 
     def face(i):
         closed = (south_end & (i == RIM - 1)) | (north_end & (i == RIM + ROWS - 1))
@@ -198,15 +236,16 @@
 
     def start(i):
         face(i)
+        face_east(i)
         at_end = (south_end & (i == RIM)) | (north_end & (i == RIM + ROWS - 1))
-        whole = react[i] + jnp.where(at_end, 0.5, 0.0) * lat_weight[i]
+        whole = react_in[i] + jnp.where(at_end, 0.5, 0.0) * lat_weight[i]
         react[i] = whole
         whole = whole + east[i] + prev_lane(east[i]) + north[i] + north[i - 1]
         whole = whole + upper[i] + prev_level(upper[i])
         diag[i] = whole
         inverse = DAMP / whole
         winv[i] = inverse
-        left = s[i] - (whole * x[i] - around(x, i, east, north, upper, 1))
+        left = b[i] - (whole * x[i] - around(x, i, east, north, upper, 1))
         s[i] = left
         e0[i] = inverse * left
 
@@ -273,12 +312,14 @@
     return sweep(2, f2, later, weights2), sweep(3, f2, later, weights2)
 
 
-def coarse_kernel(mine, from_north, from_south, weights2, f2, e2, now, later):
+def coarse_kernel(mine, from_north, from_south, weights2, f2, e2, e2_again, now, later):
     e2[0], e2[1] = two_sweeps(mine, from_north, from_south, weights2, f2, now, later)
-
-
-def coarse_dot_kernel(mine, from_north, from_south, weights2, sums, sum_wq, f2, e2, dots, now, later):
+    e2_again[...] = e2[...]
+
+
+def coarse_dot_kernel(mine, from_north, from_south, weights2, sums, sum_wq, f2, e2, e2_again, dots, now, later):
     e2[0], e2[1] = two_sweeps(mine, from_north, from_south, weights2, f2, now, later)
+    e2_again[...] = e2[...]
     total = jnp.zeros((LEV, OWN_COLS), F32)
     for r in range(2):
         k = 2 + r
@@ -360,8 +401,8 @@
     def down(m):
         return restrict(m, w, e0, f1, e1, winv1[m], east, north, upper, even)
 
-    loop(1, 3, down)
-    loop(7, MID - 1, down)
+    loop(1, 3, down, 2)
+    loop(7, MID - 1, down, 2)
 
     def down_own(m, total):
         left_0, left_1 = down(m)
@@ -423,10 +464,13 @@
 
 
 def shards(right_side, initial_guess, land_mask, coefficient_sets):
-    lat_size, lon_size = lax.axis_size("lat"), lax.axis_size("lon")
+    z_size, lat_size = lax.axis_size("z"), lax.axis_size("lat")
+    lines = (lax.axis_size("x") * lat_size, 128)
+    lon = ("x", "z")
+    sizes = {lon: lax.axis_size("x") * z_size, "lat": lat_size}
 
     def trade(to_next, to_last, axis):
-        size = lax.axis_size(axis)
+        size = sizes[axis]
         up = [(i, (i + 1) % size) for i in range(size)]
         from_last = lax.ppermute(to_next, axis, up)
         return lax.ppermute(to_last, axis, [(j, i) for i, j in up]), from_last
@@ -436,15 +480,14 @@
     blocks = blocks_matrix()
     to_north, to_south, to_east, to_west = call(
         pack_kernel,
-        [(RIM, 3, LEV, OWN)] * 2 + [(12, LEV, 128)] * 2,
+        [(RIM, 3, LEV, OWN)] * 2 + [(ROWS, LEV, 128)] * 2,
         fields,
         [(3, LEV, ROWS, OWN), (3, ROWS, LEV, 256)],
         specs=[HBM] * 3,
         copies=3,
     )
     lat_rows = trade(to_north, to_south, "lat")
-    lon_rims = trade(to_east, to_west, "lon")
-    (own,) = call(own_kernel, [(ROWS, 3, LEV, OWN)], [to_west] + fields, specs=[HBM])
+    lon_rims = trade(to_east, to_west, lon)
     rim, to_north, to_south = call(
         rim_kernel, [(ROWS, 3, LEV, 128), (RIM, 3, LEV, 128), (RIM, 3, LEV, 128)], lon_rims
     )
@@ -452,21 +495,26 @@
     sea, land = coefficient_sets[0], coefficient_sets[1]
     sets = jnp.broadcast_to(jnp.concatenate([sea, land - sea])[:, :, None], (8, LEV, 128))
 
-    (f2, to_north, to_south, weights2, s, e0, f1, e1, east, north, upper, winv, diag, east1, north1, upper1, winv1) = call(
+    main, side = (EXT, LEV, OWN), (EXT, LEV, 128)
+    weighed = call(weigh_kernel, [main] * 6, fields + [*lat_rows, sets], [(ROWS, LEV, OWN)])
+    (s, f2, to_north, to_south, weights2, e0, f1, e1, east, north, upper, winv, diag, east1, north1, upper1, winv1) = call(
         first_down_kernel,
-        [(2,) + line] * 3 + [(4, NEAR) + line, fine, fine, mid, mid, fine, fine, fine, fine, fine, mid, mid, mid, mid],
-        [own, *lat_rows, rim, *lat_rims, sets, blocks],
-        [fine, fine, fine, mid, (19,) + row],
+        [fine] + [(2,) + line] * 3 + [(4, NEAR) + line, fine, mid, mid, fine, fine, fine, fine, fine, mid, mid, mid, mid],
+        [*weighed, rim, *lat_rims, sets, blocks],
+        [side] * 6 + [fine, mid, (19,) + row],
     )
     grids = [winv, east, north, upper, winv1, east1, north1, upper1]
     near = (NEAR,) + line
-    f2_near, e2 = call(
-        coarse_kernel, [near, (2,) + line], [f2, *trade(to_north, to_south, "lat"), weights2], [near, near]
+    f2_near, e2, e2_again = call(
+        coarse_kernel,
+        [near, (2,) + line, (2,) + line],
+        [f2, *trade(to_north, to_south, "lat"), weights2],
+        [near, near],
     )
     p_own, w_own, to_north, to_south, s_own, sums = call(
         first_up_kernel,
         [(ROWS, LEV, OWN), (ROWS,) + row, (SEND,) + row, (SEND,) + row, (ROWS, LEV, OWN), (2, LEV, OWN)],
-        [e2, *trade(e2, e2, "lat"), f2_near, weights2, blocks, s, e0, f1, e1] + grids + [diag],
+        [e2, *trade(e2, e2_again, "lat"), f2_near, weights2, blocks, s, e0, f1, e1] + grids + [diag],
         [near, mid, fine, fine],
     )
     w_rows = trade(to_north, to_south, "lat")
@@ -477,25 +525,28 @@
         [w_own, *w_rows, weights2, blocks] + grids,
         [fine, (2,) + row],
     )
-    f2_near, e2, dots = call(
+    f2_near, e2, e2_again, dots = call(
         coarse_dot_kernel,
-        [near, (2,) + line, (lon_size, 128)],
+        [near, (2,) + line, (2,) + line, lines],
         [f2, *trade(to_north, to_south, "lat"), weights2, sums, sum_wq],
         [near, near],
     )
     q, dots = call(
         second_up_kernel,
-        [(LEV, ROWS, OWN), (lon_size, 128)],
-        [e2, *trade(e2, e2, "lat"), f2_near, weights2, blocks, w_own, e0, f1, e1] + grids + [dots],
+        [(LEV, ROWS, OWN), lines],
+        [e2, *trade(e2, e2_again, "lat"), f2_near, weights2, blocks, w_own, e0, f1, e1] + grids + [dots],
         [near, mid, fine, fine, fine],
     )
-    (dots,) = call(total_kernel, [(lat_size, 128)], [lax.all_to_all(dots, "lon", 0, 0, tiled=True)])
-    dots = lax.all_to_all(dots, "lat", 0, 0, tiled=True)
+    (dots,) = call(total_kernel, [(z_size, 128)], [lax.all_to_all(dots, ("x", "lat"), 0, 0, tiled=True)])
+    dots = lax.all_to_all(dots, "z", 0, 0, tiled=True)
     return tuple(call(finish_kernel, [(LEV, ROWS, OWN)] * 3, [dots, initial_guess, p, w, q, s]))
 
 
 def solution(mesh):
-    field = P(None, "lat", "lon")
+    lon, lat = mesh.shape["lon"], mesh.shape["lat"]
+    z = 16 if lon % 16 == 0 else lon
+    grid = jax.sharding.Mesh(mesh.devices.reshape(lon // z, z, lat), ("x", "z", "lat"))
+    field = P(None, "lat", ("x", "z"))
     return jax.shard_map(
-        shards, mesh=mesh, in_specs=(field, field, field, P()), out_specs=(field, field, field), check_vma=False
-    )
+        shards, mesh=grid, in_specs=(field, field, field, P()), out_specs=(field, field, field), check_vma=False
+    )

time: 106 us -> 99.2 us (0.936)
  blocking collectives: 23.2 us -> 13 us
  waiting for transfers between devices: 19.5 us -> 27.1 us
  starting transfers between devices: 46.8 us -> 42.6 us
    all_to_all x1, blocking collectives: 23.2 us -> 13 us  [shards(): lax.all_to_all(dots, ('x', 'lat'), 0, 0, tiled=True)]
    all_to_all x1, waiting for transfers between devices: 4.37 us -> 11 us  [shards(): dots = lax.all_to_all(dots, 'z', 0, 0, tiled=True)]
    ppermute x8, waiting for transfers between devices: 3.62 us -> 8.47 us  [trade(): from_last = lax.ppermute(to_next, axis, up)]
    ppermute x8, starting transfers between devices: 6.22 us -> 1.94 us  [trade(): from_last = lax.ppermute(to_next, axis, up)]
    ppermute x8, waiting for transfers between devices: 11.5 us -> 7.65 us  [trade(): return (lax.ppermute(to_last, axis, [(j, i) for i, j in up]), from_last)]
    ppermute x8, starting transfers between devices: 33.5 us -> 37.2 us  [trade(): return (lax.ppermute(to_last, axis, [(j, i) for i, j in up]), from_last)]
    all_to_all x1, starting transfers between devices: 7.1 us -> 3.47 us  [shards(): dots = lax.all_to_all(dots, 'z', 0, 0, tiled=True)]
  transfers between devices with their start and end apart: 17 -> 17, of which waited for: 15 -> 13; matrix products, arithmetic and copies ran while one was open for 0% -> 0% of each run, Pallas kernels for 0% -> 1%
where the time goes in v2:
time: 99.2 us; the launch traced here: 98.9 us
  starting transfers between devices  42.6 us (43%)
  waiting for transfers between devices  27.1 us (27%)
  Pallas kernels  15.3 us (15%)
  blocking collectives  13 us (13%)
    ppermute x8, starting transfers between devices, trade(): return (lax.ppermute(to_last, axis, [(j, i) for i, j in up]), from_last)  37.2 us
    pallas_call x12, Pallas kernels, call(): pl.pallas_call(body, out_shape=[jax.ShapeDtypeStruct(o, F32) for o in out...  15.3 us
    all_to_all x1, blocking collectives, shards(): lax.all_to_all(dots, ('x', 'lat'), 0, 0, tiled=True)  13 us
    all_to_all x1, waiting for transfers between devices, shards(): dots = lax.all_to_all(dots, 'z', 0, 0, tiled=True)  11 us
    ppermute x8, waiting for transfers between devices, trade(): from_last = lax.ppermute(to_next, axis, up)  8.47 us
    ppermute x8, waiting for transfers between devices, trade(): return (lax.ppermute(to_last, axis, [(j, i) for i, j in up]), from_last)  7.65 us
    all_to_all x1, starting transfers between devices, shards(): dots = lax.all_to_all(dots, 'z', 0, 0, tiled=True)  3.47 us
  transfers between devices with their start and end apart: 17, of which 13 were waited for; matrix products, arithmetic and copies ran while one was open for 0% of the time, Pallas kernels for 1%

profile of v2, /device:TPU:1, one launch (start us, length us, event | category | flops | bytes accessed | tf_op | source)
XLA Modules:
  0.0 98.9 jit_solution(7366295248232155509)
XLA Ops:
  0.7 2.3 %shard_map.76 = (f32[6,3,16,512]{3,2,1,0:T(8,128)}, f32[6,3,16,512]{3,2,1,0:T(8,128)}, f32[8,16,128]{2,1,0:T(8,128)}, f32[8,16,128]{2,1,0:T(8,128)}) custom-call(f32[16,8,512]{2,1,0:T(8,128)} %b_ref.3, f32[16,8,512]{2,1,0:T(8,128)} %x.1, f32[16,8,512]{2,1,0:T(8,128)} %c_ref.3), custom_call_target="tpu_custom_call" | custom-call | flops 1000000 | bytes 1000000 | tf_op jit(solution)/shard_map/pallas_call | solution.py:33
  3.0 6.9 %collective-permute-start = (f32[6,3,16,512]{3,2,1,0:T(8,128)}, f32[6,3,16,512]{3,2,1,0:T(8,128)S(1)}, u32[]{:S(2)}, u32[]{:S(2)}) collective-permute-start(f32[6,3,16,512]{3,2,1,0:T(8,128)} %get-tuple-element.58), channel_id=1, source_target_pairs={{1,0},{2,1},{3,2},{4,3},{5,4},{6,5},{7,6},{0,7},{9,8},{10,9},{11,1... | collective-permute-start | bytes 1769480 | tf_op jit(solution)/shard_map/ppermute | solution.py:476
  9.9 9.1 %collective-permute-start.2 = (f32[8,16,128]{2,1,0:T(8,128)}, f32[8,16,128]{2,1,0:T(8,128)S(1)}, u32[]{:S(2)}, u32[]{:S(2)}) collective-permute-start(f32[8,16,128]{2,1,0:T(8,128)} %get-tuple-element.66), channel_id=1, source_target_pairs={{8,0},{16,8},{24,16},{32,24},{40,32},{48,40},{56,48},{64,56},{72,6... | collective-permute-start | bytes 196616 | tf_op jit(solution)/shard_map/ppermute | solution.py:476
  19.1 1.9 %collective-permute-start.3 = (f32[8,16,128]{2,1,0:T(8,128)}, f32[8,16,128]{2,1,0:T(8,128)S(1)}, u32[]{:S(2)}, u32[]{:S(2)}) collective-permute-start(f32[8,16,128]{2,1,0:T(8,128)} %get-tuple-element.67), channel_id=1, source_target_pairs={{0,8},{8,16},{16,24},{24,32},{32,40},{40,48},{48,56},{56,64},{64,7... | collective-permute-start | bytes 196616 | tf_op jit(solution)/shard_map/ppermute | solution.py:475
  21.0 6.6 %collective-permute-done.3.from_west = f32[8,16,128]{2,1,0:T(8,128)S(1)} collective-permute-done((f32[8,16,128]{2,1,0:T(8,128)}, f32[8,16,128]{2,1,0:T(8,128)S(1)}, u32[]{:S(2)}, u32[]{:S(2)}) %collective-permute-start.3) | collective-permute-done | bytes 65568 | tf_op jit(solution)/shard_map/ppermute | solution.py:475
  27.8 2.7 %collective-permute-start.4 = (f32[6,3,16,128]{3,2,1,0:T(8,128)S(1)}, f32[6,3,16,128]{3,2,1,0:T(8,128)S(1)}, u32[]{:S(2)}, u32[]{:S(2)}) collective-permute-start(f32[6,3,16,128]{3,2,1,0:T(8,128)S(1)} %get-tuple-element.69), channel_id=1, source_target_pairs={{1,0},{2,1},{3,2},{4,3},{5,4},{6,5},{7,6},{0,7},{9,8},{10,9},{11,1... | collective-permute-start | bytes 442376 | tf_op jit(solution)/shard_map/ppermute | solution.py:476
  31.2 2.0 %collective-permute-done.4.rim_north = f32[6,3,16,128]{3,2,1,0:T(8,128)S(1)} collective-permute-done((f32[6,3,16,128]{3,2,1,0:T(8,128)S(1)}, f32[6,3,16,128]{3,2,1,0:T(8,128)S(1)}, u32[]{:S(2)}, u32[]{:S(2)}) %collective-permute-start.4) | collective-permute-done | bytes 147488 | tf_op jit(solution)/shard_map/ppermute | solution.py:476
  33.2 4.9 %shard_map.79 = (f32[20,16,640]{2,1,0:T(8,128)S(1)}, f32[2,16,256]{2,1,0:T(8,128)S(1)}, f32[2,16,256]{2,1,0:T(8,128)S(1)}, f32[2,16,256]{2,1,0:T(8,128)S(1)}, f3...) custom-call(f32[20,16,512]{2,1,0:T(8,128)S(1)} %get-tuple-element.60, ...), custom_call_target="tpu_custom_call" | custom-call | flops 1000000 | bytes 1000000 | tf_op jit(solution)/shard_map/pallas_call | solution.py:33
  38.1 4.6 %collective-permute-start.6 = (f32[2,16,256]{2,1,0:T(8,128)S(1)}, f32[2,16,256]{2,1,0:T(8,128)S(1)}, u32[]{:S(2)}, u32[]{:S(2)}) collective-permute-start(f32[2,16,256]{2,1,0:T(8,128)S(1)} %get-tuple-element.72), channel_id=1, source_target_pairs={{1,0},{2,1},{3,2},{4,3},{5,4},{6,5},{7,6},{0,7},{9,8},{10,9},{11,1... | collective-permute-start | bytes 98312 | tf_op jit(solution)/shard_map/ppermute | solution.py:476
  42.7 0.9 collective-permute-done.6.from_north
  44.1 3.4 %collective-permute-start.8 = (f32[2,16,256]{2,1,0:T(8,128)S(1)}, f32[2,16,256]{2,1,0:T(8,128)S(1)}, u32[]{:S(2)}, u32[]{:S(2)}) collective-permute-start(f32[2,16,256]{2,1,0:T(8,128)S(1)} %get-tuple-element.76), channel_id=1, source_target_pairs={{1,0},{2,1},{3,2},{4,3},{5,4},{6,5},{7,6},{0,7},{9,8},{10,9},{11,1... | collective-permute-start | bytes 98312 | tf_op jit(solution)/shard_map/ppermute | solution.py:476
  47.5 0.9 collective-permute-done.8.e2_north
  48.7 1.9 %shard_map.81 = (f32[8,16,512]{2,1,0:T(8,128)S(1)}, f32[8,16,640]{2,1,0:T(8,128)S(1)}, f32[5,16,640]{2,1,0:T(8,128)S(1)}, f32[5,16,640]{2,1,0:T(8,128)S(1)}, f32...) custom-call(f32[2,16,256]{2,1,0:T(8,128)S(1)} %get-tuple-element.75.e2, ...), custom_call_target="tpu_custom_call" | custom-call | flops 1000000 | bytes 1000000 | tf_op jit(solution)/shard_map/pallas_call | solution.py:33
  50.6 3.4 %collective-permute-start.10 = (f32[5,16,640]{2,1,0:T(8,128)S(1)}, f32[5,16,640]{2,1,0:T(8,128)S(1)}, u32[]{:S(2)}, u32[]{:S(2)}) collective-permute-start(f32[5,16,640]{2,1,0:T(8,128)S(1)} %get-tuple-element.92), channel_id=1, source_target_pairs={{1,0},{2,1},{3,2},{4,3},{5,4},{6,5},{7,6},{0,7},{9,8},{10,9},{11,1... | collective-permute-start | bytes 614408 | tf_op jit(solution)/shard_map/ppermute | solution.py:476
  54.0 2.2 %collective-permute-done.10.from_north = f32[5,16,640]{2,1,0:T(8,128)S(1)} collective-permute-done((f32[5,16,640]{2,1,0:T(8,128)S(1)}, f32[5,16,640]{2,1,0:T(8,128)S(1)}, u32[]{:S(2)}, u32[]{:S(2)}) %collective-permute-start.10) | collective-permute-done | bytes 204832 | tf_op jit(solution)/shard_map/ppermute | solution.py:476
  56.7 1.7 %shard_map.82 = (f32[2,16,256]{2,1,0:T(8,128)S(1)}, f32[2,16,256]{2,1,0:T(8,128)S(1)}, f32[2,16,256]{2,1,0:T(8,128)S(1)}, f32[20,16,640]{2,1,0:T(8,128)S(1)}, f3...) custom-call(f32[8,16,640]{2,1,0:T(8,128)S(1)} %get-tuple-element.91.w_own.w, ...), custom_call_target="tpu_custom_call" | custom-call | flops 1000000 | bytes 1000000 | tf_op jit(solution)/shard_map/pallas_call | solution.py:33
  58.4 3.7 %collective-permute-start.12 = (f32[2,16,256]{2,1,0:T(8,128)S(1)}, f32[2,16,256]{2,1,0:T(8,128)S(1)}, u32[]{:S(2)}, u32[]{:S(2)}) collective-permute-start(f32[2,16,256]{2,1,0:T(8,128)S(1)} %get-tuple-element.95), channel_id=1, source_target_pairs={{1,0},{2,1},{3,2},{4,3},{5,4},{6,5},{7,6},{0,7},{9,8},{10,9},{11,1... | collective-permute-start | bytes 98312 | tf_op jit(solution)/shard_map/ppermute | solution.py:476
  63.7 3.4 %collective-permute-start.14 = (f32[2,16,256]{2,1,0:T(8,128)S(1)}, f32[2,16,256]{2,1,0:T(8,128)S(1)}, u32[]{:S(2)}, u32[]{:S(2)}) collective-permute-start(f32[2,16,256]{2,1,0:T(8,128)S(1)} %get-tuple-element.100), channel_id=1, source_target_pairs={{1,0},{2,1},{3,2},{4,3},{5,4},{6,5},{7,6},{0,7},{9,8},{10,9},{11,1... | collective-permute-start | bytes 98312 | tf_op jit(solution)/shard_map/ppermute | solution.py:476
  67.1 0.9 collective-permute-done.14.e2_north
  68.3 1.4 %shard_map.84 = (f32[16,8,512]{2,1,0:T(8,128)S(1)}, f32[32,128]{1,0:T(8,128)S(1)}) custom-call(f32[2,16,256]{2,1,0:T(8,128)S(1)} %get-tuple-element.99.e2, f32[2,16,256]{2,1,0:T(8,128)S(1)} %collective-permute-done.14.e2_north, f32[2,16,256]{2,1,0:T(8,128)S(1)} %collective-permute-done.15.e2_south, f32[6,16,256]{2,1,0:T(8,128)S(1)} %get-tuple-element.101.f2, ...), custom_call_target="tpu_custom_call" | custom-call | flops 1000000 | bytes 1000000 | tf_op jit(solution)/shard_map/pallas_call | solution.py:33
  69.7 13.0 %all_to_all.22 = f32[32,1,128]{2,1,0:T(1,128)S(1)} all-to-all(f32[32,1,128]{2,1,0:T(1,128)S(1)} %bitcast.16), channel_id=1, replica_groups=mesh['x'=4,'z'=16,'lat'=8] {'x','lat'}, dimensions={0} | all-to-all | bytes 32768 | tf_op jit(solution)/shard_map/all_to_all | solution.py:540
  83.3 3.5 %all-to-all-start.1 = ((f32[16,1,128]{2,1,0:T(1,128)}), f32[16,1,128]{2,1,0:T(1,128)S(1)}, u32[]{:S(2)}, u32[]{:S(2)}) async-start(f32[16,1,128]{2,1,0:T(1,128)} %bitcast.6), calls=%async_computation.1 | async-start | bytes 16384 | tf_op jit(solution)/shard_map/all_to_all | solution.py:541
  87.0 11.0 %all-to-all-done.1 = f32[16,1,128]{2,1,0:T(1,128)S(1)} async-done(((f32[16,1,128]{2,1,0:T(1,128)}), f32[16,1,128]{2,1,0:T(1,128)S(1)}, u32[]{:S(2)}, u32[]{:S(2)}) %all-to-all-start.1) | async-done | bytes 8224 | tf_op jit(solution)/shard_map/all_to_all | solution.py:541
  97.9 1.0 %shard_map.87 = (f32[16,8,512]{2,1,0:T(8,128)}, f32[16,8,512]{2,1,0:T(8,128)}, f32[16,8,512]{2,1,0:T(8,128)}) custom-call(f32[16,128]{1,0:T(8,128)S(1)} %bitcast.15, f32[16,8,512]{2,1,0:T(8,128)S(1)} %copy-done.1, f32[16,8,512]{2,1,0:T(8,128)S(1)} %get-tuple-element.109.p, f32[16,8,512]{2,1,0:T(8,128)S(1)} %get-tuple-element.110.w, ...), custom_call_target="tpu_custom_call" | custom-call | flops 1000000 | bytes 1000000 | tf_op jit(solution)/shard_map/pallas_call | solution.py:33
  (37 shorter events, 4.8 us)
Async XLA Ops:
  0.6 29.9 %copy-start.1 = (f32[16,8,512]{2,1,0:T(8,128)S(1)}, f32[16,8,512]{2,1,0:T(8,128)}, u32[]{:S(2)}) copy-start(f32[16,8,512]{2,1,0:T(8,128)} %x.1) | copy-start | bytes 786436
  0.6 29.9 %copy-start.2 = (f32[16,8,512]{2,1,0:T(8,128)S(1)}, f32[16,8,512]{2,1,0:T(8,128)}, u32[]{:S(2)}) copy-start(f32[16,8,512]{2,1,0:T(8,128)} %b_ref.3) | copy-start | bytes 786436
  0.7 29.9 %copy-start.3 = (f32[16,8,512]{2,1,0:T(8,128)S(1)}, f32[16,8,512]{2,1,0:T(8,128)}, u32[]{:S(2)}) copy-start(f32[16,8,512]{2,1,0:T(8,128)} %c_ref.3) | copy-start | bytes 786436
  3.0 18.0 %copy-start.4 = (f32[2,4,16]{2,1,0:T(4,128)S(1)}, f32[2,4,16]{2,1,0:T(4,128)}, u32[]{:S(2)}) copy-start(f32[2,4,16]{2,1,0:T(4,128)} %param.8) | copy-start | bytes 1540
  3.0 27.5 %collective-permute-start = (f32[6,3,16,512]{3,2,1,0:T(8,128)}, f32[6,3,16,512]{3,2,1,0:T(8,128)S(1)}, u32[]{:S(2)}, u32[]{:S(2)}) collective-permute-start(f32[6,3,16,512]{3,2,1,0:T(8,128)} %get-tuple-element.58), channel_id=1, source_target_pairs={{1,0},{2,1},{3,2},{4,3},{5,4},{6,5},{7,6},{0,7},{9,8},{10,9},{11,1... | collective-permute-start | bytes 1769480 | tf_op jit(solution)/shard_map/ppermute | solution.py:476
  9.9 20.6 %collective-permute-start.1 = (f32[6,3,16,512]{3,2,1,0:T(8,128)}, f32[6,3,16,512]{3,2,1,0:T(8,128)S(1)}, u32[]{:S(2)}, u32[]{:S(2)}) collective-permute-start(f32[6,3,16,512]{3,2,1,0:T(8,128)} %get-tuple-element.59), channel_id=1, source_target_pairs={{0,1},{1,2},{2,3},{3,4},{4,5},{5,6},{6,7},{7,0},{8,9},{9,10},{10,1... | collective-permute-start | bytes 1769480 | tf_op jit(solution)/shard_map/ppermute | solution.py:475
  9.9 11.1 %collective-permute-start.2 = (f32[8,16,128]{2,1,0:T(8,128)}, f32[8,16,128]{2,1,0:T(8,128)S(1)}, u32[]{:S(2)}, u32[]{:S(2)}) collective-permute-start(f32[8,16,128]{2,1,0:T(8,128)} %get-tuple-element.66), channel_id=1, source_target_pairs={{8,0},{16,8},{24,16},{32,24},{40,32},{48,40},{56,48},{64,56},{72,6... | collective-permute-start | bytes 196616 | tf_op jit(solution)/shard_map/ppermute | solution.py:476
  19.1 8.5 %collective-permute-start.3 = (f32[8,16,128]{2,1,0:T(8,128)}, f32[8,16,128]{2,1,0:T(8,128)S(1)}, u32[]{:S(2)}, u32[]{:S(2)}) collective-permute-start(f32[8,16,128]{2,1,0:T(8,128)} %get-tuple-element.67), channel_id=1, source_target_pairs={{0,8},{8,16},{16,24},{24,32},{32,40},{40,48},{48,56},{56,64},{64,7... | collective-permute-start | bytes 196616 | tf_op jit(solution)/shard_map/ppermute | solution.py:475
  27.8 5.4 %collective-permute-start.4 = (f32[6,3,16,128]{3,2,1,0:T(8,128)S(1)}, f32[6,3,16,128]{3,2,1,0:T(8,128)S(1)}, u32[]{:S(2)}, u32[]{:S(2)}) collective-permute-start(f32[6,3,16,128]{3,2,1,0:T(8,128)S(1)} %get-tuple-element.69), channel_id=1, source_target_pairs={{1,0},{2,1},{3,2},{4,3},{5,4},{6,5},{7,6},{0,7},{9,8},{10,9},{11,1... | collective-permute-start | bytes 442376 | tf_op jit(solution)/shard_map/ppermute | solution.py:476
  30.5 2.7 %collective-permute-start.5 = (f32[6,3,16,128]{3,2,1,0:T(8,128)S(1)}, f32[6,3,16,128]{3,2,1,0:T(8,128)S(1)}, u32[]{:S(2)}, u32[]{:S(2)}) collective-permute-start(f32[6,3,16,128]{3,2,1,0:T(8,128)S(1)} %get-tuple-element.70), channel_id=1, source_target_pairs={{0,1},{1,2},{2,3},{3,4},{4,5},{5,6},{6,7},{7,0},{8,9},{9,10},{10,1... | collective-permute-start | bytes 442376 | tf_op jit(solution)/shard_map/ppermute | solution.py:475
  30.6 2.6 %copy-start = (bf16[640,256]{1,0:T(8,128)(2,1)S(1)}, bf16[640,256]{1,0:T(8,128)(2,1)}, u32[]{:S(2)}) copy-start(bf16[640,256]{1,0:T(8,128)(2,1)} %constant.2.clone.blocks) | copy-start | bytes 983044
  38.1 5.4 %collective-permute-start.6 = (f32[2,16,256]{2,1,0:T(8,128)S(1)}, f32[2,16,256]{2,1,0:T(8,128)S(1)}, u32[]{:S(2)}, u32[]{:S(2)}) collective-permute-start(f32[2,16,256]{2,1,0:T(8,128)S(1)} %get-tuple-element.72), channel_id=1, source_target_pairs={{1,0},{2,1},{3,2},{4,3},{5,4},{6,5},{7,6},{0,7},{9,8},{10,9},{11,1... | collective-permute-start | bytes 98312 | tf_op jit(solution)/shard_map/ppermute | solution.py:476
  42.7 1.2 %collective-permute-start.7 = (f32[2,16,256]{2,1,0:T(8,128)S(1)}, f32[2,16,256]{2,1,0:T(8,128)S(1)}, u32[]{:S(2)}, u32[]{:S(2)}) collective-permute-start(f32[2,16,256]{2,1,0:T(8,128)S(1)} %get-tuple-element.73), channel_id=1, source_target_pairs={{0,1},{1,2},{2,3},{3,4},{4,5},{5,6},{6,7},{7,0},{8,9},{9,10},{10,1... | collective-permute-start | bytes 98312 | tf_op jit(solution)/shard_map/ppermute | solution.py:475
  44.1 4.2 %collective-permute-start.8 = (f32[2,16,256]{2,1,0:T(8,128)S(1)}, f32[2,16,256]{2,1,0:T(8,128)S(1)}, u32[]{:S(2)}, u32[]{:S(2)}) collective-permute-start(f32[2,16,256]{2,1,0:T(8,128)S(1)} %get-tuple-element.76), channel_id=1, source_target_pairs={{1,0},{2,1},{3,2},{4,3},{5,4},{6,5},{7,6},{0,7},{9,8},{10,9},{11,1... | collective-permute-start | bytes 98312 | tf_op jit(solution)/shard_map/ppermute | solution.py:476
  47.5 1.2 %collective-permute-start.9 = (f32[2,16,256]{2,1,0:T(8,128)S(1)}, f32[2,16,256]{2,1,0:T(8,128)S(1)}, u32[]{:S(2)}, u32[]{:S(2)}) collective-permute-start(f32[2,16,256]{2,1,0:T(8,128)S(1)} %get-tuple-element.75.e2), channel_id=1, source_target_pairs={{0,1},{1,2},{2,3},{3,4},{4,5},{5,6},{6,7},{7,0},{8,9},{9,10},{10,1... | collective-permute-start | bytes 98312 | tf_op jit(solution)/shard_map/ppermute | solution.py:475
  50.6 5.6 %collective-permute-start.10 = (f32[5,16,640]{2,1,0:T(8,128)S(1)}, f32[5,16,640]{2,1,0:T(8,128)S(1)}, u32[]{:S(2)}, u32[]{:S(2)}) collective-permute-start(f32[5,16,640]{2,1,0:T(8,128)S(1)} %get-tuple-element.92), channel_id=1, source_target_pairs={{1,0},{2,1},{3,2},{4,3},{5,4},{6,5},{7,6},{0,7},{9,8},{10,9},{11,1... | collective-permute-start | bytes 614408 | tf_op jit(solution)/shard_map/ppermute | solution.py:476
  54.0 2.7 %collective-permute-start.11 = (f32[5,16,640]{2,1,0:T(8,128)S(1)}, f32[5,16,640]{2,1,0:T(8,128)S(1)}, u32[]{:S(2)}, u32[]{:S(2)}) collective-permute-start(f32[5,16,640]{2,1,0:T(8,128)S(1)} %get-tuple-element.93), channel_id=1, source_target_pairs={{0,1},{1,2},{2,3},{3,4},{4,5},{5,6},{6,7},{7,0},{8,9},{9,10},{10,1... | collective-permute-start | bytes 614408 | tf_op jit(solution)/shard_map/ppermute | solution.py:475
  58.4 4.6 %collective-permute-start.12 = (f32[2,16,256]{2,1,0:T(8,128)S(1)}, f32[2,16,256]{2,1,0:T(8,128)S(1)}, u32[]{:S(2)}, u32[]{:S(2)}) collective-permute-start(f32[2,16,256]{2,1,0:T(8,128)S(1)} %get-tuple-element.95), channel_id=1, source_target_pairs={{1,0},{2,1},{3,2},{4,3},{5,4},{6,5},{7,6},{0,7},{9,8},{10,9},{11,1... | collective-permute-start | bytes 98312 | tf_op jit(solution)/shard_map/ppermute | solution.py:476
  62.2 1.2 %collective-permute-start.13 = (f32[2,16,256]{2,1,0:T(8,128)S(1)}, f32[2,16,256]{2,1,0:T(8,128)S(1)}, u32[]{:S(2)}, u32[]{:S(2)}) collective-permute-start(f32[2,16,256]{2,1,0:T(8,128)S(1)} %get-tuple-element.96), channel_id=1, source_target_pairs={{0,1},{1,2},{2,3},{3,4},{4,5},{5,6},{6,7},{7,0},{8,9},{9,10},{10,1... | collective-permute-start | bytes 98312 | tf_op jit(solution)/shard_map/ppermute | solution.py:475
  63.7 4.2 %collective-permute-start.14 = (f32[2,16,256]{2,1,0:T(8,128)S(1)}, f32[2,16,256]{2,1,0:T(8,128)S(1)}, u32[]{:S(2)}, u32[]{:S(2)}) collective-permute-start(f32[2,16,256]{2,1,0:T(8,128)S(1)} %get-tuple-element.100), channel_id=1, source_target_pairs={{1,0},{2,1},{3,2},{4,3},{5,4},{6,5},{7,6},{0,7},{9,8},{10,9},{11,1... | collective-permute-start | bytes 98312 | tf_op jit(solution)/shard_map/ppermute | solution.py:476
  67.1 1.2 %collective-permute-start.15 = (f32[2,16,256]{2,1,0:T(8,128)S(1)}, f32[2,16,256]{2,1,0:T(8,128)S(1)}, u32[]{:S(2)}, u32[]{:S(2)}) collective-permute-start(f32[2,16,256]{2,1,0:T(8,128)S(1)} %get-tuple-element.99.e2), channel_id=1, source_target_pairs={{0,1},{1,2},{2,3},{3,4},{4,5},{5,6},{6,7},{7,0},{8,9},{9,10},{10,1... | collective-permute-start | bytes 98312 | tf_op jit(solution)/shard_map/ppermute | solution.py:475
  83.3 14.6 %all-to-all-start.1 = ((f32[16,1,128]{2,1,0:T(1,128)}), f32[16,1,128]{2,1,0:T(1,128)S(1)}, u32[]{:S(2)}, u32[]{:S(2)}) async-start(f32[16,1,128]{2,1,0:T(1,128)} %bitcast.6), calls=%async_computation.1 | async-start | bytes 16384 | tf_op jit(solution)/shard_map/all_to_all | solution.py:541

commit v3 on v2

--- a/solution.py
+++ b/solution.py
@@ -13,10 +13,10 @@
 HALF = 64
 DEEP = 42
 LANES = OWN + 2 * HALF
-RIM = 6
+RIM = 4
 EXT = ROWS + 2 * RIM
 MID = EXT // 2
-SEND = 5
+SEND = 3
 NEAR = 6
 COLS = 256
 OWN_COLS = OWN // 4
@@ -41,12 +41,14 @@
     )(*ins)
 
 
-def loop(first, end, body, unroll=3):
+def loop(first, end, body):
+    rows = end - first
+
     def step(i, carry):
         body(i)
         return carry
 
-    lax.fori_loop(first, end, step, 0, unroll=unroll)
+    lax.fori_loop(first, end, step, 0, unroll=rows if rows <= 8 else rows // 2)
 
 
 def lane_ids():
@@ -145,9 +147,15 @@
     return KEEP * f1[m] + around(e1, m, east1, north1, upper1, 2)
 
 
-def hand_out(f2, e2, to_north, to_south):
+def hand_out(f2, e2, weights2, to_north, to_south):
     to_north[0], to_north[1] = f2[1], e2[0]
     to_south[0], to_south[1] = f2[0], e2[1]
+    if to_north.shape[0] > 2:
+        for j, kind in enumerate((0, 1, 3)):
+            to_north[2 + j] = weights2[kind, 3]
+            to_south[2 + j] = weights2[kind, 2]
+        to_north[5] = weights2[2, 2]
+        to_south[5] = weights2[2, 2]
 
 
 def weigh(sets, share, width):
@@ -268,32 +276,30 @@
     loop(1, MID - 1, middle)
 
     last_of_four = lane % 4 == 3
-    for c in range(4):
-        m = 1 + 2 * c
+    for c in range(2):
+        m = 2 + 2 * c
         stage[c] = 0.125 * (react1[m] + react1[m + 1])
-        stage[4 + c] = 0.125 * (upper1[m] + upper1[m + 1])
-        stage[8 + c] = jnp.where(last_of_four, 0.25 * (east1[m] + east1[m + 1]), 0.0)
-    for c in range(5):
-        stage[12 + c] = 0.125 * north1[2 * c]
-    for c in range(2):
-        m = 3 + 2 * c
+        stage[2 + c] = 0.125 * (upper1[m] + upper1[m + 1])
+        stage[4 + c] = jnp.where(last_of_four, 0.25 * (east1[m] + east1[m + 1]), 0.0)
         left = middle_left(m, f1, e1, east1, north1, upper1)
-        stage[17 + c] = 0.125 * (left + middle_left(m + 1, f1, e1, east1, north1, upper1))
-    packed = times_blocks(stage[...].reshape(19 * LEV, LANES), blocks, 0).reshape(19, LEV, COLS)
+        stage[6 + c] = 0.125 * (left + middle_left(m + 1, f1, e1, east1, north1, upper1))
+    for c in range(3):
+        stage[8 + c] = 0.125 * north1[1 + 2 * c]
+    packed = times_blocks(stage[...].reshape(11 * LEV, LANES), blocks, 0).reshape(11, LEV, COLS)
     col = lax.broadcasted_iota(jnp.int32, (LEV, COLS), 1)
     empty = (col >= OWN_COLS + HALF_COLS) & (col < COLS - HALF_COLS)
-    for c in range(4):
-        upper2, east2, north2 = packed[4 + c], packed[8 + c], packed[13 + c]
-        whole = packed[c] + east2 + prev_lane(east2) + north2 + packed[12 + c]
+    for c in range(2):
+        upper2, east2, north2 = packed[2 + c], packed[4 + c], packed[9 + c]
+        whole = packed[c] + east2 + prev_lane(east2) + north2 + packed[8 + c]
         whole = whole + upper2 + prev_level(upper2)
-        weights2[0, 1 + c] = DAMP / jnp.where(empty, 1.0, whole)
-        weights2[1, 1 + c] = east2
-        weights2[2, 1 + c] = north2
-        weights2[3, 1 + c] = upper2
-    weights2[2, 0] = packed[12]
-    f2 = (packed[17], packed[18])
+        weights2[0, 2 + c] = DAMP / jnp.where(empty, 1.0, whole)
+        weights2[1, 2 + c] = east2
+        weights2[2, 2 + c] = north2
+        weights2[3, 2 + c] = upper2
+    weights2[2, 1] = packed[8]
+    f2 = (packed[6], packed[7])
     f2_out[0], f2_out[1] = f2
-    hand_out(f2, (weights2[0, 2] * f2[0], weights2[0, 3] * f2[1]), to_north, to_south)
+    hand_out(f2, (weights2[0, 2] * f2[0], weights2[0, 3] * f2[1]), weights2, to_north, to_south)
 
 
 def sweep(k, f2, now, weights2):
@@ -312,14 +318,30 @@
     return sweep(2, f2, later, weights2), sweep(3, f2, later, weights2)
 
 
-def coarse_kernel(mine, from_north, from_south, weights2, f2, e2, e2_again, now, later):
+def hand_on(e2, e1, to_north, to_south):
+    for to, m in ((to_north, 4), (to_south, 3)):
+        to[:, :COLS] = e2[0]
+        to[:, COLS:2 * COLS] = e2[1]
+        to[:, 2 * COLS:] = e1[m]
+
+
+def coarse_kernel(mine, from_north, from_south, weights2, e1, f2, e2, to_north, to_south, whole2, now, later):
+    for kind in range(4):
+        for k in (2, 3):
+            whole2[kind, k] = weights2[kind, k]
+    for j, kind in enumerate((0, 1, 3)):
+        whole2[kind, 1] = from_south[2 + j]
+        whole2[kind, 4] = from_north[2 + j]
+    whole2[2, 0], whole2[2, 1], whole2[2, 4] = from_south[5], weights2[2, 1], from_north[5]
+    e2[0], e2[1] = two_sweeps(mine, from_north, from_south, whole2, f2, now, later)
+    hand_on(e2, e1, to_north, to_south)
+
+
+def coarse_dot_kernel(
+    mine, from_north, from_south, weights2, e1, sums, sum_wq, f2, e2, to_north, to_south, dots, now, later
+):
     e2[0], e2[1] = two_sweeps(mine, from_north, from_south, weights2, f2, now, later)
-    e2_again[...] = e2[...]
-
-
-def coarse_dot_kernel(mine, from_north, from_south, weights2, sums, sum_wq, f2, e2, e2_again, dots, now, later):
-    e2[0], e2[1] = two_sweeps(mine, from_north, from_south, weights2, f2, now, later)
-    e2_again[...] = e2[...]
+    hand_on(e2, e1, to_north, to_south)
     total = jnp.zeros((LEV, OWN_COLS), F32)
     for r in range(2):
         k = 2 + r
@@ -333,22 +355,25 @@
 
 
 def ascend(
-    e2, e2_north, e2_south, f2, weights2, blocks, first, end, f, e0, f1, e1, winv, east, north, upper,
+    e2, from_north, from_south, f2, weights2, blocks, first, end, f, e0, f1, e1, winv, east, north, upper,
     winv1, east1, north1, upper1, now, sum1, sum0, result,
 ):
     for r in range(2):
-        now[r], now[2 + r], now[4 + r] = e2_south[r], e2[r], e2_north[r]
+        cols = slice(r * COLS, (r + 1) * COLS)
+        now[r], now[2 + r], now[4 + r] = from_south[:, cols], e2[r], from_north[:, cols]
     rows = jnp.concatenate([sweep(k, f2, now, weights2) for k in range(1, 5)], axis=0)
     wide = times_blocks(rows, blocks, 1).reshape(4, LEV, LANES)
     for m in range(1, MID - 1):
-        sum1[m] = e1[m] + wide[(m - 1) // 2]
+        sum1[m] = e1[m] + wide[m // 2]
+    sum1[0] = from_south[:, 2 * COLS:] + wide[0]
+    sum1[MID - 1] = from_north[:, 2 * COLS:] + wide[3]
 
     def middle(m):
         better = KEEP * sum1[m] + winv1[m] * (f1[m] + around(sum1, m, east1, north1, upper1, 2))
         sum0[2 * m] = e0[2 * m] + better
         sum0[2 * m + 1] = e0[2 * m + 1] + better
 
-    loop(2, MID - 2, middle)
+    loop(1, MID - 1, middle)
 
     def fine(i):
         result[i] = KEEP * sum0[i] + winv[i] * (f[i] + around(sum0, i, east, north, upper, 1))
@@ -357,13 +382,13 @@
 
 
 def first_up_kernel(
-    e2, e2_north, e2_south, f2, weights2, blocks,
+    e2, from_north, from_south, f2, weights2, blocks,
     s, e0, f1, e1, winv, east, north, upper, winv1, east1, north1, upper1, diag,
     p_own, w_own, w_north, w_south, s_own, sums,
     now, sum1, sum0, p,
 ):
     ascend(
-        e2, e2_north, e2_south, f2, weights2, blocks, RIM - 1, RIM + ROWS + 1, s, e0, f1, e1, winv, east, north, upper,
+        e2, from_north, from_south, f2, weights2, blocks, RIM - 1, RIM + ROWS + 1, s, e0, f1, e1, winv, east, north, upper,
         winv1, east1, north1, upper1, now, sum1, sum0, p,
     )
 
@@ -377,7 +402,7 @@
         return totals[0] + s_row * p_row, totals[1] + p_row * w_row[:, :OWN]
 
     zero = jnp.zeros((LEV, OWN), F32)
-    sums[0], sums[1] = lax.fori_loop(0, ROWS, image, (zero, zero), unroll=2)
+    sums[0], sums[1] = lax.fori_loop(0, ROWS, image, (zero, zero), unroll=4)
     w_south[...] = w_own[:SEND]
     w_north[...] = w_own[ROWS - SEND:]
 
@@ -401,8 +426,8 @@
     def down(m):
         return restrict(m, w, e0, f1, e1, winv1[m], east, north, upper, even)
 
-    loop(1, 3, down, 2)
-    loop(7, MID - 1, down, 2)
+    down(1)
+    down(MID - 2)
 
     def down_own(m, total):
         left_0, left_1 = down(m)
@@ -410,10 +435,10 @@
         term = e0[i] * (w[i] + left_0) + e0[i + 1] * (w[i + 1] + left_1)
         return total + term[:, :OWN]
 
-    total = lax.fori_loop(3, 7, down_own, jnp.zeros((LEV, OWN), F32), unroll=2)
+    total = lax.fori_loop(2, 6, down_own, jnp.zeros((LEV, OWN), F32), unroll=4)
     for c in range(2):
         pair = 0.0
-        for m in (3 + 2 * c, 4 + 2 * c):
+        for m in (2 + 2 * c, 3 + 2 * c):
             left = middle_left(m, f1, e1, east1, north1, upper1)
             total = total + 2.0 * (e1[m] * (f1[m] + left))[:, :OWN]
             pair = pair + left
@@ -422,11 +447,11 @@
     packed = times_blocks(stage[...].reshape(2 * LEV, LANES), blocks, 0).reshape(2, LEV, COLS)
     f2 = (packed[0], packed[1])
     f2_out[0], f2_out[1] = f2
-    hand_out(f2, (weights2[0, 2] * f2[0], weights2[0, 3] * f2[1]), to_north, to_south)
+    hand_out(f2, (weights2[0, 2] * f2[0], weights2[0, 3] * f2[1]), weights2, to_north, to_south)
 
 
 def second_up_kernel(
-    e2, e2_north, e2_south, f2, weights2, blocks,
+    e2, from_north, from_south, f2, weights2, blocks,
     w_own, e0, f1, e1, winv, east, north, upper, winv1, east1, north1, upper1, dots,
     q_out, dots_out,
     now, sum1, sum0, w, result,
@@ -434,7 +459,7 @@
     for r in range(ROWS):
         w[RIM + r] = w_own[r]
     ascend(
-        e2, e2_north, e2_south, f2, weights2, blocks, RIM, RIM + ROWS, w, e0, f1, e1, winv, east, north, upper,
+        e2, from_north, from_south, f2, weights2, blocks, RIM, RIM + ROWS, w, e0, f1, e1, winv, east, north, upper,
         winv1, east1, north1, upper1, now, sum1, sum0, result,
     )
     dots_out[...] = dots[...]
@@ -499,22 +524,23 @@
     weighed = call(weigh_kernel, [main] * 6, fields + [*lat_rows, sets], [(ROWS, LEV, OWN)])
     (s, f2, to_north, to_south, weights2, e0, f1, e1, east, north, upper, winv, diag, east1, north1, upper1, winv1) = call(
         first_down_kernel,
-        [fine] + [(2,) + line] * 3 + [(4, NEAR) + line, fine, mid, mid, fine, fine, fine, fine, fine, mid, mid, mid, mid],
+        [fine, (2,) + line, (6,) + line, (6,) + line, (4, NEAR) + line, fine, mid, mid, fine, fine, fine, fine, fine, mid, mid, mid, mid],
         [*weighed, rim, *lat_rims, sets, blocks],
-        [side] * 6 + [fine, mid, (19,) + row],
+        [side] * 6 + [fine, mid, (11,) + row],
     )
     grids = [winv, east, north, upper, winv1, east1, north1, upper1]
     near = (NEAR,) + line
-    f2_near, e2, e2_again = call(
+    edge = (LEV, 2 * COLS + LANES)
+    f2_near, e2, edge_north, edge_south, weights2 = call(
         coarse_kernel,
-        [near, (2,) + line, (2,) + line],
-        [f2, *trade(to_north, to_south, "lat"), weights2],
+        [near, (2,) + line, edge, edge, (4, NEAR) + line],
+        [f2, *trade(to_north, to_south, "lat"), weights2, e1],
         [near, near],
     )
     p_own, w_own, to_north, to_south, s_own, sums = call(
         first_up_kernel,
         [(ROWS, LEV, OWN), (ROWS,) + row, (SEND,) + row, (SEND,) + row, (ROWS, LEV, OWN), (2, LEV, OWN)],
-        [e2, *trade(e2, e2_again, "lat"), f2_near, weights2, blocks, s, e0, f1, e1] + grids + [diag],
+        [e2, *trade(edge_north, edge_south, "lat"), f2_near, weights2, blocks, s, e0, f1, e1] + grids + [diag],
         [near, mid, fine, fine],
     )
     w_rows = trade(to_north, to_south, "lat")
@@ -525,16 +551,16 @@
         [w_own, *w_rows, weights2, blocks] + grids,
         [fine, (2,) + row],
     )
-    f2_near, e2, e2_again, dots = call(
+    f2_near, e2, edge_north, edge_south, dots = call(
         coarse_dot_kernel,
-        [near, (2,) + line, (2,) + line, lines],
-        [f2, *trade(to_north, to_south, "lat"), weights2, sums, sum_wq],
+        [near, (2,) + line, edge, edge, lines],
+        [f2, *trade(to_north, to_south, "lat"), weights2, e1, sums, sum_wq],
         [near, near],
     )
     q, dots = call(
         second_up_kernel,
         [(LEV, ROWS, OWN), lines],
-        [e2, *trade(e2, e2_again, "lat"), f2_near, weights2, blocks, w_own, e0, f1, e1] + grids + [dots],
+        [e2, *trade(edge_north, edge_south, "lat"), f2_near, weights2, blocks, w_own, e0, f1, e1] + grids + [dots],
         [near, mid, fine, fine, fine],
     )
     (dots,) = call(total_kernel, [(z_size, 128)], [lax.all_to_all(dots, ("x", "lat"), 0, 0, tiled=True)])

time: 99.2 us -> 94.1 us (0.949)
  Pallas kernels: 15.3 us -> 12 us
  waiting for transfers between devices: 27.1 us -> 24.7 us
    pallas_call x12, Pallas kernels: 15.3 us -> 12 us  [call(): pl.pallas_call(body, out_shape=[jax.ShapeDtypeStruct(o, F32) for o in out...]
    ppermute x8, starting transfers between devices: 37.2 us -> 34.4 us  [trade(): return (lax.ppermute(to_last, axis, [(j, i) for i, j in up]), from_last)]
    ppermute x8, starting transfers between devices: 1.94 us -> 4.35 us  [trade(): from_last = lax.ppermute(to_next, axis, up)]
    ppermute x8, waiting for transfers between devices: 8.47 us -> 6.69 us  [trade(): from_last = lax.ppermute(to_next, axis, up)]
where the time goes in v3:
time: 94.1 us; the launch traced here: 93.8 us
  starting transfers between devices  42.8 us (45%)
  waiting for transfers between devices  24.7 us (26%)
  blocking collectives  13.3 us (14%)
  Pallas kernels  12 us (13%)
    ppermute x8, starting transfers between devices, trade(): return (lax.ppermute(to_last, axis, [(j, i) for i, j in up]), from_last)  34.4 us
    all_to_all x1, blocking collectives, shards(): lax.all_to_all(dots, ('x', 'lat'), 0, 0, tiled=True)  13.3 us
    pallas_call x12, Pallas kernels, call(): pl.pallas_call(body, out_shape=[jax.ShapeDtypeStruct(o, F32) for o in out...  12 us
    all_to_all x1, waiting for transfers between devices, shards(): dots = lax.all_to_all(dots, 'z', 0, 0, tiled=True)  11.1 us
    ppermute x8, waiting for transfers between devices, trade(): return (lax.ppermute(to_last, axis, [(j, i) for i, j in up]), from_last)  6.98 us
    ppermute x8, waiting for transfers between devices, trade(): from_last = lax.ppermute(to_next, axis, up)  6.69 us
    ppermute x8, starting transfers between devices, trade(): from_last = lax.ppermute(to_next, axis, up)  4.35 us
    all_to_all x1, starting transfers between devices, shards(): dots = lax.all_to_all(dots, 'z', 0, 0, tiled=True)  4.14 us
  transfers between devices with their start and end apart: 17, of which 13 were waited for; matrix products, arithmetic and copies ran while one was open for 0% of the time, Pallas kernels for 1%

profile of v3, /device:TPU:1, one launch (start us, length us, event | category | flops | bytes accessed | tf_op | source)
XLA Modules:
  0.0 93.8 jit_solution(2991404160559611175)
XLA Ops:
  0.7 2.2 %shard_map.76 = (f32[4,3,16,512]{3,2,1,0:T(8,128)}, f32[4,3,16,512]{3,2,1,0:T(8,128)}, f32[8,16,128]{2,1,0:T(8,128)}, f32[8,16,128]{2,1,0:T(8,128)}) custom-call(f32[16,8,512]{2,1,0:T(8,128)} %b_ref.3, f32[16,8,512]{2,1,0:T(8,128)} %x.1, f32[16,8,512]{2,1,0:T(8,128)} %c_ref.3), custom_call_target="tpu_custom_call" | custom-call | flops 1000000 | bytes 1000000 | tf_op jit(solution)/shard_map/pallas_call | solution.py:33
  2.9 14.1 %collective-permute-start.2 = (f32[8,16,128]{2,1,0:T(8,128)}, f32[8,16,128]{2,1,0:T(8,128)S(1)}, u32[]{:S(2)}, u32[]{:S(2)}) collective-permute-start(f32[8,16,128]{2,1,0:T(8,128)} %get-tuple-element.69), channel_id=1, source_target_pairs={{8,0},{16,8},{24,16},{32,24},{40,32},{48,40},{56,48},{64,56},{72,6... | collective-permute-start | bytes 196616 | tf_op jit(solution)/shard_map/ppermute | solution.py:501
  17.0 1.9 %collective-permute-start.3 = (f32[8,16,128]{2,1,0:T(8,128)}, f32[8,16,128]{2,1,0:T(8,128)S(1)}, u32[]{:S(2)}, u32[]{:S(2)}) collective-permute-start(f32[8,16,128]{2,1,0:T(8,128)} %get-tuple-element.70), channel_id=1, source_target_pairs={{0,8},{8,16},{16,24},{24,32},{32,40},{40,48},{48,56},{56,64},{64,7... | collective-permute-start | bytes 196616 | tf_op jit(solution)/shard_map/ppermute | solution.py:500
  19.0 1.0 %collective-permute-start = (f32[4,3,16,512]{3,2,1,0:T(8,128)}, f32[4,3,16,512]{3,2,1,0:T(8,128)S(1)}, u32[]{:S(2)}, u32[]{:S(2)}) collective-permute-start(f32[4,3,16,512]{3,2,1,0:T(8,128)} %get-tuple-element.61), channel_id=1, source_target_pairs={{1,0},{2,1},{3,2},{4,3},{5,4},{6,5},{7,6},{0,7},{9,8},{10,9},{11,1... | collective-permute-start | bytes 1179656 | tf_op jit(solution)/shard_map/ppermute | solution.py:501
  19.9 1.2 %collective-permute-start.1 = (f32[4,3,16,512]{3,2,1,0:T(8,128)}, f32[4,3,16,512]{3,2,1,0:T(8,128)S(1)}, u32[]{:S(2)}, u32[]{:S(2)}) collective-permute-start(f32[4,3,16,512]{3,2,1,0:T(8,128)} %get-tuple-element.62), channel_id=1, source_target_pairs={{0,1},{1,2},{2,3},{3,4},{4,5},{5,6},{6,7},{7,0},{8,9},{9,10},{10,1... | collective-permute-start | bytes 1179656 | tf_op jit(solution)/shard_map/ppermute | solution.py:500
  21.2 4.4 %collective-permute-done.3.from_west = f32[8,16,128]{2,1,0:T(8,128)S(1)} collective-permute-done((f32[8,16,128]{2,1,0:T(8,128)}, f32[8,16,128]{2,1,0:T(8,128)S(1)}, u32[]{:S(2)}, u32[]{:S(2)}) %collective-permute-start.3) | collective-permute-done | bytes 65568 | tf_op jit(solution)/shard_map/ppermute | solution.py:500
  25.8 2.1 %collective-permute-start.4 = (f32[4,3,16,128]{3,2,1,0:T(8,128)S(1)}, f32[4,3,16,128]{3,2,1,0:T(8,128)S(1)}, u32[]{:S(2)}, u32[]{:S(2)}) collective-permute-start(f32[4,3,16,128]{3,2,1,0:T(8,128)S(1)} %get-tuple-element.72), channel_id=1, source_target_pairs={{1,0},{2,1},{3,2},{4,3},{5,4},{6,5},{7,6},{0,7},{9,8},{10,9},{11,1... | collective-permute-start | bytes 294920 | tf_op jit(solution)/shard_map/ppermute | solution.py:501
  27.9 1.2 %collective-permute-start.5 = (f32[4,3,16,128]{3,2,1,0:T(8,128)S(1)}, f32[4,3,16,128]{3,2,1,0:T(8,128)S(1)}, u32[]{:S(2)}, u32[]{:S(2)}) collective-permute-start(f32[4,3,16,128]{3,2,1,0:T(8,128)S(1)} %get-tuple-element.73), channel_id=1, source_target_pairs={{0,1},{1,2},{2,3},{3,4},{4,5},{5,6},{6,7},{7,0},{8,9},{9,10},{10,1... | collective-permute-start | bytes 294920 | tf_op jit(solution)/shard_map/ppermute | solution.py:500
  29.7 1.7 %collective-permute-done.4.rim_north = f32[4,3,16,128]{3,2,1,0:T(8,128)S(1)} collective-permute-done((f32[4,3,16,128]{3,2,1,0:T(8,128)S(1)}, f32[4,3,16,128]{3,2,1,0:T(8,128)S(1)}, u32[]{:S(2)}, u32[]{:S(2)}) %collective-permute-start.4) | collective-permute-done | bytes 98336 | tf_op jit(solution)/shard_map/ppermute | solution.py:501
  31.4 3.4 %shard_map.79 = (f32[16,16,640]{2,1,0:T(8,128)S(1)}, f32[2,16,256]{2,1,0:T(8,128)S(1)}, f32[6,16,256]{2,1,0:T(8,128)S(1)}, f32[6,16,256]{2,1,0:T(8,128)S(1)}, f3...) custom-call(f32[16,16,512]{2,1,0:T(8,128)S(1)} %get-tuple-element.63, ...), custom_call_target="tpu_custom_call" | custom-call | flops 1000000 | bytes 1000000 | tf_op jit(solution)/shard_map/pallas_call | solution.py:33
  34.8 2.8 %collective-permute-start.6 = (f32[6,16,256]{2,1,0:T(8,128)S(1)}, f32[6,16,256]{2,1,0:T(8,128)S(1)}, u32[]{:S(2)}, u32[]{:S(2)}) collective-permute-start(f32[6,16,256]{2,1,0:T(8,128)S(1)} %get-tuple-element.75), channel_id=1, source_target_pairs={{1,0},{2,1},{3,2},{4,3},{5,4},{6,5},{7,6},{0,7},{9,8},{10,9},{11,1... | collective-permute-start | bytes 294920 | tf_op jit(solution)/shard_map/ppermute | solution.py:501
  37.6 1.3 %collective-permute-done.6.from_north = f32[6,16,256]{2,1,0:T(8,128)S(1)} collective-permute-done((f32[6,16,256]{2,1,0:T(8,128)S(1)}, f32[6,16,256]{2,1,0:T(8,128)S(1)}, u32[]{:S(2)}, u32[]{:S(2)}) %collective-permute-start.6) | collective-permute-done | bytes 98336 | tf_op jit(solution)/shard_map/ppermute | solution.py:501
  39.4 3.6 %collective-permute-start.8 = (f32[16,1152]{1,0:T(8,128)S(1)}, f32[16,1152]{1,0:T(8,128)S(1)}, u32[]{:S(2)}, u32[]{:S(2)}) collective-permute-start(f32[16,1152]{1,0:T(8,128)S(1)} %get-tuple-element.80), channel_id=1, source_target_pairs={{1,0},{2,1},{3,2},{4,3},{5,4},{6,5},{7,6},{0,7},{9,8},{10,9},{11,1... | collective-permute-start | bytes 221192 | tf_op jit(solution)/shard_map/ppermute | solution.py:501
  44.5 1.5 %shard_map.81 = (f32[8,16,512]{2,1,0:T(8,128)S(1)}, f32[8,16,640]{2,1,0:T(8,128)S(1)}, f32[3,16,640]{2,1,0:T(8,128)S(1)}, f32[3,16,640]{2,1,0:T(8,128)S(1)}, f32...) custom-call(f32[2,16,256]{2,1,0:T(8,128)S(1)} %get-tuple-element.79.e2, ...), custom_call_target="tpu_custom_call" | custom-call | flops 1000000 | bytes 1000000 | tf_op jit(solution)/shard_map/pallas_call | solution.py:33
  46.0 3.6 %collective-permute-start.10 = (f32[3,16,640]{2,1,0:T(8,128)S(1)}, f32[3,16,640]{2,1,0:T(8,128)S(1)}, u32[]{:S(2)}, u32[]{:S(2)}) collective-permute-start(f32[3,16,640]{2,1,0:T(8,128)S(1)} %get-tuple-element.97), channel_id=1, source_target_pairs={{1,0},{2,1},{3,2},{4,3},{5,4},{6,5},{7,6},{0,7},{9,8},{10,9},{11,1... | collective-permute-start | bytes 368648 | tf_op jit(solution)/shard_map/ppermute | solution.py:501
  49.7 1.3 %collective-permute-done.10.from_north = f32[3,16,640]{2,1,0:T(8,128)S(1)} collective-permute-done((f32[3,16,640]{2,1,0:T(8,128)S(1)}, f32[3,16,640]{2,1,0:T(8,128)S(1)}, u32[]{:S(2)}, u32[]{:S(2)}) %collective-permute-start.10) | collective-permute-done | bytes 122912 | tf_op jit(solution)/shard_map/ppermute | solution.py:501
  51.5 1.1 %shard_map.82 = (f32[2,16,256]{2,1,0:T(8,128)S(1)}, f32[2,16,256]{2,1,0:T(8,128)S(1)}, f32[2,16,256]{2,1,0:T(8,128)S(1)}, f32[16,16,640]{2,1,0:T(8,128)S(1)}, f3...) custom-call(f32[8,16,640]{2,1,0:T(8,128)S(1)} %get-tuple-element.96.w_own.w, ...), custom_call_target="tpu_custom_call" | custom-call | flops 1000000 | bytes 1000000 | tf_op jit(solution)/shard_map/pallas_call | solution.py:33
  52.6 3.7 %collective-permute-start.12 = (f32[2,16,256]{2,1,0:T(8,128)S(1)}, f32[2,16,256]{2,1,0:T(8,128)S(1)}, u32[]{:S(2)}, u32[]{:S(2)}) collective-permute-start(f32[2,16,256]{2,1,0:T(8,128)S(1)} %get-tuple-element.100), channel_id=1, source_target_pairs={{1,0},{2,1},{3,2},{4,3},{5,4},{6,5},{7,6},{0,7},{9,8},{10,9},{11,1... | collective-permute-start | bytes 98312 | tf_op jit(solution)/shard_map/ppermute | solution.py:501
  57.8 3.4 %collective-permute-start.14 = (f32[16,1152]{1,0:T(8,128)S(1)}, f32[16,1152]{1,0:T(8,128)S(1)}, u32[]{:S(2)}, u32[]{:S(2)}) collective-permute-start(f32[16,1152]{1,0:T(8,128)S(1)} %get-tuple-element.106), channel_id=1, source_target_pairs={{1,0},{2,1},{3,2},{4,3},{5,4},{6,5},{7,6},{0,7},{9,8},{10,9},{11,1... | collective-permute-start | bytes 221192 | tf_op jit(solution)/shard_map/ppermute | solution.py:501
  62.6 0.9 shard_map.84
  63.6 13.3 %all_to_all.22 = f32[32,1,128]{2,1,0:T(1,128)S(1)} all-to-all(f32[32,1,128]{2,1,0:T(1,128)S(1)} %bitcast.16), channel_id=1, replica_groups=mesh['x'=4,'z'=16,'lat'=8] {'x','lat'}, dimensions={0} | all-to-all | bytes 32768 | tf_op jit(solution)/shard_map/all_to_all | solution.py:566
  77.5 4.1 %all-to-all-start.1 = ((f32[16,1,128]{2,1,0:T(1,128)}), f32[16,1,128]{2,1,0:T(1,128)S(1)}, u32[]{:S(2)}, u32[]{:S(2)}) async-start(f32[16,1,128]{2,1,0:T(1,128)} %bitcast.6), calls=%async_computation.1 | async-start | bytes 16384 | tf_op jit(solution)/shard_map/all_to_all | solution.py:567
  81.8 11.1 %all-to-all-done.1 = f32[16,1,128]{2,1,0:T(1,128)S(1)} async-done(((f32[16,1,128]{2,1,0:T(1,128)}), f32[16,1,128]{2,1,0:T(1,128)S(1)}, u32[]{:S(2)}, u32[]{:S(2)}) %all-to-all-start.1) | async-done | bytes 8224 | tf_op jit(solution)/shard_map/all_to_all | solution.py:567
  92.8 1.0 %shard_map.87 = (f32[16,8,512]{2,1,0:T(8,128)}, f32[16,8,512]{2,1,0:T(8,128)}, f32[16,8,512]{2,1,0:T(8,128)}) custom-call(f32[16,128]{1,0:T(8,128)S(1)} %bitcast.15, f32[16,8,512]{2,1,0:T(8,128)S(1)} %copy-done.1, f32[16,8,512]{2,1,0:T(8,128)S(1)} %get-tuple-element.115.p, f32[16,8,512]{2,1,0:T(8,128)S(1)} %get-tuple-element.116.w, ...), custom_call_target="tpu_custom_call" | custom-call | flops 1000000 | bytes 1000000 | tf_op jit(solution)/shard_map/pallas_call | solution.py:33
  (37 shorter events, 6.9 us)
Async XLA Ops:
  0.6 28.5 %copy-start.1 = (f32[16,8,512]{2,1,0:T(8,128)S(1)}, f32[16,8,512]{2,1,0:T(8,128)}, u32[]{:S(2)}) copy-start(f32[16,8,512]{2,1,0:T(8,128)} %x.1) | copy-start | bytes 786436
  0.6 28.5 %copy-start.2 = (f32[16,8,512]{2,1,0:T(8,128)S(1)}, f32[16,8,512]{2,1,0:T(8,128)}, u32[]{:S(2)}) copy-start(f32[16,8,512]{2,1,0:T(8,128)} %b_ref.3) | copy-start | bytes 786436
  0.7 28.5 %copy-start.3 = (f32[16,8,512]{2,1,0:T(8,128)S(1)}, f32[16,8,512]{2,1,0:T(8,128)}, u32[]{:S(2)}) copy-start(f32[16,8,512]{2,1,0:T(8,128)} %c_ref.3) | copy-start | bytes 786436
  2.9 18.3 %copy-start.4 = (f32[2,4,16]{2,1,0:T(4,128)S(1)}, f32[2,4,16]{2,1,0:T(4,128)}, u32[]{:S(2)}) copy-start(f32[2,4,16]{2,1,0:T(4,128)} %param.8) | copy-start | bytes 1540
  2.9 18.3 %collective-permute-start.2 = (f32[8,16,128]{2,1,0:T(8,128)}, f32[8,16,128]{2,1,0:T(8,128)S(1)}, u32[]{:S(2)}, u32[]{:S(2)}) collective-permute-start(f32[8,16,128]{2,1,0:T(8,128)} %get-tuple-element.69), channel_id=1, source_target_pairs={{8,0},{16,8},{24,16},{32,24},{40,32},{48,40},{56,48},{64,56},{72,6... | collective-permute-start | bytes 196616 | tf_op jit(solution)/shard_map/ppermute | solution.py:501
  17.0 8.5 %collective-permute-start.3 = (f32[8,16,128]{2,1,0:T(8,128)}, f32[8,16,128]{2,1,0:T(8,128)S(1)}, u32[]{:S(2)}, u32[]{:S(2)}) collective-permute-start(f32[8,16,128]{2,1,0:T(8,128)} %get-tuple-element.70), channel_id=1, source_target_pairs={{0,8},{8,16},{16,24},{24,32},{32,40},{40,48},{48,56},{56,64},{64,7... | collective-permute-start | bytes 196616 | tf_op jit(solution)/shard_map/ppermute | solution.py:500
  19.0 10.1 %collective-permute-start = (f32[4,3,16,512]{3,2,1,0:T(8,128)}, f32[4,3,16,512]{3,2,1,0:T(8,128)S(1)}, u32[]{:S(2)}, u32[]{:S(2)}) collective-permute-start(f32[4,3,16,512]{3,2,1,0:T(8,128)} %get-tuple-element.61), channel_id=1, source_target_pairs={{1,0},{2,1},{3,2},{4,3},{5,4},{6,5},{7,6},{0,7},{9,8},{10,9},{11,1... | collective-permute-start | bytes 1179656 | tf_op jit(solution)/shard_map/ppermute | solution.py:501
  19.9 9.2 %collective-permute-start.1 = (f32[4,3,16,512]{3,2,1,0:T(8,128)}, f32[4,3,16,512]{3,2,1,0:T(8,128)S(1)}, u32[]{:S(2)}, u32[]{:S(2)}) collective-permute-start(f32[4,3,16,512]{3,2,1,0:T(8,128)} %get-tuple-element.62), channel_id=1, source_target_pairs={{0,1},{1,2},{2,3},{3,4},{4,5},{5,6},{6,7},{7,0},{8,9},{9,10},{10,1... | collective-permute-start | bytes 1179656 | tf_op jit(solution)/shard_map/ppermute | solution.py:500
  25.8 5.6 %collective-permute-start.4 = (f32[4,3,16,128]{3,2,1,0:T(8,128)S(1)}, f32[4,3,16,128]{3,2,1,0:T(8,128)S(1)}, u32[]{:S(2)}, u32[]{:S(2)}) collective-permute-start(f32[4,3,16,128]{3,2,1,0:T(8,128)S(1)} %get-tuple-element.72), channel_id=1, source_target_pairs={{1,0},{2,1},{3,2},{4,3},{5,4},{6,5},{7,6},{0,7},{9,8},{10,9},{11,1... | collective-permute-start | bytes 294920 | tf_op jit(solution)/shard_map/ppermute | solution.py:501
  27.9 3.5 %collective-permute-start.5 = (f32[4,3,16,128]{3,2,1,0:T(8,128)S(1)}, f32[4,3,16,128]{3,2,1,0:T(8,128)S(1)}, u32[]{:S(2)}, u32[]{:S(2)}) collective-permute-start(f32[4,3,16,128]{3,2,1,0:T(8,128)S(1)} %get-tuple-element.73), channel_id=1, source_target_pairs={{0,1},{1,2},{2,3},{3,4},{4,5},{5,6},{6,7},{7,0},{8,9},{9,10},{10,1... | collective-permute-start | bytes 294920 | tf_op jit(solution)/shard_map/ppermute | solution.py:500
  29.2 2.2 %copy-start = (bf16[640,256]{1,0:T(8,128)(2,1)S(1)}, bf16[640,256]{1,0:T(8,128)(2,1)}, u32[]{:S(2)}) copy-start(bf16[640,256]{1,0:T(8,128)(2,1)} %constant.2.clone.blocks) | copy-start | bytes 983044
  34.8 4.1 %collective-permute-start.6 = (f32[6,16,256]{2,1,0:T(8,128)S(1)}, f32[6,16,256]{2,1,0:T(8,128)S(1)}, u32[]{:S(2)}, u32[]{:S(2)}) collective-permute-start(f32[6,16,256]{2,1,0:T(8,128)S(1)} %get-tuple-element.75), channel_id=1, source_target_pairs={{1,0},{2,1},{3,2},{4,3},{5,4},{6,5},{7,6},{0,7},{9,8},{10,9},{11,1... | collective-permute-start | bytes 294920 | tf_op jit(solution)/shard_map/ppermute | solution.py:501
  37.6 1.6 %collective-permute-start.7 = (f32[6,16,256]{2,1,0:T(8,128)S(1)}, f32[6,16,256]{2,1,0:T(8,128)S(1)}, u32[]{:S(2)}, u32[]{:S(2)}) collective-permute-start(f32[6,16,256]{2,1,0:T(8,128)S(1)} %get-tuple-element.76), channel_id=1, source_target_pairs={{0,1},{1,2},{2,3},{3,4},{4,5},{5,6},{6,7},{7,0},{8,9},{9,10},{10,1... | collective-permute-start | bytes 294920 | tf_op jit(solution)/shard_map/ppermute | solution.py:500
  39.4 4.6 %collective-permute-start.8 = (f32[16,1152]{1,0:T(8,128)S(1)}, f32[16,1152]{1,0:T(8,128)S(1)}, u32[]{:S(2)}, u32[]{:S(2)}) collective-permute-start(f32[16,1152]{1,0:T(8,128)S(1)} %get-tuple-element.80), channel_id=1, source_target_pairs={{1,0},{2,1},{3,2},{4,3},{5,4},{6,5},{7,6},{0,7},{9,8},{10,9},{11,1... | collective-permute-start | bytes 221192 | tf_op jit(solution)/shard_map/ppermute | solution.py:501
  43.1 1.4 %collective-permute-start.9 = (f32[16,1152]{1,0:T(8,128)S(1)}, f32[16,1152]{1,0:T(8,128)S(1)}, u32[]{:S(2)}, u32[]{:S(2)}) collective-permute-start(f32[16,1152]{1,0:T(8,128)S(1)} %get-tuple-element.81), channel_id=1, source_target_pairs={{0,1},{1,2},{2,3},{3,4},{4,5},{5,6},{6,7},{7,0},{8,9},{9,10},{10,1... | collective-permute-start | bytes 221192 | tf_op jit(solution)/shard_map/ppermute | solution.py:500
  46.0 4.9 %collective-permute-start.10 = (f32[3,16,640]{2,1,0:T(8,128)S(1)}, f32[3,16,640]{2,1,0:T(8,128)S(1)}, u32[]{:S(2)}, u32[]{:S(2)}) collective-permute-start(f32[3,16,640]{2,1,0:T(8,128)S(1)} %get-tuple-element.97), channel_id=1, source_target_pairs={{1,0},{2,1},{3,2},{4,3},{5,4},{6,5},{7,6},{0,7},{9,8},{10,9},{11,1... | collective-permute-start | bytes 368648 | tf_op jit(solution)/shard_map/ppermute | solution.py:501
  49.6 1.9 %collective-permute-start.11 = (f32[3,16,640]{2,1,0:T(8,128)S(1)}, f32[3,16,640]{2,1,0:T(8,128)S(1)}, u32[]{:S(2)}, u32[]{:S(2)}) collective-permute-start(f32[3,16,640]{2,1,0:T(8,128)S(1)} %get-tuple-element.98), channel_id=1, source_target_pairs={{0,1},{1,2},{2,3},{3,4},{4,5},{5,6},{6,7},{7,0},{8,9},{9,10},{10,1... | collective-permute-start | bytes 368648 | tf_op jit(solution)/shard_map/ppermute | solution.py:500
  52.6 4.5 %collective-permute-start.12 = (f32[2,16,256]{2,1,0:T(8,128)S(1)}, f32[2,16,256]{2,1,0:T(8,128)S(1)}, u32[]{:S(2)}, u32[]{:S(2)}) collective-permute-start(f32[2,16,256]{2,1,0:T(8,128)S(1)} %get-tuple-element.100), channel_id=1, source_target_pairs={{1,0},{2,1},{3,2},{4,3},{5,4},{6,5},{7,6},{0,7},{9,8},{10,9},{11,1... | collective-permute-start | bytes 98312 | tf_op jit(solution)/shard_map/ppermute | solution.py:501
  56.3 1.2 %collective-permute-start.13 = (f32[2,16,256]{2,1,0:T(8,128)S(1)}, f32[2,16,256]{2,1,0:T(8,128)S(1)}, u32[]{:S(2)}, u32[]{:S(2)}) collective-permute-start(f32[2,16,256]{2,1,0:T(8,128)S(1)} %get-tuple-element.101), channel_id=1, source_target_pairs={{0,1},{1,2},{2,3},{3,4},{4,5},{5,6},{6,7},{7,0},{8,9},{9,10},{10,1... | collective-permute-start | bytes 98312 | tf_op jit(solution)/shard_map/ppermute | solution.py:500
  57.8 4.3 %collective-permute-start.14 = (f32[16,1152]{1,0:T(8,128)S(1)}, f32[16,1152]{1,0:T(8,128)S(1)}, u32[]{:S(2)}, u32[]{:S(2)}) collective-permute-start(f32[16,1152]{1,0:T(8,128)S(1)} %get-tuple-element.106), channel_id=1, source_target_pairs={{1,0},{2,1},{3,2},{4,3},{5,4},{6,5},{7,6},{0,7},{9,8},{10,9},{11,1... | collective-permute-start | bytes 221192 | tf_op jit(solution)/shard_map/ppermute | solution.py:501
  61.2 1.4 %collective-permute-start.15 = (f32[16,1152]{1,0:T(8,128)S(1)}, f32[16,1152]{1,0:T(8,128)S(1)}, u32[]{:S(2)}, u32[]{:S(2)}) collective-permute-start(f32[16,1152]{1,0:T(8,128)S(1)} %get-tuple-element.107), channel_id=1, source_target_pairs={{0,1},{1,2},{2,3},{3,4},{4,5},{5,6},{6,7},{7,0},{8,9},{9,10},{10,1... | collective-permute-start | bytes 221192 | tf_op jit(solution)/shard_map/ppermute | solution.py:500
  77.5 15.4 %all-to-all-start.1 = ((f32[16,1,128]{2,1,0:T(1,128)}), f32[16,1,128]{2,1,0:T(1,128)S(1)}, u32[]{:S(2)}, u32[]{:S(2)}) async-start(f32[16,1,128]{2,1,0:T(1,128)} %bitcast.6), calls=%async_computation.1 | async-start | bytes 16384 | tf_op jit(solution)/shard_map/all_to_all | solution.py:567

commit v4 on v3

--- a/solution.py
+++ b/solution.py
@@ -29,12 +29,12 @@
 HBM = pl.BlockSpec(memory_space=pltpu.HBM)
 
 
-def call(body, outs, ins, scratch=(), specs=(), copies=0):
+def call(body, outs, ins, scratch=(), specs=(), copies=0, out_spec=VMEM):
     return pl.pallas_call(
         body,
         out_shape=[jax.ShapeDtypeStruct(o, F32) for o in outs],
         in_specs=list(specs) + [VMEM] * (len(ins) - len(specs)),
-        out_specs=[VMEM] * len(outs),
+        out_specs=[out_spec] * len(outs),
         scratch_shapes=[pltpu.VMEM(s, F32) for s in scratch] + [pltpu.SemaphoreType.DMA((copies,))] * (copies > 0),
         compiler_params=pltpu.CompilerParams(vmem_limit_bytes=(60 if copies else 24) * 1024 * 1024),
         cost_estimate=pl.CostEstimate(flops=1000000, bytes_accessed=1000000, transcendentals=0),
@@ -42,13 +42,11 @@
 
 
 def loop(first, end, body):
-    rows = end - first
-
     def step(i, carry):
         body(i)
         return carry
 
-    lax.fori_loop(first, end, step, 0, unroll=rows if rows <= 8 else rows // 2)
+    lax.fori_loop(first, end, step, 0, unroll=True)
 
 
 def lane_ids():
@@ -101,24 +99,35 @@
     return total
 
 
-def pack_kernel(b_ref, x_ref, c_ref, north_ref, south_ref, east_ref, west_ref, held, turned, arrived):
+def pack_kernel(
+    b_ref, x_ref, c_ref, to_north, to_south, to_east, to_west,
+    held, turned, north_ref, south_ref, east_ref, west_ref, moved,
+):
     lane = lax.broadcasted_iota(jnp.int32, (LEV, 128), 1)
-    copies = [pltpu.make_async_copy(ref, held.at[j], arrived.at[j]) for j, ref in enumerate((b_ref, x_ref, c_ref))]
+    copies = [pltpu.make_async_copy(ref, held.at[j], moved.at[j]) for j, ref in enumerate((b_ref, x_ref, c_ref))]
     for copy in copies:
         copy.start()
     for j, copy in enumerate(copies):
         copy.wait()
         field = jnp.swapaxes(held[j], 0, 1)
+        turned[j, :, :, :128] = field[:, :, :128]
+        turned[j, :, :, 128:] = field[:, :, OWN - 128:]
         south_ref[:, j] = field[:RIM]
         north_ref[:, j] = field[ROWS - RIM:]
-        turned[j, :, :, :128] = field[:, :, :128]
-        turned[j, :, :, 128:] = field[:, :, OWN - 128:]
+    results = ((north_ref, to_north), (south_ref, to_south), (east_ref, to_east), (west_ref, to_west))
+    copies = [pltpu.make_async_copy(a, b, moved.at[3 + j]) for j, (a, b) in enumerate(results)]
+    copies[0].start()
+    copies[1].start()
     for r in range(ROWS):
         b, x, c = [turned[j, r, :, :128] for j in range(3)]
         west_ref[r] = jnp.where(lane < DEEP, b, jnp.where(lane < 2 * DEEP, prev_lane(x, DEEP), prev_lane(c, 2 * DEEP)))
         b, x, c = [turned[j, r, :, 128:] for j in range(3)]
         x, c = next_lane(x, DEEP), next_lane(c, 2 * DEEP)
         east_ref[r] = jnp.where(lane >= 128 - DEEP, b, jnp.where(lane >= 128 - 2 * DEEP, x, c))
+    copies[2].start()
+    copies[3].start()
+    for copy in copies:
+        copy.wait()
 
 
 def rim_kernel(from_east, from_west, rim_ref, north_ref, south_ref):
@@ -402,7 +411,7 @@
         return totals[0] + s_row * p_row, totals[1] + p_row * w_row[:, :OWN]
 
     zero = jnp.zeros((LEV, OWN), F32)
-    sums[0], sums[1] = lax.fori_loop(0, ROWS, image, (zero, zero), unroll=4)
+    sums[0], sums[1] = lax.fori_loop(0, ROWS, image, (zero, zero), unroll=True)
     w_south[...] = w_own[:SEND]
     w_north[...] = w_own[ROWS - SEND:]
 
@@ -507,9 +516,10 @@
         pack_kernel,
         [(RIM, 3, LEV, OWN)] * 2 + [(ROWS, LEV, 128)] * 2,
         fields,
-        [(3, LEV, ROWS, OWN), (3, ROWS, LEV, 256)],
+        [(3, LEV, ROWS, OWN), (3, ROWS, LEV, 256)] + [(RIM, 3, LEV, OWN)] * 2 + [(ROWS, LEV, 128)] * 2,
         specs=[HBM] * 3,
-        copies=3,
+        copies=7,
+        out_spec=HBM,
     )
     lat_rows = trade(to_north, to_south, "lat")
     lon_rims = trade(to_east, to_west, lon)

time: 94.1 us -> 93.7 us (level)
  no operation moved by 1% of the time
where the time goes in v4:
time: 93.7 us; the launch traced here: 93.5 us
  starting transfers between devices  42.8 us (46%)
  waiting for transfers between devices  24.7 us (26%)
  blocking collectives  13.3 us (14%)
  Pallas kernels  11.7 us (12%)
    ppermute x8, starting transfers between devices, trade(): return (lax.ppermute(to_last, axis, [(j, i) for i, j in up]), from_last)  34.4 us
    all_to_all x1, blocking collectives, shards(): lax.all_to_all(dots, ('x', 'lat'), 0, 0, tiled=True)  13.3 us
    pallas_call x12, Pallas kernels, call(): pl.pallas_call(body, out_shape=[jax.ShapeDtypeStruct(o, F32) for o in out...  11.7 us
    all_to_all x1, waiting for transfers between devices, shards(): dots = lax.all_to_all(dots, 'z', 0, 0, tiled=True)  11.1 us
    ppermute x8, waiting for transfers between devices, trade(): return (lax.ppermute(to_last, axis, [(j, i) for i, j in up]), from_last)  6.98 us
    ppermute x8, waiting for transfers between devices, trade(): from_last = lax.ppermute(to_next, axis, up)  6.69 us
    ppermute x8, starting transfers between devices, trade(): from_last = lax.ppermute(to_next, axis, up)  4.35 us
    all_to_all x1, starting transfers between devices, shards(): dots = lax.all_to_all(dots, 'z', 0, 0, tiled=True)  4.14 us
  transfers between devices with their start and end apart: 17, of which 13 were waited for; matrix products, arithmetic and copies ran while one was open for 0% of the time, Pallas kernels for 1%

profile of v4, /device:TPU:1, one launch (start us, length us, event | category | flops | bytes accessed | tf_op | source)
XLA Modules:
  0.0 93.5 jit_solution(8105596725685625370)
XLA Ops:
  0.7 2.2 %shard_map.76 = (f32[4,3,16,512]{3,2,1,0:T(8,128)}, f32[4,3,16,512]{3,2,1,0:T(8,128)}, f32[8,16,128]{2,1,0:T(8,128)}, f32[8,16,128]{2,1,0:T(8,128)}) custom-call(f32[16,8,512]{2,1,0:T(8,128)} %b_ref.3, f32[16,8,512]{2,1,0:T(8,128)} %x.1, f32[16,8,512]{2,1,0:T(8,128)} %c_ref.3), custom_call_target="tpu_custom_call" | custom-call | flops 1000000 | bytes 1000000 | tf_op jit(solution)/shard_map/pallas_call | solution.py:33
  2.9 14.1 %collective-permute-start.2 = (f32[8,16,128]{2,1,0:T(8,128)}, f32[8,16,128]{2,1,0:T(8,128)S(1)}, u32[]{:S(2)}, u32[]{:S(2)}) collective-permute-start(f32[8,16,128]{2,1,0:T(8,128)} %get-tuple-element.69), channel_id=1, source_target_pairs={{8,0},{16,8},{24,16},{32,24},{40,32},{48,40},{56,48},{64,56},{72,6... | collective-permute-start | bytes 196616 | tf_op jit(solution)/shard_map/ppermute | solution.py:510
  17.1 1.9 %collective-permute-start.3 = (f32[8,16,128]{2,1,0:T(8,128)}, f32[8,16,128]{2,1,0:T(8,128)S(1)}, u32[]{:S(2)}, u32[]{:S(2)}) collective-permute-start(f32[8,16,128]{2,1,0:T(8,128)} %get-tuple-element.70), channel_id=1, source_target_pairs={{0,8},{8,16},{16,24},{24,32},{32,40},{40,48},{48,56},{56,64},{64,7... | collective-permute-start | bytes 196616 | tf_op jit(solution)/shard_map/ppermute | solution.py:509
  19.0 1.0 %collective-permute-start = (f32[4,3,16,512]{3,2,1,0:T(8,128)}, f32[4,3,16,512]{3,2,1,0:T(8,128)S(1)}, u32[]{:S(2)}, u32[]{:S(2)}) collective-permute-start(f32[4,3,16,512]{3,2,1,0:T(8,128)} %get-tuple-element.61), channel_id=1, source_target_pairs={{1,0},{2,1},{3,2},{4,3},{5,4},{6,5},{7,6},{0,7},{9,8},{10,9},{11,1... | collective-permute-start | bytes 1179656 | tf_op jit(solution)/shard_map/ppermute | solution.py:510
  20.0 1.2 %collective-permute-start.1 = (f32[4,3,16,512]{3,2,1,0:T(8,128)}, f32[4,3,16,512]{3,2,1,0:T(8,128)S(1)}, u32[]{:S(2)}, u32[]{:S(2)}) collective-permute-start(f32[4,3,16,512]{3,2,1,0:T(8,128)} %get-tuple-element.62), channel_id=1, source_target_pairs={{0,1},{1,2},{2,3},{3,4},{4,5},{5,6},{6,7},{7,0},{8,9},{9,10},{10,1... | collective-permute-start | bytes 1179656 | tf_op jit(solution)/shard_map/ppermute | solution.py:509
  21.2 4.4 %collective-permute-done.3.from_west = f32[8,16,128]{2,1,0:T(8,128)S(1)} collective-permute-done((f32[8,16,128]{2,1,0:T(8,128)}, f32[8,16,128]{2,1,0:T(8,128)S(1)}, u32[]{:S(2)}, u32[]{:S(2)}) %collective-permute-start.3) | collective-permute-done | bytes 65568 | tf_op jit(solution)/shard_map/ppermute | solution.py:509
  25.8 2.1 %collective-permute-start.4 = (f32[4,3,16,128]{3,2,1,0:T(8,128)S(1)}, f32[4,3,16,128]{3,2,1,0:T(8,128)S(1)}, u32[]{:S(2)}, u32[]{:S(2)}) collective-permute-start(f32[4,3,16,128]{3,2,1,0:T(8,128)S(1)} %get-tuple-element.72), channel_id=1, source_target_pairs={{1,0},{2,1},{3,2},{4,3},{5,4},{6,5},{7,6},{0,7},{9,8},{10,9},{11,1... | collective-permute-start | bytes 294920 | tf_op jit(solution)/shard_map/ppermute | solution.py:510
  27.9 1.2 %collective-permute-start.5 = (f32[4,3,16,128]{3,2,1,0:T(8,128)S(1)}, f32[4,3,16,128]{3,2,1,0:T(8,128)S(1)}, u32[]{:S(2)}, u32[]{:S(2)}) collective-permute-start(f32[4,3,16,128]{3,2,1,0:T(8,128)S(1)} %get-tuple-element.73), channel_id=1, source_target_pairs={{0,1},{1,2},{2,3},{3,4},{4,5},{5,6},{6,7},{7,0},{8,9},{9,10},{10,1... | collective-permute-start | bytes 294920 | tf_op jit(solution)/shard_map/ppermute | solution.py:509
  29.7 1.7 %collective-permute-done.4.rim_north = f32[4,3,16,128]{3,2,1,0:T(8,128)S(1)} collective-permute-done((f32[4,3,16,128]{3,2,1,0:T(8,128)S(1)}, f32[4,3,16,128]{3,2,1,0:T(8,128)S(1)}, u32[]{:S(2)}, u32[]{:S(2)}) %collective-permute-start.4) | collective-permute-done | bytes 98336 | tf_op jit(solution)/shard_map/ppermute | solution.py:510
  31.4 3.4 %shard_map.79 = (f32[16,16,640]{2,1,0:T(8,128)S(1)}, f32[2,16,256]{2,1,0:T(8,128)S(1)}, f32[6,16,256]{2,1,0:T(8,128)S(1)}, f32[6,16,256]{2,1,0:T(8,128)S(1)}, f3...) custom-call(f32[16,16,512]{2,1,0:T(8,128)S(1)} %get-tuple-element.63, ...), custom_call_target="tpu_custom_call" | custom-call | flops 1000000 | bytes 1000000 | tf_op jit(solution)/shard_map/pallas_call | solution.py:33
  34.8 2.8 %collective-permute-start.6 = (f32[6,16,256]{2,1,0:T(8,128)S(1)}, f32[6,16,256]{2,1,0:T(8,128)S(1)}, u32[]{:S(2)}, u32[]{:S(2)}) collective-permute-start(f32[6,16,256]{2,1,0:T(8,128)S(1)} %get-tuple-element.75), channel_id=1, source_target_pairs={{1,0},{2,1},{3,2},{4,3},{5,4},{6,5},{7,6},{0,7},{9,8},{10,9},{11,1... | collective-permute-start | bytes 294920 | tf_op jit(solution)/shard_map/ppermute | solution.py:510
  37.6 1.3 %collective-permute-done.6.from_north = f32[6,16,256]{2,1,0:T(8,128)S(1)} collective-permute-done((f32[6,16,256]{2,1,0:T(8,128)S(1)}, f32[6,16,256]{2,1,0:T(8,128)S(1)}, u32[]{:S(2)}, u32[]{:S(2)}) %collective-permute-start.6) | collective-permute-done | bytes 98336 | tf_op jit(solution)/shard_map/ppermute | solution.py:510
  39.4 3.6 %collective-permute-start.8 = (f32[16,1152]{1,0:T(8,128)S(1)}, f32[16,1152]{1,0:T(8,128)S(1)}, u32[]{:S(2)}, u32[]{:S(2)}) collective-permute-start(f32[16,1152]{1,0:T(8,128)S(1)} %get-tuple-element.80), channel_id=1, source_target_pairs={{1,0},{2,1},{3,2},{4,3},{5,4},{6,5},{7,6},{0,7},{9,8},{10,9},{11,1... | collective-permute-start | bytes 221192 | tf_op jit(solution)/shard_map/ppermute | solution.py:510
  44.5 1.3 %shard_map.81 = (f32[8,16,512]{2,1,0:T(8,128)S(1)}, f32[8,16,640]{2,1,0:T(8,128)S(1)}, f32[3,16,640]{2,1,0:T(8,128)S(1)}, f32[3,16,640]{2,1,0:T(8,128)S(1)}, f32...) custom-call(f32[2,16,256]{2,1,0:T(8,128)S(1)} %get-tuple-element.79.e2, ...), custom_call_target="tpu_custom_call" | custom-call | flops 1000000 | bytes 1000000 | tf_op jit(solution)/shard_map/pallas_call | solution.py:33
  45.7 3.6 %collective-permute-start.10 = (f32[3,16,640]{2,1,0:T(8,128)S(1)}, f32[3,16,640]{2,1,0:T(8,128)S(1)}, u32[]{:S(2)}, u32[]{:S(2)}) collective-permute-start(f32[3,16,640]{2,1,0:T(8,128)S(1)} %get-tuple-element.97), channel_id=1, source_target_pairs={{1,0},{2,1},{3,2},{4,3},{5,4},{6,5},{7,6},{0,7},{9,8},{10,9},{11,1... | collective-permute-start | bytes 368648 | tf_op jit(solution)/shard_map/ppermute | solution.py:510
  49.4 1.3 %collective-permute-done.10.from_north = f32[3,16,640]{2,1,0:T(8,128)S(1)} collective-permute-done((f32[3,16,640]{2,1,0:T(8,128)S(1)}, f32[3,16,640]{2,1,0:T(8,128)S(1)}, u32[]{:S(2)}, u32[]{:S(2)}) %collective-permute-start.10) | collective-permute-done | bytes 122912 | tf_op jit(solution)/shard_map/ppermute | solution.py:510
  51.2 1.0 %shard_map.82 = (f32[2,16,256]{2,1,0:T(8,128)S(1)}, f32[2,16,256]{2,1,0:T(8,128)S(1)}, f32[2,16,256]{2,1,0:T(8,128)S(1)}, f32[16,16,640]{2,1,0:T(8,128)S(1)}, f3...) custom-call(f32[8,16,640]{2,1,0:T(8,128)S(1)} %get-tuple-element.96.w_own.w, ...), custom_call_target="tpu_custom_call" | custom-call | flops 1000000 | bytes 1000000 | tf_op jit(solution)/shard_map/pallas_call | solution.py:33
  52.3 3.7 %collective-permute-start.12 = (f32[2,16,256]{2,1,0:T(8,128)S(1)}, f32[2,16,256]{2,1,0:T(8,128)S(1)}, u32[]{:S(2)}, u32[]{:S(2)}) collective-permute-start(f32[2,16,256]{2,1,0:T(8,128)S(1)} %get-tuple-element.100), channel_id=1, source_target_pairs={{1,0},{2,1},{3,2},{4,3},{5,4},{6,5},{7,6},{0,7},{9,8},{10,9},{11,1... | collective-permute-start | bytes 98312 | tf_op jit(solution)/shard_map/ppermute | solution.py:510
  57.5 3.4 %collective-permute-start.14 = (f32[16,1152]{1,0:T(8,128)S(1)}, f32[16,1152]{1,0:T(8,128)S(1)}, u32[]{:S(2)}, u32[]{:S(2)}) collective-permute-start(f32[16,1152]{1,0:T(8,128)S(1)} %get-tuple-element.106), channel_id=1, source_target_pairs={{1,0},{2,1},{3,2},{4,3},{5,4},{6,5},{7,6},{0,7},{9,8},{10,9},{11,1... | collective-permute-start | bytes 221192 | tf_op jit(solution)/shard_map/ppermute | solution.py:510
  62.2 0.9 %shard_map.84 = (f32[16,8,512]{2,1,0:T(8,128)S(1)}, f32[32,128]{1,0:T(8,128)S(1)}) custom-call(f32[2,16,256]{2,1,0:T(8,128)S(1)} %get-tuple-element.105.e2, f32[16,1152]{1,0:T(8,128)S(1)} %collective-permute-done.14.from_north, f32[16,1152]{1,0:T(8,128)S(1)} %collective-permute-done.15.from_south, f32[6,16,256]{2,1,0:T(8,128)S(1)} %get-tuple-element.108.f2, ...), custom_call_target="tpu_custom_call" | custom-call | flops 1000000 | bytes 1000000 | tf_op jit(solution)/shard_map/pallas_call | solution.py:33
  63.2 13.3 %all_to_all.22 = f32[32,1,128]{2,1,0:T(1,128)S(1)} all-to-all(f32[32,1,128]{2,1,0:T(1,128)S(1)} %bitcast.16), channel_id=1, replica_groups=mesh['x'=4,'z'=16,'lat'=8] {'x','lat'}, dimensions={0} | all-to-all | bytes 32768 | tf_op jit(solution)/shard_map/all_to_all | solution.py:576
  77.1 4.1 %all-to-all-start.1 = ((f32[16,1,128]{2,1,0:T(1,128)}), f32[16,1,128]{2,1,0:T(1,128)S(1)}, u32[]{:S(2)}, u32[]{:S(2)}) async-start(f32[16,1,128]{2,1,0:T(1,128)} %bitcast.6), calls=%async_computation.1 | async-start | bytes 16384 | tf_op jit(solution)/shard_map/all_to_all | solution.py:577
  81.4 11.1 %all-to-all-done.1 = f32[16,1,128]{2,1,0:T(1,128)S(1)} async-done(((f32[16,1,128]{2,1,0:T(1,128)}), f32[16,1,128]{2,1,0:T(1,128)S(1)}, u32[]{:S(2)}, u32[]{:S(2)}) %all-to-all-start.1) | async-done | bytes 8224 | tf_op jit(solution)/shard_map/all_to_all | solution.py:577
  92.5 1.0 %shard_map.87 = (f32[16,8,512]{2,1,0:T(8,128)}, f32[16,8,512]{2,1,0:T(8,128)}, f32[16,8,512]{2,1,0:T(8,128)}) custom-call(f32[16,128]{1,0:T(8,128)S(1)} %bitcast.15, f32[16,8,512]{2,1,0:T(8,128)S(1)} %copy-done.1, f32[16,8,512]{2,1,0:T(8,128)S(1)} %get-tuple-element.115.p, f32[16,8,512]{2,1,0:T(8,128)S(1)} %get-tuple-element.116.w, ...), custom_call_target="tpu_custom_call" | custom-call | flops 1000000 | bytes 1000000 | tf_op jit(solution)/shard_map/pallas_call | solution.py:33
  (37 shorter events, 6.9 us)
Async XLA Ops:
  0.6 28.6 %copy-start.1 = (f32[16,8,512]{2,1,0:T(8,128)S(1)}, f32[16,8,512]{2,1,0:T(8,128)}, u32[]{:S(2)}) copy-start(f32[16,8,512]{2,1,0:T(8,128)} %x.1) | copy-start | bytes 786436
  0.6 28.6 %copy-start.2 = (f32[16,8,512]{2,1,0:T(8,128)S(1)}, f32[16,8,512]{2,1,0:T(8,128)}, u32[]{:S(2)}) copy-start(f32[16,8,512]{2,1,0:T(8,128)} %b_ref.3) | copy-start | bytes 786436
  0.7 28.6 %copy-start.3 = (f32[16,8,512]{2,1,0:T(8,128)S(1)}, f32[16,8,512]{2,1,0:T(8,128)}, u32[]{:S(2)}) copy-start(f32[16,8,512]{2,1,0:T(8,128)} %c_ref.3) | copy-start | bytes 786436
  2.9 18.3 %copy-start.4 = (f32[2,4,16]{2,1,0:T(4,128)S(1)}, f32[2,4,16]{2,1,0:T(4,128)}, u32[]{:S(2)}) copy-start(f32[2,4,16]{2,1,0:T(4,128)} %param.8) | copy-start | bytes 1540
  2.9 18.3 %collective-permute-start.2 = (f32[8,16,128]{2,1,0:T(8,128)}, f32[8,16,128]{2,1,0:T(8,128)S(1)}, u32[]{:S(2)}, u32[]{:S(2)}) collective-permute-start(f32[8,16,128]{2,1,0:T(8,128)} %get-tuple-element.69), channel_id=1, source_target_pairs={{8,0},{16,8},{24,16},{32,24},{40,32},{48,40},{56,48},{64,56},{72,6... | collective-permute-start | bytes 196616 | tf_op jit(solution)/shard_map/ppermute | solution.py:510
  17.1 8.5 %collective-permute-start.3 = (f32[8,16,128]{2,1,0:T(8,128)}, f32[8,16,128]{2,1,0:T(8,128)S(1)}, u32[]{:S(2)}, u32[]{:S(2)}) collective-permute-start(f32[8,16,128]{2,1,0:T(8,128)} %get-tuple-element.70), channel_id=1, source_target_pairs={{0,8},{8,16},{16,24},{24,32},{32,40},{40,48},{48,56},{56,64},{64,7... | collective-permute-start | bytes 196616 | tf_op jit(solution)/shard_map/ppermute | solution.py:509
  19.0 10.1 %collective-permute-start = (f32[4,3,16,512]{3,2,1,0:T(8,128)}, f32[4,3,16,512]{3,2,1,0:T(8,128)S(1)}, u32[]{:S(2)}, u32[]{:S(2)}) collective-permute-start(f32[4,3,16,512]{3,2,1,0:T(8,128)} %get-tuple-element.61), channel_id=1, source_target_pairs={{1,0},{2,1},{3,2},{4,3},{5,4},{6,5},{7,6},{0,7},{9,8},{10,9},{11,1... | collective-permute-start | bytes 1179656 | tf_op jit(solution)/shard_map/ppermute | solution.py:510
  20.0 9.2 %collective-permute-start.1 = (f32[4,3,16,512]{3,2,1,0:T(8,128)}, f32[4,3,16,512]{3,2,1,0:T(8,128)S(1)}, u32[]{:S(2)}, u32[]{:S(2)}) collective-permute-start(f32[4,3,16,512]{3,2,1,0:T(8,128)} %get-tuple-element.62), channel_id=1, source_target_pairs={{0,1},{1,2},{2,3},{3,4},{4,5},{5,6},{6,7},{7,0},{8,9},{9,10},{10,1... | collective-permute-start | bytes 1179656 | tf_op jit(solution)/shard_map/ppermute | solution.py:509
  25.8 5.6 %collective-permute-start.4 = (f32[4,3,16,128]{3,2,1,0:T(8,128)S(1)}, f32[4,3,16,128]{3,2,1,0:T(8,128)S(1)}, u32[]{:S(2)}, u32[]{:S(2)}) collective-permute-start(f32[4,3,16,128]{3,2,1,0:T(8,128)S(1)} %get-tuple-element.72), channel_id=1, source_target_pairs={{1,0},{2,1},{3,2},{4,3},{5,4},{6,5},{7,6},{0,7},{9,8},{10,9},{11,1... | collective-permute-start | bytes 294920 | tf_op jit(solution)/shard_map/ppermute | solution.py:510
  27.9 3.5 %collective-permute-start.5 = (f32[4,3,16,128]{3,2,1,0:T(8,128)S(1)}, f32[4,3,16,128]{3,2,1,0:T(8,128)S(1)}, u32[]{:S(2)}, u32[]{:S(2)}) collective-permute-start(f32[4,3,16,128]{3,2,1,0:T(8,128)S(1)} %get-tuple-element.73), channel_id=1, source_target_pairs={{0,1},{1,2},{2,3},{3,4},{4,5},{5,6},{6,7},{7,0},{8,9},{9,10},{10,1... | collective-permute-start | bytes 294920 | tf_op jit(solution)/shard_map/ppermute | solution.py:509
  29.2 2.2 %copy-start = (bf16[640,256]{1,0:T(8,128)(2,1)S(1)}, bf16[640,256]{1,0:T(8,128)(2,1)}, u32[]{:S(2)}) copy-start(bf16[640,256]{1,0:T(8,128)(2,1)} %constant.2.clone.blocks) | copy-start | bytes 983044
  34.8 4.1 %collective-permute-start.6 = (f32[6,16,256]{2,1,0:T(8,128)S(1)}, f32[6,16,256]{2,1,0:T(8,128)S(1)}, u32[]{:S(2)}, u32[]{:S(2)}) collective-permute-start(f32[6,16,256]{2,1,0:T(8,128)S(1)} %get-tuple-element.75), channel_id=1, source_target_pairs={{1,0},{2,1},{3,2},{4,3},{5,4},{6,5},{7,6},{0,7},{9,8},{10,9},{11,1... | collective-permute-start | bytes 294920 | tf_op jit(solution)/shard_map/ppermute | solution.py:510
  37.6 1.6 %collective-permute-start.7 = (f32[6,16,256]{2,1,0:T(8,128)S(1)}, f32[6,16,256]{2,1,0:T(8,128)S(1)}, u32[]{:S(2)}, u32[]{:S(2)}) collective-permute-start(f32[6,16,256]{2,1,0:T(8,128)S(1)} %get-tuple-element.76), channel_id=1, source_target_pairs={{0,1},{1,2},{2,3},{3,4},{4,5},{5,6},{6,7},{7,0},{8,9},{9,10},{10,1... | collective-permute-start | bytes 294920 | tf_op jit(solution)/shard_map/ppermute | solution.py:509
  39.4 4.6 %collective-permute-start.8 = (f32[16,1152]{1,0:T(8,128)S(1)}, f32[16,1152]{1,0:T(8,128)S(1)}, u32[]{:S(2)}, u32[]{:S(2)}) collective-permute-start(f32[16,1152]{1,0:T(8,128)S(1)} %get-tuple-element.80), channel_id=1, source_target_pairs={{1,0},{2,1},{3,2},{4,3},{5,4},{6,5},{7,6},{0,7},{9,8},{10,9},{11,1... | collective-permute-start | bytes 221192 | tf_op jit(solution)/shard_map/ppermute | solution.py:510
  43.1 1.4 %collective-permute-start.9 = (f32[16,1152]{1,0:T(8,128)S(1)}, f32[16,1152]{1,0:T(8,128)S(1)}, u32[]{:S(2)}, u32[]{:S(2)}) collective-permute-start(f32[16,1152]{1,0:T(8,128)S(1)} %get-tuple-element.81), channel_id=1, source_target_pairs={{0,1},{1,2},{2,3},{3,4},{4,5},{5,6},{6,7},{7,0},{8,9},{9,10},{10,1... | collective-permute-start | bytes 221192 | tf_op jit(solution)/shard_map/ppermute | solution.py:509
  45.7 4.9 %collective-permute-start.10 = (f32[3,16,640]{2,1,0:T(8,128)S(1)}, f32[3,16,640]{2,1,0:T(8,128)S(1)}, u32[]{:S(2)}, u32[]{:S(2)}) collective-permute-start(f32[3,16,640]{2,1,0:T(8,128)S(1)} %get-tuple-element.97), channel_id=1, source_target_pairs={{1,0},{2,1},{3,2},{4,3},{5,4},{6,5},{7,6},{0,7},{9,8},{10,9},{11,1... | collective-permute-start | bytes 368648 | tf_op jit(solution)/shard_map/ppermute | solution.py:510
  49.4 1.9 %collective-permute-start.11 = (f32[3,16,640]{2,1,0:T(8,128)S(1)}, f32[3,16,640]{2,1,0:T(8,128)S(1)}, u32[]{:S(2)}, u32[]{:S(2)}) collective-permute-start(f32[3,16,640]{2,1,0:T(8,128)S(1)} %get-tuple-element.98), channel_id=1, source_target_pairs={{0,1},{1,2},{2,3},{3,4},{4,5},{5,6},{6,7},{7,0},{8,9},{9,10},{10,1... | collective-permute-start | bytes 368648 | tf_op jit(solution)/shard_map/ppermute | solution.py:509
  52.3 4.5 %collective-permute-start.12 = (f32[2,16,256]{2,1,0:T(8,128)S(1)}, f32[2,16,256]{2,1,0:T(8,128)S(1)}, u32[]{:S(2)}, u32[]{:S(2)}) collective-permute-start(f32[2,16,256]{2,1,0:T(8,128)S(1)} %get-tuple-element.100), channel_id=1, source_target_pairs={{1,0},{2,1},{3,2},{4,3},{5,4},{6,5},{7,6},{0,7},{9,8},{10,9},{11,1... | collective-permute-start | bytes 98312 | tf_op jit(solution)/shard_map/ppermute | solution.py:510
  55.9 1.2 %collective-permute-start.13 = (f32[2,16,256]{2,1,0:T(8,128)S(1)}, f32[2,16,256]{2,1,0:T(8,128)S(1)}, u32[]{:S(2)}, u32[]{:S(2)}) collective-permute-start(f32[2,16,256]{2,1,0:T(8,128)S(1)} %get-tuple-element.101), channel_id=1, source_target_pairs={{0,1},{1,2},{2,3},{3,4},{4,5},{5,6},{6,7},{7,0},{8,9},{9,10},{10,1... | collective-permute-start | bytes 98312 | tf_op jit(solution)/shard_map/ppermute | solution.py:509
  57.5 4.3 %collective-permute-start.14 = (f32[16,1152]{1,0:T(8,128)S(1)}, f32[16,1152]{1,0:T(8,128)S(1)}, u32[]{:S(2)}, u32[]{:S(2)}) collective-permute-start(f32[16,1152]{1,0:T(8,128)S(1)} %get-tuple-element.106), channel_id=1, source_target_pairs={{1,0},{2,1},{3,2},{4,3},{5,4},{6,5},{7,6},{0,7},{9,8},{10,9},{11,1... | collective-permute-start | bytes 221192 | tf_op jit(solution)/shard_map/ppermute | solution.py:510
  60.8 1.4 %collective-permute-start.15 = (f32[16,1152]{1,0:T(8,128)S(1)}, f32[16,1152]{1,0:T(8,128)S(1)}, u32[]{:S(2)}, u32[]{:S(2)}) collective-permute-start(f32[16,1152]{1,0:T(8,128)S(1)} %get-tuple-element.107), channel_id=1, source_target_pairs={{0,1},{1,2},{2,3},{3,4},{4,5},{5,6},{6,7},{7,0},{8,9},{9,10},{10,1... | collective-permute-start | bytes 221192 | tf_op jit(solution)/shard_map/ppermute | solution.py:509
  77.1 15.4 %all-to-all-start.1 = ((f32[16,1,128]{2,1,0:T(1,128)}), f32[16,1,128]{2,1,0:T(1,128)S(1)}, u32[]{:S(2)}, u32[]{:S(2)}) async-start(f32[16,1,128]{2,1,0:T(1,128)} %bitcast.6), calls=%async_computation.1 | async-start | bytes 16384 | tf_op jit(solution)/shard_map/all_to_all | solution.py:577

commit v5 on v4

--- a/solution.py
+++ b/solution.py
@@ -17,6 +17,7 @@
 EXT = ROWS + 2 * RIM
 MID = EXT // 2
 SEND = 3
+PLANES = 2 * RIM + SEND
 NEAR = 6
 COLS = 256
 OWN_COLS = OWN // 4
@@ -42,11 +43,8 @@
 
 
 def loop(first, end, body):
-    def step(i, carry):
+    for i in range(first, end):
         body(i)
-        return carry
-
-    lax.fori_loop(first, end, step, 0, unroll=True)
 
 
 def lane_ids():
@@ -97,6 +95,21 @@
         left = left - part.astype(F32)
         total = total + lax.dot_general(part, blocks[...], (((1,), (side,)), ((), ())), preferred_element_type=F32)
     return total
+
+
+def put_planes(j, rows, north_ref, south_ref):
+    count = RIM if j else SEND
+    first = (j - 1) * RIM if j else 2 * RIM
+    south_ref[first:first + count] = rows(0, count)
+    north_ref[first:first + count] = rows(ROWS - count, ROWS)
+
+
+def outer_planes(from_north, from_south):
+    for r in range(RIM):
+        b = from_south[2 * RIM + r - 1] if r >= RIM - SEND else None
+        yield r, b, from_south[r], from_south[RIM + r]
+        b = from_north[2 * RIM + r] if r < SEND else None
+        yield RIM + ROWS + r, b, from_north[r], from_north[RIM + r]
 
 
 def pack_kernel(
@@ -112,8 +125,7 @@
         field = jnp.swapaxes(held[j], 0, 1)
         turned[j, :, :, :128] = field[:, :, :128]
         turned[j, :, :, 128:] = field[:, :, OWN - 128:]
-        south_ref[:, j] = field[:RIM]
-        north_ref[:, j] = field[ROWS - RIM:]
+        put_planes(j, lambda first, end: field[first:end], north_ref, south_ref)
     results = ((north_ref, to_north), (south_ref, to_south), (east_ref, to_east), (west_ref, to_west))
     copies = [pltpu.make_async_copy(a, b, moved.at[3 + j]) for j, (a, b) in enumerate(results)]
     copies[0].start()
@@ -138,8 +150,8 @@
             if j > 0:
                 east, west = next_lane(east, DEEP), prev_lane(west, DEEP)
             rim_ref[r, j] = jnp.where(lane < DEEP, east, jnp.where(lane >= 128 - DEEP, west, 0.0))
-    south_ref[...] = rim_ref[:RIM]
-    north_ref[...] = rim_ref[ROWS - RIM:]
+    for j in range(3):
+        put_planes(j, lambda first, end: rim_ref[first:end, j], north_ref, south_ref)
 
 
 def restrict(m, f, e0, f1, e1, winv1, east, north, upper, even):
@@ -195,14 +207,12 @@
         i = r + RIM
         react[i], upper[i], lon_weight[i], lat_weight[i] = weigh(sets, share[r], OWN)
 
-    def outer(i, rows, r):
-        b[i] = rows[r, 0]
-        x[i] = rows[r, 1]
-        react[i], upper[i], lon_weight[i], lat_weight[i] = weigh(sets, rows[r, 2], OWN)
-
     loop(0, ROWS, own)
-    loop(0, RIM, lambda r: outer(r, from_south, r))
-    loop(0, RIM, lambda r: outer(r + RIM + ROWS, from_north, r))
+    for i, b_row, x_row, c_row in outer_planes(from_north, from_south):
+        if b_row is not None:
+            b[i] = b_row
+        x[i] = x_row
+        react[i], upper[i], lon_weight[i], lat_weight[i] = weigh(sets, c_row, OWN)
 
 
 class Joined:
@@ -226,16 +236,13 @@
     south_end = lat == 0
     north_end = lat == lax.axis_size("lat") - 1
 
-    def take(i, rows, r):
-        b_rims[i] = rows[r, 0]
-        x_rims[i] = rows[r, 1]
-        react_rims[i], upper_rims[i], lon_rims[i], lat_rims[i] = weigh(sets, rows[r, 2], 128)
-
-    for r in range(RIM):
-        take(r, rim_south, r)
-        take(r + RIM + ROWS, rim_north, r)
-    for r in range(ROWS):
-        take(r + RIM, rim, r)
+    rows = list(outer_planes(rim_north, rim_south))
+    rows += [(RIM + r, rim[r, 0], rim[r, 1], rim[r, 2]) for r in range(ROWS)]
+    for i, b_row, x_row, c_row in rows:
+        if b_row is not None:
+            b_rims[i] = b_row
+        x_rims[i] = x_row
+        react_rims[i], upper_rims[i], lon_rims[i], lat_rims[i] = weigh(sets, c_row, 128)
 
     def face_east(i):
         here = lon_weight[i]
@@ -514,9 +521,9 @@
     blocks = blocks_matrix()
     to_north, to_south, to_east, to_west = call(
         pack_kernel,
-        [(RIM, 3, LEV, OWN)] * 2 + [(ROWS, LEV, 128)] * 2,
+        [(PLANES, LEV, OWN)] * 2 + [(ROWS, LEV, 128)] * 2,
         fields,
-        [(3, LEV, ROWS, OWN), (3, ROWS, LEV, 256)] + [(RIM, 3, LEV, OWN)] * 2 + [(ROWS, LEV, 128)] * 2,
+        [(3, LEV, ROWS, OWN), (3, ROWS, LEV, 256)] + [(PLANES, LEV, OWN)] * 2 + [(ROWS, LEV, 128)] * 2,
         specs=[HBM] * 3,
         copies=7,
         out_spec=HBM,
@@ -524,7 +531,7 @@
     lat_rows = trade(to_north, to_south, "lat")
     lon_rims = trade(to_east, to_west, lon)
     rim, to_north, to_south = call(
-        rim_kernel, [(ROWS, 3, LEV, 128), (RIM, 3, LEV, 128), (RIM, 3, LEV, 128)], lon_rims
+        rim_kernel, [(ROWS, 3, LEV, 128), (PLANES, LEV, 128), (PLANES, LEV, 128)], lon_rims
     )
     lat_rims = trade(to_north, to_south, "lat")
     sea, land = coefficient_sets[0], coefficient_sets[1]

time: 93.7 us -> 93.4 us (level)
  no operation moved by 1% of the time
where the time goes in v5:
time: 93.4 us; the launch traced here: 93.1 us
  starting transfers between devices  42.6 us (46%)
  waiting for transfers between devices  24.7 us (26%)
  blocking collectives  13.3 us (14%)
  Pallas kernels  11.7 us (13%)
    ppermute x8, starting transfers between devices, trade(): return (lax.ppermute(to_last, axis, [(j, i) for i, j in up]), from_last)  34.4 us
    all_to_all x1, blocking collectives, shards(): lax.all_to_all(dots, ('x', 'lat'), 0, 0, tiled=True)  13.3 us
    pallas_call x12, Pallas kernels, call(): pl.pallas_call(body, out_shape=[jax.ShapeDtypeStruct(o, F32) for o in out...  11.7 us
    all_to_all x1, waiting for transfers between devices, shards(): dots = lax.all_to_all(dots, 'z', 0, 0, tiled=True)  11.1 us
    ppermute x8, waiting for transfers between devices, trade(): return (lax.ppermute(to_last, axis, [(j, i) for i, j in up]), from_last)  6.89 us
    ppermute x8, waiting for transfers between devices, trade(): from_last = lax.ppermute(to_next, axis, up)  6.69 us
    ppermute x8, starting transfers between devices, trade(): from_last = lax.ppermute(to_next, axis, up)  4.35 us
    all_to_all x1, starting transfers between devices, shards(): dots = lax.all_to_all(dots, 'z', 0, 0, tiled=True)  3.88 us
  transfers between devices with their start and end apart: 17, of which 13 were waited for; matrix products, arithmetic and copies ran while one was open for 0% of the time, Pallas kernels for 1%

profile of v5, /device:TPU:1, one launch (start us, length us, event | category | flops | bytes accessed | tf_op | source)
XLA Modules:
  0.0 93.1 jit_solution(4259862747865457865)
XLA Ops:
  0.7 2.2 %shard_map.76 = (f32[11,16,512]{2,1,0:T(8,128)}, f32[11,16,512]{2,1,0:T(8,128)}, f32[8,16,128]{2,1,0:T(8,128)}, f32[8,16,128]{2,1,0:T(8,128)}) custom-call(f32[16,8,512]{2,1,0:T(8,128)} %b_ref.3, f32[16,8,512]{2,1,0:T(8,128)} %x.1, f32[16,8,512]{2,1,0:T(8,128)} %c_ref.3), custom_call_target="tpu_custom_call" | custom-call | flops 1000000 | bytes 1000000 | tf_op jit(solution)/shard_map/pallas_call | solution.py:34
  2.9 14.1 %collective-permute-start.2 = (f32[8,16,128]{2,1,0:T(8,128)}, f32[8,16,128]{2,1,0:T(8,128)S(1)}, u32[]{:S(2)}, u32[]{:S(2)}) collective-permute-start(f32[8,16,128]{2,1,0:T(8,128)} %get-tuple-element.69), channel_id=1, source_target_pairs={{8,0},{16,8},{24,16},{32,24},{40,32},{48,40},{56,48},{64,56},{72,6... | collective-permute-start | bytes 196616 | tf_op jit(solution)/shard_map/ppermute | solution.py:517
  17.1 1.9 %collective-permute-start.3 = (f32[8,16,128]{2,1,0:T(8,128)}, f32[8,16,128]{2,1,0:T(8,128)S(1)}, u32[]{:S(2)}, u32[]{:S(2)}) collective-permute-start(f32[8,16,128]{2,1,0:T(8,128)} %get-tuple-element.70), channel_id=1, source_target_pairs={{0,8},{8,16},{16,24},{24,32},{32,40},{40,48},{48,56},{56,64},{64,7... | collective-permute-start | bytes 196616 | tf_op jit(solution)/shard_map/ppermute | solution.py:516
  19.0 1.0 %collective-permute-start = (f32[11,16,512]{2,1,0:T(8,128)}, f32[11,16,512]{2,1,0:T(8,128)S(1)}, u32[]{:S(2)}, u32[]{:S(2)}) collective-permute-start(f32[11,16,512]{2,1,0:T(8,128)} %get-tuple-element.61), channel_id=1, source_target_pairs={{1,0},{2,1},{3,2},{4,3},{5,4},{6,5},{7,6},{0,7},{9,8},{10,9},{11,1... | collective-permute-start | bytes 1081352 | tf_op jit(solution)/shard_map/ppermute | solution.py:517
  19.9 1.2 %collective-permute-start.1 = (f32[11,16,512]{2,1,0:T(8,128)}, f32[11,16,512]{2,1,0:T(8,128)S(1)}, u32[]{:S(2)}, u32[]{:S(2)}) collective-permute-start(f32[11,16,512]{2,1,0:T(8,128)} %get-tuple-element.62), channel_id=1, source_target_pairs={{0,1},{1,2},{2,3},{3,4},{4,5},{5,6},{6,7},{7,0},{8,9},{9,10},{10,1... | collective-permute-start | bytes 1081352 | tf_op jit(solution)/shard_map/ppermute | solution.py:516
  21.2 4.4 %collective-permute-done.3.from_west = f32[8,16,128]{2,1,0:T(8,128)S(1)} collective-permute-done((f32[8,16,128]{2,1,0:T(8,128)}, f32[8,16,128]{2,1,0:T(8,128)S(1)}, u32[]{:S(2)}, u32[]{:S(2)}) %collective-permute-start.3) | collective-permute-done | bytes 65568 | tf_op jit(solution)/shard_map/ppermute | solution.py:516
  25.8 2.1 %collective-permute-start.4 = (f32[11,16,128]{2,1,0:T(8,128)S(1)}, f32[11,16,128]{2,1,0:T(8,128)S(1)}, u32[]{:S(2)}, u32[]{:S(2)}) collective-permute-start(f32[11,16,128]{2,1,0:T(8,128)S(1)} %get-tuple-element.72), channel_id=1, source_target_pairs={{1,0},{2,1},{3,2},{4,3},{5,4},{6,5},{7,6},{0,7},{9,8},{10,9},{11,1... | collective-permute-start | bytes 270344 | tf_op jit(solution)/shard_map/ppermute | solution.py:517
  27.9 1.2 %collective-permute-start.5 = (f32[11,16,128]{2,1,0:T(8,128)S(1)}, f32[11,16,128]{2,1,0:T(8,128)S(1)}, u32[]{:S(2)}, u32[]{:S(2)}) collective-permute-start(f32[11,16,128]{2,1,0:T(8,128)S(1)} %get-tuple-element.73), channel_id=1, source_target_pairs={{0,1},{1,2},{2,3},{3,4},{4,5},{5,6},{6,7},{7,0},{8,9},{9,10},{10,1... | collective-permute-start | bytes 270344 | tf_op jit(solution)/shard_map/ppermute | solution.py:516
  29.7 1.6 %collective-permute-done.4.rim_north = f32[11,16,128]{2,1,0:T(8,128)S(1)} collective-permute-done((f32[11,16,128]{2,1,0:T(8,128)S(1)}, f32[11,16,128]{2,1,0:T(8,128)S(1)}, u32[]{:S(2)}, u32[]{:S(2)}) %collective-permute-start.4) | collective-permute-done | bytes 90144 | tf_op jit(solution)/shard_map/ppermute | solution.py:517
  31.3 3.4 %shard_map.79 = (f32[16,16,640]{2,1,0:T(8,128)S(1)}, f32[2,16,256]{2,1,0:T(8,128)S(1)}, f32[6,16,256]{2,1,0:T(8,128)S(1)}, f32[6,16,256]{2,1,0:T(8,128)S(1)}, f3...) custom-call(f32[16,16,512]{2,1,0:T(8,128)S(1)} %get-tuple-element.63, ...), custom_call_target="tpu_custom_call" | custom-call | flops 1000000 | bytes 1000000 | tf_op jit(solution)/shard_map/pallas_call | solution.py:34
  34.7 2.8 %collective-permute-start.6 = (f32[6,16,256]{2,1,0:T(8,128)S(1)}, f32[6,16,256]{2,1,0:T(8,128)S(1)}, u32[]{:S(2)}, u32[]{:S(2)}) collective-permute-start(f32[6,16,256]{2,1,0:T(8,128)S(1)} %get-tuple-element.75), channel_id=1, source_target_pairs={{1,0},{2,1},{3,2},{4,3},{5,4},{6,5},{7,6},{0,7},{9,8},{10,9},{11,1... | collective-permute-start | bytes 294920 | tf_op jit(solution)/shard_map/ppermute | solution.py:517
  37.5 1.3 %collective-permute-done.6.from_north = f32[6,16,256]{2,1,0:T(8,128)S(1)} collective-permute-done((f32[6,16,256]{2,1,0:T(8,128)S(1)}, f32[6,16,256]{2,1,0:T(8,128)S(1)}, u32[]{:S(2)}, u32[]{:S(2)}) %collective-permute-start.6) | collective-permute-done | bytes 98336 | tf_op jit(solution)/shard_map/ppermute | solution.py:517
  39.3 3.6 %collective-permute-start.8 = (f32[16,1152]{1,0:T(8,128)S(1)}, f32[16,1152]{1,0:T(8,128)S(1)}, u32[]{:S(2)}, u32[]{:S(2)}) collective-permute-start(f32[16,1152]{1,0:T(8,128)S(1)} %get-tuple-element.80), channel_id=1, source_target_pairs={{1,0},{2,1},{3,2},{4,3},{5,4},{6,5},{7,6},{0,7},{9,8},{10,9},{11,1... | collective-permute-start | bytes 221192 | tf_op jit(solution)/shard_map/ppermute | solution.py:517
  44.4 1.3 %shard_map.81 = (f32[8,16,512]{2,1,0:T(8,128)S(1)}, f32[8,16,640]{2,1,0:T(8,128)S(1)}, f32[3,16,640]{2,1,0:T(8,128)S(1)}, f32[3,16,640]{2,1,0:T(8,128)S(1)}, f32...) custom-call(f32[2,16,256]{2,1,0:T(8,128)S(1)} %get-tuple-element.79.e2, ...), custom_call_target="tpu_custom_call" | custom-call | flops 1000000 | bytes 1000000 | tf_op jit(solution)/shard_map/pallas_call | solution.py:34
  45.6 3.6 %collective-permute-start.10 = (f32[3,16,640]{2,1,0:T(8,128)S(1)}, f32[3,16,640]{2,1,0:T(8,128)S(1)}, u32[]{:S(2)}, u32[]{:S(2)}) collective-permute-start(f32[3,16,640]{2,1,0:T(8,128)S(1)} %get-tuple-element.97), channel_id=1, source_target_pairs={{1,0},{2,1},{3,2},{4,3},{5,4},{6,5},{7,6},{0,7},{9,8},{10,9},{11,1... | collective-permute-start | bytes 368648 | tf_op jit(solution)/shard_map/ppermute | solution.py:517
  49.3 1.3 %collective-permute-done.10.from_north = f32[3,16,640]{2,1,0:T(8,128)S(1)} collective-permute-done((f32[3,16,640]{2,1,0:T(8,128)S(1)}, f32[3,16,640]{2,1,0:T(8,128)S(1)}, u32[]{:S(2)}, u32[]{:S(2)}) %collective-permute-start.10) | collective-permute-done | bytes 122912 | tf_op jit(solution)/shard_map/ppermute | solution.py:517
  51.1 1.0 %shard_map.82 = (f32[2,16,256]{2,1,0:T(8,128)S(1)}, f32[2,16,256]{2,1,0:T(8,128)S(1)}, f32[2,16,256]{2,1,0:T(8,128)S(1)}, f32[16,16,640]{2,1,0:T(8,128)S(1)}, f3...) custom-call(f32[8,16,640]{2,1,0:T(8,128)S(1)} %get-tuple-element.96.w_own.w, ...), custom_call_target="tpu_custom_call" | custom-call | flops 1000000 | bytes 1000000 | tf_op jit(solution)/shard_map/pallas_call | solution.py:34
  52.2 3.7 %collective-permute-start.12 = (f32[2,16,256]{2,1,0:T(8,128)S(1)}, f32[2,16,256]{2,1,0:T(8,128)S(1)}, u32[]{:S(2)}, u32[]{:S(2)}) collective-permute-start(f32[2,16,256]{2,1,0:T(8,128)S(1)} %get-tuple-element.100), channel_id=1, source_target_pairs={{1,0},{2,1},{3,2},{4,3},{5,4},{6,5},{7,6},{0,7},{9,8},{10,9},{11,1... | collective-permute-start | bytes 98312 | tf_op jit(solution)/shard_map/ppermute | solution.py:517
  57.4 3.4 %collective-permute-start.14 = (f32[16,1152]{1,0:T(8,128)S(1)}, f32[16,1152]{1,0:T(8,128)S(1)}, u32[]{:S(2)}, u32[]{:S(2)}) collective-permute-start(f32[16,1152]{1,0:T(8,128)S(1)} %get-tuple-element.106), channel_id=1, source_target_pairs={{1,0},{2,1},{3,2},{4,3},{5,4},{6,5},{7,6},{0,7},{9,8},{10,9},{11,1... | collective-permute-start | bytes 221192 | tf_op jit(solution)/shard_map/ppermute | solution.py:517
  62.1 0.9 %shard_map.84 = (f32[16,8,512]{2,1,0:T(8,128)S(1)}, f32[32,128]{1,0:T(8,128)S(1)}) custom-call(f32[2,16,256]{2,1,0:T(8,128)S(1)} %get-tuple-element.105.e2, f32[16,1152]{1,0:T(8,128)S(1)} %collective-permute-done.14.from_north, f32[16,1152]{1,0:T(8,128)S(1)} %collective-permute-done.15.from_south, f32[6,16,256]{2,1,0:T(8,128)S(1)} %get-tuple-element.108.f2, ...), custom_call_target="tpu_custom_call" | custom-call | flops 1000000 | bytes 1000000 | tf_op jit(solution)/shard_map/pallas_call | solution.py:34
  63.1 13.3 %all_to_all.22 = f32[32,1,128]{2,1,0:T(1,128)S(1)} all-to-all(f32[32,1,128]{2,1,0:T(1,128)S(1)} %bitcast.16), channel_id=1, replica_groups=mesh['x'=4,'z'=16,'lat'=8] {'x','lat'}, dimensions={0} | all-to-all | bytes 32768 | tf_op jit(solution)/shard_map/all_to_all | solution.py:583
  77.0 3.9 %all-to-all-start.1 = ((f32[16,1,128]{2,1,0:T(1,128)}), f32[16,1,128]{2,1,0:T(1,128)S(1)}, u32[]{:S(2)}, u32[]{:S(2)}) async-start(f32[16,1,128]{2,1,0:T(1,128)} %bitcast.6), calls=%async_computation.1 | async-start | bytes 16384 | tf_op jit(solution)/shard_map/all_to_all | solution.py:584
  81.0 11.1 %all-to-all-done.1 = f32[16,1,128]{2,1,0:T(1,128)S(1)} async-done(((f32[16,1,128]{2,1,0:T(1,128)}), f32[16,1,128]{2,1,0:T(1,128)S(1)}, u32[]{:S(2)}, u32[]{:S(2)}) %all-to-all-start.1) | async-done | bytes 8224 | tf_op jit(solution)/shard_map/all_to_all | solution.py:584
  92.1 1.0 %shard_map.87 = (f32[16,8,512]{2,1,0:T(8,128)}, f32[16,8,512]{2,1,0:T(8,128)}, f32[16,8,512]{2,1,0:T(8,128)}) custom-call(f32[16,128]{1,0:T(8,128)S(1)} %bitcast.15, f32[16,8,512]{2,1,0:T(8,128)S(1)} %copy-done.1, f32[16,8,512]{2,1,0:T(8,128)S(1)} %get-tuple-element.115.p, f32[16,8,512]{2,1,0:T(8,128)S(1)} %get-tuple-element.116.w, ...), custom_call_target="tpu_custom_call" | custom-call | flops 1000000 | bytes 1000000 | tf_op jit(solution)/shard_map/pallas_call | solution.py:34
  (37 shorter events, 6.9 us)
Async XLA Ops:
  0.6 28.6 %copy-start.1 = (f32[16,8,512]{2,1,0:T(8,128)S(1)}, f32[16,8,512]{2,1,0:T(8,128)}, u32[]{:S(2)}) copy-start(f32[16,8,512]{2,1,0:T(8,128)} %x.1) | copy-start | bytes 786436
  0.6 28.6 %copy-start.2 = (f32[16,8,512]{2,1,0:T(8,128)S(1)}, f32[16,8,512]{2,1,0:T(8,128)}, u32[]{:S(2)}) copy-start(f32[16,8,512]{2,1,0:T(8,128)} %b_ref.3) | copy-start | bytes 786436
  0.7 28.6 %copy-start.3 = (f32[16,8,512]{2,1,0:T(8,128)S(1)}, f32[16,8,512]{2,1,0:T(8,128)}, u32[]{:S(2)}) copy-start(f32[16,8,512]{2,1,0:T(8,128)} %c_ref.3) | copy-start | bytes 786436
  2.9 18.3 %copy-start.4 = (f32[2,4,16]{2,1,0:T(4,128)S(1)}, f32[2,4,16]{2,1,0:T(4,128)}, u32[]{:S(2)}) copy-start(f32[2,4,16]{2,1,0:T(4,128)} %param.8) | copy-start | bytes 1540
  2.9 18.3 %collective-permute-start.2 = (f32[8,16,128]{2,1,0:T(8,128)}, f32[8,16,128]{2,1,0:T(8,128)S(1)}, u32[]{:S(2)}, u32[]{:S(2)}) collective-permute-start(f32[8,16,128]{2,1,0:T(8,128)} %get-tuple-element.69), channel_id=1, source_target_pairs={{8,0},{16,8},{24,16},{32,24},{40,32},{48,40},{56,48},{64,56},{72,6... | collective-permute-start | bytes 196616 | tf_op jit(solution)/shard_map/ppermute | solution.py:517
  17.1 8.5 %collective-permute-start.3 = (f32[8,16,128]{2,1,0:T(8,128)}, f32[8,16,128]{2,1,0:T(8,128)S(1)}, u32[]{:S(2)}, u32[]{:S(2)}) collective-permute-start(f32[8,16,128]{2,1,0:T(8,128)} %get-tuple-element.70), channel_id=1, source_target_pairs={{0,8},{8,16},{16,24},{24,32},{32,40},{40,48},{48,56},{56,64},{64,7... | collective-permute-start | bytes 196616 | tf_op jit(solution)/shard_map/ppermute | solution.py:516
  19.0 10.1 %collective-permute-start = (f32[11,16,512]{2,1,0:T(8,128)}, f32[11,16,512]{2,1,0:T(8,128)S(1)}, u32[]{:S(2)}, u32[]{:S(2)}) collective-permute-start(f32[11,16,512]{2,1,0:T(8,128)} %get-tuple-element.61), channel_id=1, source_target_pairs={{1,0},{2,1},{3,2},{4,3},{5,4},{6,5},{7,6},{0,7},{9,8},{10,9},{11,1... | collective-permute-start | bytes 1081352 | tf_op jit(solution)/shard_map/ppermute | solution.py:517
  19.9 9.2 %collective-permute-start.1 = (f32[11,16,512]{2,1,0:T(8,128)}, f32[11,16,512]{2,1,0:T(8,128)S(1)}, u32[]{:S(2)}, u32[]{:S(2)}) collective-permute-start(f32[11,16,512]{2,1,0:T(8,128)} %get-tuple-element.62), channel_id=1, source_target_pairs={{0,1},{1,2},{2,3},{3,4},{4,5},{5,6},{6,7},{7,0},{8,9},{9,10},{10,1... | collective-permute-start | bytes 1081352 | tf_op jit(solution)/shard_map/ppermute | solution.py:516
  25.8 5.5 %collective-permute-start.4 = (f32[11,16,128]{2,1,0:T(8,128)S(1)}, f32[11,16,128]{2,1,0:T(8,128)S(1)}, u32[]{:S(2)}, u32[]{:S(2)}) collective-permute-start(f32[11,16,128]{2,1,0:T(8,128)S(1)} %get-tuple-element.72), channel_id=1, source_target_pairs={{1,0},{2,1},{3,2},{4,3},{5,4},{6,5},{7,6},{0,7},{9,8},{10,9},{11,1... | collective-permute-start | bytes 270344 | tf_op jit(solution)/shard_map/ppermute | solution.py:517
  27.9 3.4 %collective-permute-start.5 = (f32[11,16,128]{2,1,0:T(8,128)S(1)}, f32[11,16,128]{2,1,0:T(8,128)S(1)}, u32[]{:S(2)}, u32[]{:S(2)}) collective-permute-start(f32[11,16,128]{2,1,0:T(8,128)S(1)} %get-tuple-element.73), channel_id=1, source_target_pairs={{0,1},{1,2},{2,3},{3,4},{4,5},{5,6},{6,7},{7,0},{8,9},{9,10},{10,1... | collective-permute-start | bytes 270344 | tf_op jit(solution)/shard_map/ppermute | solution.py:516
  29.2 2.1 %copy-start = (bf16[640,256]{1,0:T(8,128)(2,1)S(1)}, bf16[640,256]{1,0:T(8,128)(2,1)}, u32[]{:S(2)}) copy-start(bf16[640,256]{1,0:T(8,128)(2,1)} %constant.2.clone.blocks) | copy-start | bytes 983044
  34.7 4.1 %collective-permute-start.6 = (f32[6,16,256]{2,1,0:T(8,128)S(1)}, f32[6,16,256]{2,1,0:T(8,128)S(1)}, u32[]{:S(2)}, u32[]{:S(2)}) collective-permute-start(f32[6,16,256]{2,1,0:T(8,128)S(1)} %get-tuple-element.75), channel_id=1, source_target_pairs={{1,0},{2,1},{3,2},{4,3},{5,4},{6,5},{7,6},{0,7},{9,8},{10,9},{11,1... | collective-permute-start | bytes 294920 | tf_op jit(solution)/shard_map/ppermute | solution.py:517
  37.5 1.6 %collective-permute-start.7 = (f32[6,16,256]{2,1,0:T(8,128)S(1)}, f32[6,16,256]{2,1,0:T(8,128)S(1)}, u32[]{:S(2)}, u32[]{:S(2)}) collective-permute-start(f32[6,16,256]{2,1,0:T(8,128)S(1)} %get-tuple-element.76), channel_id=1, source_target_pairs={{0,1},{1,2},{2,3},{3,4},{4,5},{5,6},{6,7},{7,0},{8,9},{9,10},{10,1... | collective-permute-start | bytes 294920 | tf_op jit(solution)/shard_map/ppermute | solution.py:516
  39.3 4.6 %collective-permute-start.8 = (f32[16,1152]{1,0:T(8,128)S(1)}, f32[16,1152]{1,0:T(8,128)S(1)}, u32[]{:S(2)}, u32[]{:S(2)}) collective-permute-start(f32[16,1152]{1,0:T(8,128)S(1)} %get-tuple-element.80), channel_id=1, source_target_pairs={{1,0},{2,1},{3,2},{4,3},{5,4},{6,5},{7,6},{0,7},{9,8},{10,9},{11,1... | collective-permute-start | bytes 221192 | tf_op jit(solution)/shard_map/ppermute | solution.py:517
  43.0 1.4 %collective-permute-start.9 = (f32[16,1152]{1,0:T(8,128)S(1)}, f32[16,1152]{1,0:T(8,128)S(1)}, u32[]{:S(2)}, u32[]{:S(2)}) collective-permute-start(f32[16,1152]{1,0:T(8,128)S(1)} %get-tuple-element.81), channel_id=1, source_target_pairs={{0,1},{1,2},{2,3},{3,4},{4,5},{5,6},{6,7},{7,0},{8,9},{9,10},{10,1... | collective-permute-start | bytes 221192 | tf_op jit(solution)/shard_map/ppermute | solution.py:516
  45.6 4.9 %collective-permute-start.10 = (f32[3,16,640]{2,1,0:T(8,128)S(1)}, f32[3,16,640]{2,1,0:T(8,128)S(1)}, u32[]{:S(2)}, u32[]{:S(2)}) collective-permute-start(f32[3,16,640]{2,1,0:T(8,128)S(1)} %get-tuple-element.97), channel_id=1, source_target_pairs={{1,0},{2,1},{3,2},{4,3},{5,4},{6,5},{7,6},{0,7},{9,8},{10,9},{11,1... | collective-permute-start | bytes 368648 | tf_op jit(solution)/shard_map/ppermute | solution.py:517
  49.3 1.9 %collective-permute-start.11 = (f32[3,16,640]{2,1,0:T(8,128)S(1)}, f32[3,16,640]{2,1,0:T(8,128)S(1)}, u32[]{:S(2)}, u32[]{:S(2)}) collective-permute-start(f32[3,16,640]{2,1,0:T(8,128)S(1)} %get-tuple-element.98), channel_id=1, source_target_pairs={{0,1},{1,2},{2,3},{3,4},{4,5},{5,6},{6,7},{7,0},{8,9},{9,10},{10,1... | collective-permute-start | bytes 368648 | tf_op jit(solution)/shard_map/ppermute | solution.py:516
  52.2 4.5 %collective-permute-start.12 = (f32[2,16,256]{2,1,0:T(8,128)S(1)}, f32[2,16,256]{2,1,0:T(8,128)S(1)}, u32[]{:S(2)}, u32[]{:S(2)}) collective-permute-start(f32[2,16,256]{2,1,0:T(8,128)S(1)} %get-tuple-element.100), channel_id=1, source_target_pairs={{1,0},{2,1},{3,2},{4,3},{5,4},{6,5},{7,6},{0,7},{9,8},{10,9},{11,1... | collective-permute-start | bytes 98312 | tf_op jit(solution)/shard_map/ppermute | solution.py:517
  55.8 1.2 %collective-permute-start.13 = (f32[2,16,256]{2,1,0:T(8,128)S(1)}, f32[2,16,256]{2,1,0:T(8,128)S(1)}, u32[]{:S(2)}, u32[]{:S(2)}) collective-permute-start(f32[2,16,256]{2,1,0:T(8,128)S(1)} %get-tuple-element.101), channel_id=1, source_target_pairs={{0,1},{1,2},{2,3},{3,4},{4,5},{5,6},{6,7},{7,0},{8,9},{9,10},{10,1... | collective-permute-start | bytes 98312 | tf_op jit(solution)/shard_map/ppermute | solution.py:516
  57.4 4.3 %collective-permute-start.14 = (f32[16,1152]{1,0:T(8,128)S(1)}, f32[16,1152]{1,0:T(8,128)S(1)}, u32[]{:S(2)}, u32[]{:S(2)}) collective-permute-start(f32[16,1152]{1,0:T(8,128)S(1)} %get-tuple-element.106), channel_id=1, source_target_pairs={{1,0},{2,1},{3,2},{4,3},{5,4},{6,5},{7,6},{0,7},{9,8},{10,9},{11,1... | collective-permute-start | bytes 221192 | tf_op jit(solution)/shard_map/ppermute | solution.py:517
  60.7 1.4 %collective-permute-start.15 = (f32[16,1152]{1,0:T(8,128)S(1)}, f32[16,1152]{1,0:T(8,128)S(1)}, u32[]{:S(2)}, u32[]{:S(2)}) collective-permute-start(f32[16,1152]{1,0:T(8,128)S(1)} %get-tuple-element.107), channel_id=1, source_target_pairs={{0,1},{1,2},{2,3},{3,4},{4,5},{5,6},{6,7},{7,0},{8,9},{9,10},{10,1... | collective-permute-start | bytes 221192 | tf_op jit(solution)/shard_map/ppermute | solution.py:516
  77.0 15.1 %all-to-all-start.1 = ((f32[16,1,128]{2,1,0:T(1,128)}), f32[16,1,128]{2,1,0:T(1,128)S(1)}, u32[]{:S(2)}, u32[]{:S(2)}) async-start(f32[16,1,128]{2,1,0:T(1,128)} %bitcast.6), calls=%async_computation.1 | async-start | bytes 16384 | tf_op jit(solution)/shard_map/all_to_all | solution.py:584

commit v6 on v4

--- a/solution.py
+++ b/solution.py
@@ -499,7 +499,7 @@
 
 def shards(right_side, initial_guess, land_mask, coefficient_sets):
     z_size, lat_size = lax.axis_size("z"), lax.axis_size("lat")
-    lines = (lax.axis_size("x") * lat_size, 128)
+    lines = (z_size, 128)
     lon = ("x", "z")
     sizes = {lon: lax.axis_size("x") * z_size, "lat": lat_size}
 
@@ -573,8 +573,8 @@
         [e2, *trade(edge_north, edge_south, "lat"), f2_near, weights2, blocks, w_own, e0, f1, e1] + grids + [dots],
         [near, mid, fine, fine, fine],
     )
-    (dots,) = call(total_kernel, [(z_size, 128)], [lax.all_to_all(dots, ("x", "lat"), 0, 0, tiled=True)])
-    dots = lax.all_to_all(dots, "z", 0, 0, tiled=True)
+    (dots,) = call(total_kernel, [(lax.axis_size("x") * lat_size, 128)], [lax.all_to_all(dots, "z", 0, 0, tiled=True)])
+    dots = lax.all_to_all(dots, ("x", "lat"), 0, 0, tiled=True)
     return tuple(call(finish_kernel, [(LEV, ROWS, OWN)] * 3, [dots, initial_guess, p, w, q, s]))
 
 

time: 93.7 us -> 95.2 us (1.016)
  starting transfers between devices: 42.8 us -> 48.1 us
  waiting for transfers between devices: 24.7 us -> 20.4 us
    all_to_all x1, starting transfers between devices: 4.14 us -> 9.4 us  [shards(): dots = lax.all_to_all(dots, ('x', 'lat'), 0, 0, tiled=True)]
    all_to_all x1, waiting for transfers between devices: 11.1 us -> 6.72 us  [shards(): dots = lax.all_to_all(dots, ('x', 'lat'), 0, 0, tiled=True)]
where the time goes in v6:
time: 95.2 us; the launch traced here: 94.9 us
  starting transfers between devices  48.1 us (51%)
  waiting for transfers between devices  20.4 us (21%)
  blocking collectives  13.8 us (14%)
  Pallas kernels  11.7 us (12%)
    ppermute x8, starting transfers between devices, trade(): return (lax.ppermute(to_last, axis, [(j, i) for i, j in up]), from_last)  34.4 us
    all_to_all x1, blocking collectives, shards(): lax.all_to_all(dots, 'z', 0, 0, tiled=True)  13.8 us
    pallas_call x12, Pallas kernels, call(): pl.pallas_call(body, out_shape=[jax.ShapeDtypeStruct(o, F32) for o in out...  11.7 us
    all_to_all x1, starting transfers between devices, shards(): dots = lax.all_to_all(dots, ('x', 'lat'), 0, 0, tiled=True)  9.4 us
    ppermute x8, waiting for transfers between devices, trade(): return (lax.ppermute(to_last, axis, [(j, i) for i, j in up]), from_last)  6.98 us
    all_to_all x1, waiting for transfers between devices, shards(): dots = lax.all_to_all(dots, ('x', 'lat'), 0, 0, tiled=True)  6.72 us
    ppermute x8, waiting for transfers between devices, trade(): from_last = lax.ppermute(to_next, axis, up)  6.69 us
    ppermute x8, starting transfers between devices, trade(): from_last = lax.ppermute(to_next, axis, up)  4.35 us
  transfers between devices with their start and end apart: 17, of which 13 were waited for; matrix products, arithmetic and copies ran while one was open for 0% of the time, Pallas kernels for 1%

profile of v6, /device:TPU:1, one launch (start us, length us, event | category | flops | bytes accessed | tf_op | source)
XLA Modules:
  0.0 94.9 jit_solution(7840148766210355211)
XLA Ops:
  0.7 2.2 %shard_map.76 = (f32[4,3,16,512]{3,2,1,0:T(8,128)}, f32[4,3,16,512]{3,2,1,0:T(8,128)}, f32[8,16,128]{2,1,0:T(8,128)}, f32[8,16,128]{2,1,0:T(8,128)}) custom-call(f32[16,8,512]{2,1,0:T(8,128)} %b_ref.3, f32[16,8,512]{2,1,0:T(8,128)} %x.1, f32[16,8,512]{2,1,0:T(8,128)} %c_ref.3), custom_call_target="tpu_custom_call" | custom-call | flops 1000000 | bytes 1000000 | tf_op jit(solution)/shard_map/pallas_call | solution.py:33
  2.9 14.1 %collective-permute-start.2 = (f32[8,16,128]{2,1,0:T(8,128)}, f32[8,16,128]{2,1,0:T(8,128)S(1)}, u32[]{:S(2)}, u32[]{:S(2)}) collective-permute-start(f32[8,16,128]{2,1,0:T(8,128)} %get-tuple-element.69), channel_id=1, source_target_pairs={{8,0},{16,8},{24,16},{32,24},{40,32},{48,40},{56,48},{64,56},{72,6... | collective-permute-start | bytes 196616 | tf_op jit(solution)/shard_map/ppermute | solution.py:510
  17.1 1.9 %collective-permute-start.3 = (f32[8,16,128]{2,1,0:T(8,128)}, f32[8,16,128]{2,1,0:T(8,128)S(1)}, u32[]{:S(2)}, u32[]{:S(2)}) collective-permute-start(f32[8,16,128]{2,1,0:T(8,128)} %get-tuple-element.70), channel_id=1, source_target_pairs={{0,8},{8,16},{16,24},{24,32},{32,40},{40,48},{48,56},{56,64},{64,7... | collective-permute-start | bytes 196616 | tf_op jit(solution)/shard_map/ppermute | solution.py:509
  19.0 1.0 %collective-permute-start = (f32[4,3,16,512]{3,2,1,0:T(8,128)}, f32[4,3,16,512]{3,2,1,0:T(8,128)S(1)}, u32[]{:S(2)}, u32[]{:S(2)}) collective-permute-start(f32[4,3,16,512]{3,2,1,0:T(8,128)} %get-tuple-element.61), channel_id=1, source_target_pairs={{1,0},{2,1},{3,2},{4,3},{5,4},{6,5},{7,6},{0,7},{9,8},{10,9},{11,1... | collective-permute-start | bytes 1179656 | tf_op jit(solution)/shard_map/ppermute | solution.py:510
  20.0 1.2 %collective-permute-start.1 = (f32[4,3,16,512]{3,2,1,0:T(8,128)}, f32[4,3,16,512]{3,2,1,0:T(8,128)S(1)}, u32[]{:S(2)}, u32[]{:S(2)}) collective-permute-start(f32[4,3,16,512]{3,2,1,0:T(8,128)} %get-tuple-element.62), channel_id=1, source_target_pairs={{0,1},{1,2},{2,3},{3,4},{4,5},{5,6},{6,7},{7,0},{8,9},{9,10},{10,1... | collective-permute-start | bytes 1179656 | tf_op jit(solution)/shard_map/ppermute | solution.py:509
  21.2 4.4 %collective-permute-done.3.from_west = f32[8,16,128]{2,1,0:T(8,128)S(1)} collective-permute-done((f32[8,16,128]{2,1,0:T(8,128)}, f32[8,16,128]{2,1,0:T(8,128)S(1)}, u32[]{:S(2)}, u32[]{:S(2)}) %collective-permute-start.3) | collective-permute-done | bytes 65568 | tf_op jit(solution)/shard_map/ppermute | solution.py:509
  25.8 2.1 %collective-permute-start.4 = (f32[4,3,16,128]{3,2,1,0:T(8,128)S(1)}, f32[4,3,16,128]{3,2,1,0:T(8,128)S(1)}, u32[]{:S(2)}, u32[]{:S(2)}) collective-permute-start(f32[4,3,16,128]{3,2,1,0:T(8,128)S(1)} %get-tuple-element.72), channel_id=1, source_target_pairs={{1,0},{2,1},{3,2},{4,3},{5,4},{6,5},{7,6},{0,7},{9,8},{10,9},{11,1... | collective-permute-start | bytes 294920 | tf_op jit(solution)/shard_map/ppermute | solution.py:510
  27.9 1.2 %collective-permute-start.5 = (f32[4,3,16,128]{3,2,1,0:T(8,128)S(1)}, f32[4,3,16,128]{3,2,1,0:T(8,128)S(1)}, u32[]{:S(2)}, u32[]{:S(2)}) collective-permute-start(f32[4,3,16,128]{3,2,1,0:T(8,128)S(1)} %get-tuple-element.73), channel_id=1, source_target_pairs={{0,1},{1,2},{2,3},{3,4},{4,5},{5,6},{6,7},{7,0},{8,9},{9,10},{10,1... | collective-permute-start | bytes 294920 | tf_op jit(solution)/shard_map/ppermute | solution.py:509
  29.7 1.7 %collective-permute-done.4.rim_north = f32[4,3,16,128]{3,2,1,0:T(8,128)S(1)} collective-permute-done((f32[4,3,16,128]{3,2,1,0:T(8,128)S(1)}, f32[4,3,16,128]{3,2,1,0:T(8,128)S(1)}, u32[]{:S(2)}, u32[]{:S(2)}) %collective-permute-start.4) | collective-permute-done | bytes 98336 | tf_op jit(solution)/shard_map/ppermute | solution.py:510
  31.4 3.4 %shard_map.79 = (f32[16,16,640]{2,1,0:T(8,128)S(1)}, f32[2,16,256]{2,1,0:T(8,128)S(1)}, f32[6,16,256]{2,1,0:T(8,128)S(1)}, f32[6,16,256]{2,1,0:T(8,128)S(1)}, f3...) custom-call(f32[16,16,512]{2,1,0:T(8,128)S(1)} %get-tuple-element.63, ...), custom_call_target="tpu_custom_call" | custom-call | flops 1000000 | bytes 1000000 | tf_op jit(solution)/shard_map/pallas_call | solution.py:33
  34.8 2.8 %collective-permute-start.6 = (f32[6,16,256]{2,1,0:T(8,128)S(1)}, f32[6,16,256]{2,1,0:T(8,128)S(1)}, u32[]{:S(2)}, u32[]{:S(2)}) collective-permute-start(f32[6,16,256]{2,1,0:T(8,128)S(1)} %get-tuple-element.75), channel_id=1, source_target_pairs={{1,0},{2,1},{3,2},{4,3},{5,4},{6,5},{7,6},{0,7},{9,8},{10,9},{11,1... | collective-permute-start | bytes 294920 | tf_op jit(solution)/shard_map/ppermute | solution.py:510
  37.6 1.3 %collective-permute-done.6.from_north = f32[6,16,256]{2,1,0:T(8,128)S(1)} collective-permute-done((f32[6,16,256]{2,1,0:T(8,128)S(1)}, f32[6,16,256]{2,1,0:T(8,128)S(1)}, u32[]{:S(2)}, u32[]{:S(2)}) %collective-permute-start.6) | collective-permute-done | bytes 98336 | tf_op jit(solution)/shard_map/ppermute | solution.py:510
  39.4 3.6 %collective-permute-start.8 = (f32[16,1152]{1,0:T(8,128)S(1)}, f32[16,1152]{1,0:T(8,128)S(1)}, u32[]{:S(2)}, u32[]{:S(2)}) collective-permute-start(f32[16,1152]{1,0:T(8,128)S(1)} %get-tuple-element.80), channel_id=1, source_target_pairs={{1,0},{2,1},{3,2},{4,3},{5,4},{6,5},{7,6},{0,7},{9,8},{10,9},{11,1... | collective-permute-start | bytes 221192 | tf_op jit(solution)/shard_map/ppermute | solution.py:510
  44.5 1.3 %shard_map.81 = (f32[8,16,512]{2,1,0:T(8,128)S(1)}, f32[8,16,640]{2,1,0:T(8,128)S(1)}, f32[3,16,640]{2,1,0:T(8,128)S(1)}, f32[3,16,640]{2,1,0:T(8,128)S(1)}, f32...) custom-call(f32[2,16,256]{2,1,0:T(8,128)S(1)} %get-tuple-element.79.e2, ...), custom_call_target="tpu_custom_call" | custom-call | flops 1000000 | bytes 1000000 | tf_op jit(solution)/shard_map/pallas_call | solution.py:33
  45.7 3.6 %collective-permute-start.10 = (f32[3,16,640]{2,1,0:T(8,128)S(1)}, f32[3,16,640]{2,1,0:T(8,128)S(1)}, u32[]{:S(2)}, u32[]{:S(2)}) collective-permute-start(f32[3,16,640]{2,1,0:T(8,128)S(1)} %get-tuple-element.97), channel_id=1, source_target_pairs={{1,0},{2,1},{3,2},{4,3},{5,4},{6,5},{7,6},{0,7},{9,8},{10,9},{11,1... | collective-permute-start | bytes 368648 | tf_op jit(solution)/shard_map/ppermute | solution.py:510
  49.4 1.3 %collective-permute-done.10.from_north = f32[3,16,640]{2,1,0:T(8,128)S(1)} collective-permute-done((f32[3,16,640]{2,1,0:T(8,128)S(1)}, f32[3,16,640]{2,1,0:T(8,128)S(1)}, u32[]{:S(2)}, u32[]{:S(2)}) %collective-permute-start.10) | collective-permute-done | bytes 122912 | tf_op jit(solution)/shard_map/ppermute | solution.py:510
  51.2 1.0 %shard_map.82 = (f32[2,16,256]{2,1,0:T(8,128)S(1)}, f32[2,16,256]{2,1,0:T(8,128)S(1)}, f32[2,16,256]{2,1,0:T(8,128)S(1)}, f32[16,16,640]{2,1,0:T(8,128)S(1)}, f3...) custom-call(f32[8,16,640]{2,1,0:T(8,128)S(1)} %get-tuple-element.96.w_own.w, ...), custom_call_target="tpu_custom_call" | custom-call | flops 1000000 | bytes 1000000 | tf_op jit(solution)/shard_map/pallas_call | solution.py:33
  52.3 3.7 %collective-permute-start.12 = (f32[2,16,256]{2,1,0:T(8,128)S(1)}, f32[2,16,256]{2,1,0:T(8,128)S(1)}, u32[]{:S(2)}, u32[]{:S(2)}) collective-permute-start(f32[2,16,256]{2,1,0:T(8,128)S(1)} %get-tuple-element.100), channel_id=1, source_target_pairs={{1,0},{2,1},{3,2},{4,3},{5,4},{6,5},{7,6},{0,7},{9,8},{10,9},{11,1... | collective-permute-start | bytes 98312 | tf_op jit(solution)/shard_map/ppermute | solution.py:510
  57.5 3.4 %collective-permute-start.14 = (f32[16,1152]{1,0:T(8,128)S(1)}, f32[16,1152]{1,0:T(8,128)S(1)}, u32[]{:S(2)}, u32[]{:S(2)}) collective-permute-start(f32[16,1152]{1,0:T(8,128)S(1)} %get-tuple-element.106), channel_id=1, source_target_pairs={{1,0},{2,1},{3,2},{4,3},{5,4},{6,5},{7,6},{0,7},{9,8},{10,9},{11,1... | collective-permute-start | bytes 221192 | tf_op jit(solution)/shard_map/ppermute | solution.py:510
  62.2 0.9 shard_map.84
  63.2 13.8 %all_to_all.22 = f32[16,1,128]{2,1,0:T(1,128)S(1)} all-to-all(f32[16,1,128]{2,1,0:T(1,128)S(1)} %bitcast.16), channel_id=1, replica_groups=mesh['x'=4,'z'=16,'lat'=8] {'z'}, dimensions={0} | all-to-all | bytes 16384 | tf_op jit(solution)/shard_map/all_to_all | solution.py:576
  77.6 9.4 %all-to-all-start.1 = ((f32[32,1,128]{2,1,0:T(1,128)}), f32[32,1,128]{2,1,0:T(1,128)S(1)}, u32[]{:S(2)}, u32[]{:S(2)}) async-start(f32[32,1,128]{2,1,0:T(1,128)} %bitcast.6), calls=%async_computation.1 | async-start | bytes 32768 | tf_op jit(solution)/shard_map/all_to_all | solution.py:577
  87.2 6.7 %all-to-all-done.1 = f32[32,1,128]{2,1,0:T(1,128)S(1)} async-done(((f32[32,1,128]{2,1,0:T(1,128)}), f32[32,1,128]{2,1,0:T(1,128)S(1)}, u32[]{:S(2)}, u32[]{:S(2)}) %all-to-all-start.1) | async-done | bytes 16416 | tf_op jit(solution)/shard_map/all_to_all | solution.py:577
  93.9 1.0 %shard_map.87 = (f32[16,8,512]{2,1,0:T(8,128)}, f32[16,8,512]{2,1,0:T(8,128)}, f32[16,8,512]{2,1,0:T(8,128)}) custom-call(f32[32,128]{1,0:T(8,128)S(1)} %bitcast.14, f32[16,8,512]{2,1,0:T(8,128)S(1)} %copy-done.1, f32[16,8,512]{2,1,0:T(8,128)S(1)} %get-tuple-element.115.p, f32[16,8,512]{2,1,0:T(8,128)S(1)} %get-tuple-element.116.w, ...), custom_call_target="tpu_custom_call" | custom-call | flops 1000000 | bytes 1000000 | tf_op jit(solution)/shard_map/pallas_call | solution.py:33
  (37 shorter events, 6.9 us)
Async XLA Ops:
  0.6 28.6 %copy-start.1 = (f32[16,8,512]{2,1,0:T(8,128)S(1)}, f32[16,8,512]{2,1,0:T(8,128)}, u32[]{:S(2)}) copy-start(f32[16,8,512]{2,1,0:T(8,128)} %x.1) | copy-start | bytes 786436
  0.6 28.6 %copy-start.2 = (f32[16,8,512]{2,1,0:T(8,128)S(1)}, f32[16,8,512]{2,1,0:T(8,128)}, u32[]{:S(2)}) copy-start(f32[16,8,512]{2,1,0:T(8,128)} %b_ref.3) | copy-start | bytes 786436
  0.7 28.6 %copy-start.3 = (f32[16,8,512]{2,1,0:T(8,128)S(1)}, f32[16,8,512]{2,1,0:T(8,128)}, u32[]{:S(2)}) copy-start(f32[16,8,512]{2,1,0:T(8,128)} %c_ref.3) | copy-start | bytes 786436
  2.9 18.3 %copy-start.4 = (f32[2,4,16]{2,1,0:T(4,128)S(1)}, f32[2,4,16]{2,1,0:T(4,128)}, u32[]{:S(2)}) copy-start(f32[2,4,16]{2,1,0:T(4,128)} %param.8) | copy-start | bytes 1540
  2.9 18.3 %collective-permute-start.2 = (f32[8,16,128]{2,1,0:T(8,128)}, f32[8,16,128]{2,1,0:T(8,128)S(1)}, u32[]{:S(2)}, u32[]{:S(2)}) collective-permute-start(f32[8,16,128]{2,1,0:T(8,128)} %get-tuple-element.69), channel_id=1, source_target_pairs={{8,0},{16,8},{24,16},{32,24},{40,32},{48,40},{56,48},{64,56},{72,6... | collective-permute-start | bytes 196616 | tf_op jit(solution)/shard_map/ppermute | solution.py:510
  17.1 8.5 %collective-permute-start.3 = (f32[8,16,128]{2,1,0:T(8,128)}, f32[8,16,128]{2,1,0:T(8,128)S(1)}, u32[]{:S(2)}, u32[]{:S(2)}) collective-permute-start(f32[8,16,128]{2,1,0:T(8,128)} %get-tuple-element.70), channel_id=1, source_target_pairs={{0,8},{8,16},{16,24},{24,32},{32,40},{40,48},{48,56},{56,64},{64,7... | collective-permute-start | bytes 196616 | tf_op jit(solution)/shard_map/ppermute | solution.py:509
  19.0 10.1 %collective-permute-start = (f32[4,3,16,512]{3,2,1,0:T(8,128)}, f32[4,3,16,512]{3,2,1,0:T(8,128)S(1)}, u32[]{:S(2)}, u32[]{:S(2)}) collective-permute-start(f32[4,3,16,512]{3,2,1,0:T(8,128)} %get-tuple-element.61), channel_id=1, source_target_pairs={{1,0},{2,1},{3,2},{4,3},{5,4},{6,5},{7,6},{0,7},{9,8},{10,9},{11,1... | collective-permute-start | bytes 1179656 | tf_op jit(solution)/shard_map/ppermute | solution.py:510
  20.0 9.2 %collective-permute-start.1 = (f32[4,3,16,512]{3,2,1,0:T(8,128)}, f32[4,3,16,512]{3,2,1,0:T(8,128)S(1)}, u32[]{:S(2)}, u32[]{:S(2)}) collective-permute-start(f32[4,3,16,512]{3,2,1,0:T(8,128)} %get-tuple-element.62), channel_id=1, source_target_pairs={{0,1},{1,2},{2,3},{3,4},{4,5},{5,6},{6,7},{7,0},{8,9},{9,10},{10,1... | collective-permute-start | bytes 1179656 | tf_op jit(solution)/shard_map/ppermute | solution.py:509
  25.8 5.6 %collective-permute-start.4 = (f32[4,3,16,128]{3,2,1,0:T(8,128)S(1)}, f32[4,3,16,128]{3,2,1,0:T(8,128)S(1)}, u32[]{:S(2)}, u32[]{:S(2)}) collective-permute-start(f32[4,3,16,128]{3,2,1,0:T(8,128)S(1)} %get-tuple-element.72), channel_id=1, source_target_pairs={{1,0},{2,1},{3,2},{4,3},{5,4},{6,5},{7,6},{0,7},{9,8},{10,9},{11,1... | collective-permute-start | bytes 294920 | tf_op jit(solution)/shard_map/ppermute | solution.py:510
  27.9 3.5 %collective-permute-start.5 = (f32[4,3,16,128]{3,2,1,0:T(8,128)S(1)}, f32[4,3,16,128]{3,2,1,0:T(8,128)S(1)}, u32[]{:S(2)}, u32[]{:S(2)}) collective-permute-start(f32[4,3,16,128]{3,2,1,0:T(8,128)S(1)} %get-tuple-element.73), channel_id=1, source_target_pairs={{0,1},{1,2},{2,3},{3,4},{4,5},{5,6},{6,7},{7,0},{8,9},{9,10},{10,1... | collective-permute-start | bytes 294920 | tf_op jit(solution)/shard_map/ppermute | solution.py:509
  29.2 2.2 %copy-start = (bf16[640,256]{1,0:T(8,128)(2,1)S(1)}, bf16[640,256]{1,0:T(8,128)(2,1)}, u32[]{:S(2)}) copy-start(bf16[640,256]{1,0:T(8,128)(2,1)} %constant.2.clone.blocks) | copy-start | bytes 983044
  34.8 4.1 %collective-permute-start.6 = (f32[6,16,256]{2,1,0:T(8,128)S(1)}, f32[6,16,256]{2,1,0:T(8,128)S(1)}, u32[]{:S(2)}, u32[]{:S(2)}) collective-permute-start(f32[6,16,256]{2,1,0:T(8,128)S(1)} %get-tuple-element.75), channel_id=1, source_target_pairs={{1,0},{2,1},{3,2},{4,3},{5,4},{6,5},{7,6},{0,7},{9,8},{10,9},{11,1... | collective-permute-start | bytes 294920 | tf_op jit(solution)/shard_map/ppermute | solution.py:510
  37.6 1.6 %collective-permute-start.7 = (f32[6,16,256]{2,1,0:T(8,128)S(1)}, f32[6,16,256]{2,1,0:T(8,128)S(1)}, u32[]{:S(2)}, u32[]{:S(2)}) collective-permute-start(f32[6,16,256]{2,1,0:T(8,128)S(1)} %get-tuple-element.76), channel_id=1, source_target_pairs={{0,1},{1,2},{2,3},{3,4},{4,5},{5,6},{6,7},{7,0},{8,9},{9,10},{10,1... | collective-permute-start | bytes 294920 | tf_op jit(solution)/shard_map/ppermute | solution.py:509
  39.4 4.6 %collective-permute-start.8 = (f32[16,1152]{1,0:T(8,128)S(1)}, f32[16,1152]{1,0:T(8,128)S(1)}, u32[]{:S(2)}, u32[]{:S(2)}) collective-permute-start(f32[16,1152]{1,0:T(8,128)S(1)} %get-tuple-element.80), channel_id=1, source_target_pairs={{1,0},{2,1},{3,2},{4,3},{5,4},{6,5},{7,6},{0,7},{9,8},{10,9},{11,1... | collective-permute-start | bytes 221192 | tf_op jit(solution)/shard_map/ppermute | solution.py:510
  43.1 1.4 %collective-permute-start.9 = (f32[16,1152]{1,0:T(8,128)S(1)}, f32[16,1152]{1,0:T(8,128)S(1)}, u32[]{:S(2)}, u32[]{:S(2)}) collective-permute-start(f32[16,1152]{1,0:T(8,128)S(1)} %get-tuple-element.81), channel_id=1, source_target_pairs={{0,1},{1,2},{2,3},{3,4},{4,5},{5,6},{6,7},{7,0},{8,9},{9,10},{10,1... | collective-permute-start | bytes 221192 | tf_op jit(solution)/shard_map/ppermute | solution.py:509
  45.7 4.9 %collective-permute-start.10 = (f32[3,16,640]{2,1,0:T(8,128)S(1)}, f32[3,16,640]{2,1,0:T(8,128)S(1)}, u32[]{:S(2)}, u32[]{:S(2)}) collective-permute-start(f32[3,16,640]{2,1,0:T(8,128)S(1)} %get-tuple-element.97), channel_id=1, source_target_pairs={{1,0},{2,1},{3,2},{4,3},{5,4},{6,5},{7,6},{0,7},{9,8},{10,9},{11,1... | collective-permute-start | bytes 368648 | tf_op jit(solution)/shard_map/ppermute | solution.py:510
  49.4 1.9 %collective-permute-start.11 = (f32[3,16,640]{2,1,0:T(8,128)S(1)}, f32[3,16,640]{2,1,0:T(8,128)S(1)}, u32[]{:S(2)}, u32[]{:S(2)}) collective-permute-start(f32[3,16,640]{2,1,0:T(8,128)S(1)} %get-tuple-element.98), channel_id=1, source_target_pairs={{0,1},{1,2},{2,3},{3,4},{4,5},{5,6},{6,7},{7,0},{8,9},{9,10},{10,1... | collective-permute-start | bytes 368648 | tf_op jit(solution)/shard_map/ppermute | solution.py:509
  52.3 4.5 %collective-permute-start.12 = (f32[2,16,256]{2,1,0:T(8,128)S(1)}, f32[2,16,256]{2,1,0:T(8,128)S(1)}, u32[]{:S(2)}, u32[]{:S(2)}) collective-permute-start(f32[2,16,256]{2,1,0:T(8,128)S(1)} %get-tuple-element.100), channel_id=1, source_target_pairs={{1,0},{2,1},{3,2},{4,3},{5,4},{6,5},{7,6},{0,7},{9,8},{10,9},{11,1... | collective-permute-start | bytes 98312 | tf_op jit(solution)/shard_map/ppermute | solution.py:510
  55.9 1.2 %collective-permute-start.13 = (f32[2,16,256]{2,1,0:T(8,128)S(1)}, f32[2,16,256]{2,1,0:T(8,128)S(1)}, u32[]{:S(2)}, u32[]{:S(2)}) collective-permute-start(f32[2,16,256]{2,1,0:T(8,128)S(1)} %get-tuple-element.101), channel_id=1, source_target_pairs={{0,1},{1,2},{2,3},{3,4},{4,5},{5,6},{6,7},{7,0},{8,9},{9,10},{10,1... | collective-permute-start | bytes 98312 | tf_op jit(solution)/shard_map/ppermute | solution.py:509
  57.5 4.3 %collective-permute-start.14 = (f32[16,1152]{1,0:T(8,128)S(1)}, f32[16,1152]{1,0:T(8,128)S(1)}, u32[]{:S(2)}, u32[]{:S(2)}) collective-permute-start(f32[16,1152]{1,0:T(8,128)S(1)} %get-tuple-element.106), channel_id=1, source_target_pairs={{1,0},{2,1},{3,2},{4,3},{5,4},{6,5},{7,6},{0,7},{9,8},{10,9},{11,1... | collective-permute-start | bytes 221192 | tf_op jit(solution)/shard_map/ppermute | solution.py:510
  60.8 1.4 %collective-permute-start.15 = (f32[16,1152]{1,0:T(8,128)S(1)}, f32[16,1152]{1,0:T(8,128)S(1)}, u32[]{:S(2)}, u32[]{:S(2)}) collective-permute-start(f32[16,1152]{1,0:T(8,128)S(1)} %get-tuple-element.107), channel_id=1, source_target_pairs={{0,1},{1,2},{2,3},{3,4},{4,5},{5,6},{6,7},{7,0},{8,9},{9,10},{10,1... | collective-permute-start | bytes 221192 | tf_op jit(solution)/shard_map/ppermute | solution.py:509
  77.6 16.3 %all-to-all-start.1 = ((f32[32,1,128]{2,1,0:T(1,128)}), f32[32,1,128]{2,1,0:T(1,128)S(1)}, u32[]{:S(2)}, u32[]{:S(2)}) async-start(f32[32,1,128]{2,1,0:T(1,128)} %bitcast.6), calls=%async_computation.1 | async-start | bytes 32768 | tf_op jit(solution)/shard_map/all_to_all | solution.py:577
